TPU v7x, 128 devices: a whole 4x4x4 slice. The times are simulated.
128 devices in a mesh: doc: 32 (over x, z, core), bkt: 4 (over y).
Axes of the slice: x: 4, y: 4, z: 4, core: 2. Of those that a mesh axis runs over, the one named last changes fastest.
Arguments:
- start_vectors: float32 [64, 131072], P(None, ('doc', 'bkt')), may hold values from -6 to 6
- bucket_weight: float32 [32768], P('bkt'), may hold values from 0.1 to 1
- tile_count: int32 [32, 4], P('doc', 'bkt'), may hold values from 128 to 256, as said below
- tile_coords: int32 [32, 4, 256, 2], P('doc', 'bkt'), may hold values from 0 to 63, as said below
- patterns: int32 [32, 4, 256, 128, 128], P('doc', 'bkt'), may hold values from 0 to 1
Outputs:
- eigen_block: float32 [64, 131072], P(None, ('doc', 'bkt'))
Inputs may be any that keep to these rules, and one draw needn't show every extreme that they name: `tile_count`: the largest count is exactly 256 in every draw. `tile_coords`: row tiles lie below 32, column tiles below 64; the pairs of one document band and bucket band are distinct.
All inputs are finite; a program needn't handle non-finite values.
Results may differ from a plain program's by a relative error of at most 0.018.
Values may be sent and summed in bfloat16 or wider, within the bound.
No kernel may reach another device: no remote copies, remote signals or barrier semaphores. Data moves between devices by JAX's collectives and lax.ppermute only.
A program may use at most 128 MiB of HBM per device.

v0:
```python
import functools

import jax
import jax.numpy as jnp
from jax import lax
from jax.sharding import Mesh
from jax.sharding import PartitionSpec as P

ITERS = 2
DOC = ("doc_0", "doc_1", "doc_2")
DOC_BKT = ("doc_0", "doc_1", "doc_2", "bkt")


def copy_for_each(shard, axis):
    copies = jnp.broadcast_to(shard, (lax.axis_size(axis), *shard.shape))
    return lax.all_to_all(copies, axis, split_axis=0, concat_axis=0, tiled=True)


def over_copies(shard, axis):
    everything = copy_for_each(shard, axis)
    return jnp.sum(everything, axis=0)


def taken_together(shard, axis):
    return copy_for_each(shard, axis).astype(jnp.float32).sum(axis=0)


def joined_along(blocks, dim):
    lengths = list(blocks.shape[1:])
    lengths[dim] *= blocks.shape[0]
    return jnp.moveaxis(blocks, 0, dim).reshape(lengths)


def gathered_copies(shard, axis, dim):
    blocks = copy_for_each(shard, axis)
    return joined_along(blocks, dim)


def in_blocks(shard, dim, devices):
    lengths = shard.shape
    blocks = shard.reshape(*lengths[:dim], devices, lengths[dim] // devices, *lengths[dim + 1 :])
    return jnp.moveaxis(blocks, dim, 0)


def sum_at_owner(shard, axis, dim):
    blocks = in_blocks(shard, dim, lax.axis_size(axis))
    arrived = lax.all_to_all(blocks, axis, split_axis=0, concat_axis=0, tiled=True)
    return arrived.sum(axis=0)


def over_axes(shard, axes):
    return functools.reduce(lax.psum, axes, shard)


def body(start_vectors, bucket_weight, tile_count, tile_coords, patterns):
    highest = lax.Precision.HIGHEST
    slot_total = patterns.shape[2]
    tile_size = patterns.shape[3]
    vector_count = start_vectors.shape[0]
    own_rows = start_vectors.shape[1]
    band_rows = own_rows * lax.axis_size("bkt")
    band_cols = bucket_weight.shape[0]
    row_tiles = band_rows // tile_size
    col_tiles = band_cols // tile_size
    total_docs = band_rows * lax.axis_size(DOC)
    live_slot = (jnp.arange(slot_total) < tile_count[0, 0]).astype(jnp.int32)
    pattern_int = patterns[0, 0] * live_slot[:, None, None]
    pattern = pattern_int.astype(jnp.bfloat16)
    row_index = tile_coords[0, 0, :, 0]
    col_index = tile_coords[0, 0, :, 1]
    row_pick = jnp.arange(row_tiles)[:, None] == row_index[None, :]
    col_pick = jnp.arange(col_tiles)[:, None] == col_index[None, :]
    row_pick_f = row_pick.astype(jnp.float32)
    row_pick_b = row_pick.astype(jnp.bfloat16)
    col_pick_f = col_pick.astype(jnp.float32)
    col_pick_b = col_pick.astype(jnp.bfloat16)
    pattern_f = pattern_int.astype(jnp.float32)
    weight_tiles = bucket_weight.reshape(col_tiles, tile_size)
    slot_weight = jnp.dot(col_pick_f.T, weight_tiles, precision=highest)
    row_part = jnp.einsum("tij,tj->ti", pattern_f, slot_weight, precision=highest)
    doc_part = jnp.dot(row_pick_f, row_part, precision=highest).reshape(band_rows)
    col_part = jnp.sum(pattern_f, axis=1)
    bucket_part = jnp.dot(col_pick_f, col_part, precision=highest).reshape(band_cols)
    doc_degree = over_copies(doc_part, "bkt")
    bucket_size = taken_together(bucket_part.astype(jnp.bfloat16), DOC).astype(jnp.float32)
    inv_band = 1.0 / jnp.sqrt(jnp.maximum(doc_degree, 1.0))
    inv_own = lax.dynamic_slice_in_dim(inv_band, lax.axis_index("bkt") * own_rows, own_rows)
    bucket_scale = bucket_weight / jnp.maximum(bucket_size, 1.0)
    vectors = start_vectors
    for sweep_index in range(ITERS):
        scaled = (vectors * inv_own[None, :]).astype(jnp.bfloat16)
        band_vecs = gathered_copies(scaled, "bkt", 1)
        picked = jnp.einsum(
            "rt,kri->kti",
            row_pick_b,
            band_vecs.reshape(vector_count, row_tiles, tile_size),
            preferred_element_type=jnp.float32,
        ).astype(jnp.bfloat16)
        products = jnp.einsum("kti,tij->ktj", picked, pattern, preferred_element_type=jnp.float32)
        panel_part = (
            jnp.zeros((vector_count, col_tiles, tile_size), jnp.float32)
            .at[:, col_index, :]
            .add(products)
        )
        panel_part = panel_part.reshape(vector_count, band_cols)
        share_cols = band_cols // lax.axis_size(DOC)
        panel_own = sum_at_owner(panel_part, DOC, 1)
        scale_own = lax.dynamic_slice_in_dim(
            bucket_scale, lax.axis_index(DOC) * share_cols, share_cols
        )
        weighted_own = (panel_own * scale_own[None, :]).astype(jnp.bfloat16)
        weighted = gathered_copies(weighted_own, DOC, 1)
        spread = jnp.einsum(
            "ct,kcj->ktj",
            col_pick_b,
            weighted.reshape(vector_count, col_tiles, tile_size),
            preferred_element_type=jnp.float32,
        ).astype(jnp.bfloat16)
        returned = jnp.einsum("ktj,tij->kti", spread, pattern, preferred_element_type=jnp.float32)
        row_terms = (
            jnp.zeros((vector_count, row_tiles, tile_size), jnp.float32)
            .at[:, row_index, :]
            .add(returned)
        )
        row_terms = row_terms.reshape(vector_count, band_rows)
        rows_own = sum_at_owner(row_terms, "bkt", 1) * inv_own[None, :]
        gram_local = jnp.dot(rows_own, rows_own.T, precision=highest)
        gram_matrix = over_axes(gram_local, DOC_BKT) / total_docs
        factor = jnp.linalg.cholesky(gram_matrix)
        vectors = lax.linalg.triangular_solve(factor, rows_own, left_side=True, lower=True)
    return vectors


def solution(mesh):
    split = Mesh(
        mesh.devices.reshape(4, 4, 2, mesh.shape["bkt"]), ("doc_0", "doc_1", "doc_2", "bkt")
    )
    in_specs = (
        P(None, DOC_BKT),
        P("bkt"),
        P(DOC, "bkt"),
        P(DOC, "bkt", None, None),
        P(DOC, "bkt", None, None, None),
    )
    out_specs = P(None, DOC_BKT)
    return jax.shard_map(body, mesh=split, in_specs=in_specs, out_specs=out_specs, check_vma=False)
```

profile of v0, /device:TPU:0, one launch (start us, length us, event | category | flops | bytes accessed | tf_op | source)
XLA Modules:
  0.0 573.9 jit_solution(16291826150313600782)
XLA Ops:
  2.5 28.9 %fusion = f32[256,1,128]{2,1,0:T(1,128)S(1)} fusion(f32[256,128,1]{1,2,0:T(1,128)S(1)} %bitcast.96, s32[1,1,256,128,128]{4,3,2,1,0:T(8,128)} %param.12, s32[256]{0:T(256)S(1)} %compare_convert_fusion), kind=kOutput, calls=%fused_computation.6 | convolution fusion | flops 58720256 | bytes 17040384 | tf_op jit(solution)/shard_map/tij,tj->ti/dot_general | solution.py:80
  36.8 9.6 %fusion.2 = bf16[256,128,128]{2,1,0:T(8,128)(2,1)} fusion(s32[1,1,256,128,128]{4,3,2,1,0:T(8,128)} %param.12, s32[256]{0:T(256)S(1)} %compare_convert_fusion), kind=kLoop, calls=%fused_computation.8 | loop fusion | flops 8388608 | bytes 25166848 | tf_op jit(solution)/shard_map/convert_element_type | solution.py:68
  52.7 7.7 %convert_reduce_fusion = f32[256,128]{1,0:T(8,128)S(1)} fusion(s32[1,1,256,128,128]{4,3,2,1,0:T(8,128)} %param.12, s32[256]{0:T(256)S(1)} %compare_convert_fusion), kind=kLoop, calls=%fused_computation.5 | loop fusion | flops 12550144 | bytes 16909312 | tf_op jit(solution)/shard_map/reduce_sum | solution.py:82
  67.1 8.3 %all-to-all-start.3 = ((bf16[32,2,4096]{2,1,0:T(2,128)(2,1)}), bf16[32,2,4096]{2,1,0:T(2,128)(2,1)S(1)}, u32[]{:S(2)}, u32[]{:S(2)}) async-start(bf16[32,2,4096]{2,1,0:T(2,128)(2,1)} %reshape.137), calls=%async_computation.3 | async-start | bytes 1048576 | tf_op jit(solution)/shard_map/all_to_all | solution.py:16
  79.3 6.6 %copy.82 = bf16[64,256,128]{2,0,1:T(8,128)(2,1)} copy(bf16[64,256,128]{1,2,0:T(8,128)(2,1)} %convert_bitcast_fusion.3) | data formatting | bytes 8388608 | tf_op jit(solution)/shard_map/convert_element_type | solution.py:98
  85.9 10.2 %fusion.42 = f32[256,64,128]{2,1,0:T(8,128)} fusion(bf16[64,256,128]{2,0,1:T(8,128)(2,1)} %copy.82, bf16[256,128,128]{2,1,0:T(8,128)(2,1)} %fusion.2), kind=kOutput, calls=%fused_computation.74 | convolution fusion | flops 536870912 | bytes 20971520 | tf_op jit(solution)/shard_map/kti,tij->ktj/dot_general | solution.py:99
  96.3 26.1 %scatter_fusion = f32[64,64,128]{2,0,1:T(8,128)S(1)} fusion(f32[64,64,128]{2,0,1:T(8,128)S(1)} %broadcast.98.clone, s32[256]{0:T(256)S(1)} %bitcast.107, f32[256,64,128]{2,1,0:T(8,128)} %fusion.42), kind=kCustom, calls=%fused_computation | custom fusion | flops 2097152 | bytes 25166848 | tf_op jit(solution)/shard_map/scatter-add | solution.py:103
  129.6 7.5 %all-to-all-start.2 = ((f32[32,64,256]{2,1,0:T(8,128)}), f32[32,64,256]{2,1,0:T(8,128)S(1)}, u32[]{:S(2)}, u32[]{:S(2)}) async-start(f32[32,64,256]{2,1,0:T(8,128)} %copy.84), calls=%async_computation.2 | async-start | bytes 4194304 | tf_op jit(solution)/shard_map/all_to_all | solution.py:47
  142.1 23.9 %all-to-all-done.2 = f32[32,64,256]{2,1,0:T(8,128)S(1)} async-done(((f32[32,64,256]{2,1,0:T(8,128)}), f32[32,64,256]{2,1,0:T(8,128)S(1)}, u32[]{:S(2)}, u32[]{:S(2)}) %all-to-all-start.2) | async-done | bytes 2097184 | tf_op jit(solution)/shard_map/all_to_all | solution.py:47
  166.3 20.1 %all_to_all.52 = bf16[32,64,256]{2,1,0:T(8,128)(2,1)S(1)} all-to-all(bf16[32,64,256]{2,1,0:T(8,128)(2,1)S(1)} %broadcast_in_dim.19), channel_id=1, replica_groups=mesh['doc_0'=4,'doc_1'=4,'doc_2'=2,'bkt'=4] {'doc_0','doc_1','doc_2'}, dimensions={0} | all-to-all | bytes 2097152 | tf_op jit(solution)/shard_map/all_to_all | solution.py:16
  190.6 6.6 %copy.87 = bf16[64,256,128]{2,0,1:T(8,128)(2,1)} copy(bf16[64,256,128]{1,2,0:T(8,128)(2,1)} %convert_bitcast_fusion.2) | data formatting | bytes 8388608 | tf_op jit(solution)/shard_map/convert_element_type | solution.py:118
  197.2 13.7 %fusion.43 = f32[256,64,128]{2,1,0:T(8,128)} fusion(bf16[64,256,128]{2,0,1:T(8,128)(2,1)} %copy.87, bf16[256,128,128]{2,1,0:T(8,128)(2,1)} %fusion.2), kind=kOutput, calls=%fused_computation.75 | convolution fusion | flops 536870912 | bytes 20971520 | tf_op jit(solution)/shard_map/ktj,tij->kti/dot_general | solution.py:119
  211.1 26.1 %scatter_fusion.1 = f32[64,32,128]{2,0,1:T(8,128)S(1)} fusion(f32[64,32,128]{2,0,1:T(8,128)S(1)} %broadcast.95.clone, s32[256]{0:T(256)S(1)} %bitcast.105, f32[256,64,128]{2,1,0:T(8,128)} %fusion.43), kind=kCustom, calls=%fused_computation.1 | custom fusion | flops 2097152 | bytes 25166848 | tf_op jit(solution)/shard_map/scatter-add | solution.py:123
  238.8 20.2 %all_to_all.55 = f32[4,64,1024]{2,1,0:T(8,128)S(1)} all-to-all(f32[4,64,1024]{2,1,0:T(8,128)S(1)} %copy.89), channel_id=1, replica_groups=mesh['doc_0'=4,'doc_1'=4,'doc_2'=2,'bkt'=4] {'bkt'}, dimensions={0} | all-to-all | bytes 2097152 | tf_op jit(solution)/shard_map/all_to_all | solution.py:47
  259.4 15.3 %psum.56 = f32[64,64]{0,1:T(8,128)S(1)} all-reduce(f32[64,64]{0,1:T(8,128)S(1)} %fusion.11), channel_id=1, replica_groups=mesh['doc_0'=4,'doc_1'=4,'doc_2'=2,'bkt'=4] {'doc_0'}, use_global_device_ids=true, to_apply=%region_7.0 | all-reduce | flops 4096 | bytes 32768 | tf_op jit(solution)/shard_map/psum | solution.py:52
  274.8 15.9 %psum.57 = f32[64,64]{0,1:T(8,128)S(1)} all-reduce(f32[64,64]{0,1:T(8,128)S(1)} %psum.56), channel_id=1, replica_groups=mesh['doc_0'=4,'doc_1'=4,'doc_2'=2,'bkt'=4] {'doc_1'}, use_global_device_ids=true, to_apply=%region_8.0 | all-reduce | flops 4096 | bytes 32768 | tf_op jit(solution)/shard_map/psum | solution.py:52
  294.1 15.5 %psum.59 = f32[64,64]{0,1:T(8,128)S(1)} all-reduce(f32[64,64]{0,1:T(8,128)S(1)} %psum.58), channel_id=1, replica_groups=mesh['doc_0'=4,'doc_1'=4,'doc_2'=2,'bkt'=4] {'bkt'}, use_global_device_ids=true, to_apply=%region_10.0 | all-reduce | flops 4096 | bytes 32768 | tf_op jit(solution)/shard_map/psum | solution.py:52
  309.7 5.8 %cholesky.44 = f32[64,64]{1,0:T(8,128)S(1)} custom-call(f32[64,64]{1,0:T(8,128)S(1)} %fusion.26), custom_call_target="Cholesky" | custom-call | tf_op jit(solution)/shard_map/jit(cholesky)/cholesky | solution.py:129
  322.3 11.0 %all_to_all.53 = bf16[4,64,1024]{2,1,0:T(8,128)(2,1)S(1)} all-to-all(bf16[4,64,1024]{2,1,0:T(8,128)(2,1)S(1)} %broadcast_in_dim.20), channel_id=1, replica_groups=mesh['doc_0'=4,'doc_1'=4,'doc_2'=2,'bkt'=4] {'bkt'}, dimensions={0} | all-to-all | bytes 1048576 | tf_op jit(solution)/shard_map/all_to_all | solution.py:16
  337.2 6.6 %copy.93 = bf16[64,256,128]{2,0,1:T(8,128)(2,1)} copy(bf16[64,256,128]{1,2,0:T(8,128)(2,1)} %convert_bitcast_fusion.1) | data formatting | bytes 8388608 | tf_op jit(solution)/shard_map/convert_element_type | solution.py:98
  343.8 10.2 %fusion.44 = f32[256,64,128]{2,1,0:T(8,128)} fusion(bf16[64,256,128]{2,0,1:T(8,128)(2,1)} %copy.93, bf16[256,128,128]{2,1,0:T(8,128)(2,1)} %fusion.2), kind=kOutput, calls=%fused_computation.76 | convolution fusion | flops 536870912 | bytes 20971520 | tf_op jit(solution)/shard_map/kti,tij->ktj/dot_general | solution.py:99
  354.2 26.1 %scatter_fusion.2 = f32[64,64,128]{2,0,1:T(8,128)S(1)} fusion(f32[64,64,128]{2,0,1:T(8,128)S(1)} %broadcast.98, s32[256]{0:T(256)S(1)} %bitcast.108, f32[256,64,128]{2,1,0:T(8,128)} %fusion.44), kind=kCustom, calls=%fused_computation.2 | custom fusion | flops 2097152 | bytes 25166848 | tf_op jit(solution)/shard_map/scatter-add | solution.py:103
  386.1 31.8 %all_to_all.56 = f32[32,64,256]{2,1,0:T(8,128)S(1)} all-to-all(f32[32,64,256]{2,1,0:T(8,128)S(1)} %copy.95), channel_id=1, replica_groups=mesh['doc_0'=4,'doc_1'=4,'doc_2'=2,'bkt'=4] {'doc_0','doc_1','doc_2'}, dimensions={0} | all-to-all | bytes 4194304 | tf_op jit(solution)/shard_map/all_to_all | solution.py:47
  418.2 20.9 %all_to_all.54 = bf16[32,64,256]{2,1,0:T(8,128)(2,1)S(1)} all-to-all(bf16[32,64,256]{2,1,0:T(8,128)(2,1)S(1)} %broadcast_in_dim.40), channel_id=1, replica_groups=mesh['doc_0'=4,'doc_1'=4,'doc_2'=2,'bkt'=4] {'doc_0','doc_1','doc_2'}, dimensions={0} | all-to-all | bytes 2097152 | tf_op jit(solution)/shard_map/all_to_all | solution.py:16
  443.3 6.6 %copy.97 = bf16[64,256,128]{2,0,1:T(8,128)(2,1)} copy(bf16[64,256,128]{1,2,0:T(8,128)(2,1)} %convert_bitcast_fusion) | data formatting | bytes 8388608 | tf_op jit(solution)/shard_map/convert_element_type | solution.py:118
  449.9 13.7 %fusion.45 = f32[256,64,128]{2,1,0:T(8,128)} fusion(bf16[64,256,128]{2,0,1:T(8,128)(2,1)} %copy.97, bf16[256,128,128]{2,1,0:T(8,128)(2,1)} %fusion.2), kind=kOutput, calls=%fused_computation.77 | convolution fusion | flops 536870912 | bytes 20971520 | tf_op jit(solution)/shard_map/ktj,tij->kti/dot_general | solution.py:119
  463.7 26.1 %scatter_fusion.3 = f32[64,32,128]{2,0,1:T(8,128)S(1)} fusion(f32[64,32,128]{2,0,1:T(8,128)S(1)} %broadcast.95, s32[256]{0:T(256)S(1)} %bitcast.106, f32[256,64,128]{2,1,0:T(8,128)} %fusion.45), kind=kCustom, calls=%fused_computation.3 | custom fusion | flops 2097152 | bytes 25166848 | tf_op jit(solution)/shard_map/scatter-add | solution.py:123
  491.5 18.3 %all_to_all.57 = f32[4,64,1024]{2,1,0:T(8,128)S(1)} all-to-all(f32[4,64,1024]{2,1,0:T(8,128)S(1)} %copy.99), channel_id=1, replica_groups=mesh['doc_0'=4,'doc_1'=4,'doc_2'=2,'bkt'=4] {'bkt'}, dimensions={0} | all-to-all | bytes 2097152 | tf_op jit(solution)/shard_map/all_to_all | solution.py:47
  510.2 15.3 %psum.60 = f32[64,64]{0,1:T(8,128)S(1)} all-reduce(f32[64,64]{0,1:T(8,128)S(1)} %fusion.8), channel_id=1, replica_groups=mesh['doc_0'=4,'doc_1'=4,'doc_2'=2,'bkt'=4] {'doc_0'}, use_global_device_ids=true, to_apply=%region_17.20 | all-reduce | flops 4096 | bytes 32768 | tf_op jit(solution)/shard_map/psum | solution.py:52
  525.6 15.9 %psum.61 = f32[64,64]{0,1:T(8,128)S(1)} all-reduce(f32[64,64]{0,1:T(8,128)S(1)} %psum.60), channel_id=1, replica_groups=mesh['doc_0'=4,'doc_1'=4,'doc_2'=2,'bkt'=4] {'doc_1'}, use_global_device_ids=true, to_apply=%region_18.21 | all-reduce | flops 4096 | bytes 32768 | tf_op jit(solution)/shard_map/psum | solution.py:52
  544.9 15.5 %psum.63 = f32[64,64]{0,1:T(8,128)S(1)} all-reduce(f32[64,64]{0,1:T(8,128)S(1)} %psum.62), channel_id=1, replica_groups=mesh['doc_0'=4,'doc_1'=4,'doc_2'=2,'bkt'=4] {'bkt'}, use_global_device_ids=true, to_apply=%region_20.23 | all-reduce | flops 4096 | bytes 32768 | tf_op jit(solution)/shard_map/psum | solution.py:52
  560.5 5.8 %cholesky.55 = f32[64,64]{1,0:T(8,128)S(1)} custom-call(f32[64,64]{1,0:T(8,128)S(1)} %fusion.24), custom_call_target="Cholesky" | custom-call | tf_op jit(solution)/shard_map/jit(cholesky)/cholesky | solution.py:129
  (86 shorter events, 80.5 us)
Async XLA Ops:
  32.2 14.1 %all-to-all-start = ((f32[4,1,4096]{2,1,0:T(1,128)}), f32[4,1,4096]{2,1,0:T(1,128)S(1)}, u32[]{:S(2)}, u32[]{:S(2)}) async-start(f32[4,1,4096]{2,1,0:T(1,128)} %broadcast_in_dim.16), calls=%async_computation | async-start | bytes 131072 | tf_op jit(solution)/shard_map/all_to_all | solution.py:16
  36.8 9.7 %copy-start.1 = (f32[64,1024]{1,0:T(8,128)S(1)}, f32[64,1024]{1,0:T(8,128)}, u32[]{:S(2)}) copy-start(f32[64,1024]{1,0:T(8,128)} %param.8) | copy-start | bytes 786436
  47.4 19.7 %all-to-all-start.1 = ((bf16[4,64,1024]{2,1,0:T(8,128)(2,1)}), bf16[4,64,1024]{2,1,0:T(8,128)(2,1)S(1)}, u32[]{:S(2)}, u32[]{:S(2)}) async-start(bf16[4,64,1024]{2,1,0:T(8,128)(2,1)} %broadcast_in_dim.17), calls=%async_computation.1 | async-start | bytes 1048576 | tf_op jit(solution)/shard_map/all_to_all | solution.py:16
  52.7 14.3 %copy-start.2 = (s32[1,1,256,2]{2,3,1,0:T(2,128)S(1)}, s32[1,1,256,2]{2,3,1,0:T(2,128)}, u32[]{:S(2)}) copy-start(s32[1,1,256,2]{2,3,1,0:T(2,128)} %param.11) | copy-start | bytes 6148
  67.1 62.5 %all-to-all-start.3 = ((bf16[32,2,4096]{2,1,0:T(2,128)(2,1)}), bf16[32,2,4096]{2,1,0:T(2,128)(2,1)S(1)}, u32[]{:S(2)}, u32[]{:S(2)}) async-start(bf16[32,2,4096]{2,1,0:T(2,128)(2,1)} %reshape.137), calls=%async_computation.3 | async-start | bytes 1048576 | tf_op jit(solution)/shard_map/all_to_all | solution.py:16
  129.6 7.5 %copy-start = (bf16[32,2,4096]{2,1,0:T(2,128)(2,1)}, bf16[32,2,4096]{2,1,0:T(2,128)(2,1)S(1)}, u32[]{:S(2)}) copy-start(bf16[32,2,4096]{2,1,0:T(2,128)(2,1)S(1)} %all-to-all-done.3) | copy-start | bytes 1572868
  129.6 36.4 %all-to-all-start.2 = ((f32[32,64,256]{2,1,0:T(8,128)}), f32[32,64,256]{2,1,0:T(8,128)S(1)}, u32[]{:S(2)}, u32[]{:S(2)}) async-start(f32[32,64,256]{2,1,0:T(8,128)} %copy.84), calls=%async_computation.2 | async-start | bytes 4194304 | tf_op jit(solution)/shard_map/all_to_all | solution.py:47
where the time goes:
time: 583 us; the launch traced here: 574 us
  blocking collectives  223 us (38%)
  other arithmetic  152 us (26%)
  matrix products  93.5 us (16%)
  local copies, waits for them, and re-layouts  55.2 us (9%)
  starting transfers between devices  25.7 us (4%)
  waiting for transfers between devices  23.9 us (4%)
    psum x8, blocking collectives, over_axes(): return functools.reduce(lax.psum, axes, shard)  100 us
    all_to_all x3, blocking collectives, sum_at_owner(): lax.all_to_all(blocks, axis, split_axis=0, concat_axis=0, tiled=True)  70.3 us
    scatter-add x2, other arithmetic, body(): row_terms = jnp.zeros((vector_count, row_tiles, tile_size), jnp.float32)....  52.3 us
    scatter-add x2, other arithmetic, body(): panel_part = jnp.zeros((vector_count, col_tiles, tile_size), jnp.float32)...  52.3 us
    all_to_all x3, blocking collectives, copy_for_each(): return lax.all_to_all(copies, axis, split_axis=0, concat_axis=0, tiled=True)  52 us
    dot_general x1, matrix products, body(): jnp.einsum('tij,tj->ti', pattern_f, slot_weight, precision=highest)  28.9 us
    dot_general x2, matrix products, body(): jnp.einsum('ktj,tij->kti', spread, pattern, preferred_element_type=jnp.fl...  27.4 us
    all_to_all x1, waiting for transfers between devices, sum_at_owner(): lax.all_to_all(blocks, axis, split_axis=0, concat_axis=0, tiled=True)  23.9 us
  transfers between devices with their start and end apart: 4, of which 1 were waited for; matrix products, arithmetic and copies ran while one was open for 14% of the time, Pallas kernels for 0%

commit v1 on v0

v1 whole, which is shorter than its diff:
```python
import functools

import jax
import jax.numpy as jnp
from jax import lax
from jax.experimental import pallas as pl
from jax.experimental.pallas import tpu as pltpu
from jax.sharding import Mesh
from jax.sharding import PartitionSpec as P

ITERS = 2
K = 64
TILE = 128
SLOTS = 256
ROW_TILES = 32
COL_TILES = 64
TOTAL_DOCS = 131072
OWN = 8
CHUNK = OWN * K
COUNT_ROWS = 16
UNROLL = 32
PREP_STEP = 32
MIB = 1 << 20

X, Z, CORE, BKT = "doc_0", "doc_1", "doc_2", "bkt"
DOC = (X, Z, CORE)
DOC_BKT = (X, Z, CORE, BKT)

f32 = jnp.float32
bf16 = jnp.bfloat16
SMEM = pl.BlockSpec(memory_space=pltpu.SMEM)
VMEM = pl.BlockSpec(memory_space=pltpu.VMEM)
HIGHEST = lax.Precision.HIGHEST


def shape(*lengths, dtype=f32):
    return jax.ShapeDtypeStruct(lengths, dtype)


def call(kernel, name, out_shape, in_specs, scratch=(), limit=8, flops=0, moved=0):
    return pl.pallas_call(
        kernel,
        out_shape=out_shape,
        in_specs=in_specs,
        out_specs=jax.tree.map(lambda _: VMEM, out_shape),
        scratch_shapes=list(scratch),
        compiler_params=pltpu.CompilerParams(vmem_limit_bytes=limit * MIB),
        cost_estimate=pl.CostEstimate(flops=flops, bytes_accessed=moved, transcendentals=0),
        name=name,
    )


def swap(value, axis, mask):
    size = lax.axis_size(axis)
    return lax.ppermute(value, axis, [(i, i ^ mask) for i in range(size)])


def place_of(place):
    return place[0], place[1], place[2], place[3], place[4]


def tile_rows(k):
    return slice(k * K, (k + 1) * K)


def cast_kernel(vectors, out):
    for k in range(OWN):
        out[tile_rows(k), :] = vectors[:, k * TILE : (k + 1) * TILE].astype(bf16)


def prep_kernel(place, coords, weight, pattern_in, pattern, doc_part, size_part, split, doc_acc, size_acc):
    step = pl.program_id(0)

    @pl.when(step == 0)
    def _():
        whole = weight[...]
        high = whole.astype(bf16).astype(f32)
        rest = whole - high
        middle = rest.astype(bf16).astype(f32)
        low = rest - middle
        rows = lax.broadcasted_iota(jnp.int32, split.shape, 1)
        spread = lambda part: jnp.broadcast_to(part[:, None, :], split.shape)
        terms = jnp.where(rows == 2, spread(low), 0.0)
        terms = jnp.where(rows == 1, spread(middle), terms)
        split[...] = jnp.where(rows == 0, spread(high), terms).astype(bf16)
        doc_acc[...] = jnp.zeros_like(doc_acc)
        size_acc[...] = jnp.zeros_like(size_acc)

    count = place[4]
    group = PREP_STEP
    for first in range(0, PREP_STEP, group):
        products, sums = [], []
        for u in range(first, first + group):
            slot = step * PREP_STEP + u
            tile = jnp.where(slot < count, pattern_in[u], 0).astype(f32)
            sums.append(jnp.sum(tile.reshape(TILE // 8, 8, TILE), axis=0))
            tile = tile.astype(bf16)
            pattern[u] = tile
            products.append(
                lax.dot_general(
                    split[coords[2 * slot + 1]],
                    tile,
                    (((1,), (1,)), ((), ())),
                    preferred_element_type=f32,
                )
            )
        for u in range(first, first + group):
            slot = step * PREP_STEP + u
            doc_acc[coords[2 * slot]] += products[u - first]
            size_acc[coords[2 * slot + 1]] += sums[u - first]

    @pl.when(step == pl.num_programs(0) - 1)
    def _():
        doc_part[...] = jnp.sum(doc_acc[...], axis=1)
        size_part[...] = jnp.sum(size_acc[...], axis=1)


def prep(place, coords, weight, patterns):
    block = pl.BlockSpec((PREP_STEP, TILE, TILE), lambda i: (i, 0, 0))
    return pl.pallas_call(
        prep_kernel,
        grid=(SLOTS // PREP_STEP,),
        out_shape=(
            shape(SLOTS, TILE, TILE, dtype=bf16),
            shape(ROW_TILES, TILE),
            shape(COL_TILES, TILE),
        ),
        in_specs=[SMEM, SMEM, VMEM, block],
        out_specs=(block, VMEM, VMEM),
        scratch_shapes=[
            pltpu.VMEM((COL_TILES, 16, TILE), bf16),
            pltpu.VMEM((ROW_TILES, 16, TILE), f32),
            pltpu.VMEM((COL_TILES, 8, TILE), f32),
        ],
        compiler_params=pltpu.CompilerParams(vmem_limit_bytes=16 * MIB),
        cost_estimate=pl.CostEstimate(flops=10**9, bytes_accessed=24 * MIB, transcendentals=0),
        name="prep",
    )(place, coords, weight, patterns)


def tile_products(coords, pattern, source, acc, forward):
    acc[...] = jnp.zeros_like(acc)
    contract = (((1,), (0,)), ((), ())) if forward else (((1,), (1,)), ((), ()))

    def group(g, carry):
        products = []
        for u in range(UNROLL):
            slot = g * UNROLL + u
            at = coords[2 * slot + (0 if forward else 1)]
            products.append(
                lax.dot_general(source[at], pattern[slot], contract, preferred_element_type=f32)
            )
        for u in range(UNROLL):
            slot = g * UNROLL + u
            acc[coords[2 * slot + (1 if forward else 0)]] += products[u]
        return carry

    lax.fori_loop(0, SLOTS // UNROLL, group, 0)


def forward_kernel(first, *refs):
    if first:
        place, coords, x0, x1, x2, x3, d0, d1, d2, d3, sizes, pattern, keep, send, inv, source, acc = refs
    else:
        place, coords, x0, x1, x2, x3, pattern, keep, send, source, acc = refs
    x, z, c, y, _ = place_of(place)
    if first:
        inv[...] = 1.0 / jnp.sqrt(jnp.maximum((d0[...] + d1[...]) + (d2[...] + d3[...]), 1.0))
    for s, block in enumerate((x0, x1, x2, x3)):
        base = (y ^ s) * OWN
        for k in range(OWN):
            tile = block[tile_rows(k), :]
            if first:
                tile = (tile.astype(f32) * inv[pl.ds(base + k, 1), :]).astype(bf16)
            source[base + k] = tile
    tile_products(coords, pattern, source, acc, True)
    for out, half in ((keep, c), (send, 1 - c)):
        for r in range(4):
            base = half * (COL_TILES // 2) + (x ^ r) * OWN
            for k in range(OWN):
                out[r, tile_rows(k), :] = acc[base + k].astype(out.dtype)
            if first:
                counts = jnp.concatenate(
                    [sizes[pl.ds(pl.multiple_of(base, OWN), OWN), :], jnp.zeros((COUNT_ROWS - OWN, TILE), f32)], axis=0
                )
                out[r, CHUNK : CHUNK + COUNT_ROWS, :] = counts.astype(out.dtype)


def forward(first, place, coords, blocks, degrees, sizes, pattern):
    rows = CHUNK + (COUNT_ROWS if first else 0)
    outs = [shape(4, rows, TILE), shape(4, rows, TILE, dtype=bf16)]
    if first:
        outs.append(shape(ROW_TILES, TILE))
    args = [*blocks, *degrees, sizes, pattern] if first else [*blocks, pattern]
    return call(
        functools.partial(forward_kernel, first),
        "forward",
        tuple(outs),
        [SMEM, SMEM] + [VMEM] * len(args),
        scratch=[pltpu.VMEM((ROW_TILES, K, TILE), bf16), pltpu.VMEM((COL_TILES, K, TILE), f32)],
        limit=20,
        flops=6 * 10**9,
        moved=12 * MIB,
    )(place, coords, *args)


def halves_kernel(keep, arrived, own, s1, s2, s3):
    for r, out in enumerate((own, s1, s2, s3)):
        out[...] = (keep[r] + arrived[r].astype(f32)).astype(out.dtype)


def halves(keep, arrived):
    rows = keep.shape[1]
    outs = [shape(rows, TILE)] + [shape(rows, TILE, dtype=bf16)] * 3
    return call(halves_kernel, "halves", tuple(outs), [VMEM] * 2, moved=3 * MIB)(keep, arrived)


def total_kernel(own, r1, r2, r3, out):
    total = (own[...] + r1[...].astype(f32)) + (r2[...].astype(f32) + r3[...].astype(f32))
    out[...] = total.astype(bf16)


def weigh_kernel(first, *refs):
    if first:
        place, p0, p1, p2, p3, weight, weighted, scale = refs
    else:
        place, p0, p1, p2, p3, scale, factor, weighted = refs
    add = lambda at: (p0[at, :].astype(f32) + p1[at, :].astype(f32)) + (p2[at, :].astype(f32) + p3[at, :].astype(f32))
    if first:
        x, z, c, y, _ = place_of(place)
        base = pl.multiple_of(c * (COL_TILES // 2) + x * OWN, OWN)
        counts = add(slice(CHUNK, CHUNK + COUNT_ROWS))[:OWN]
        scale[...] = weight[pl.ds(base, OWN), :] / jnp.maximum(counts, 1.0)
    for k in range(OWN):
        tile = add(tile_rows(k))
        if not first:
            tile = jnp.dot(factor[...], tile, precision=HIGHEST, preferred_element_type=f32)
        weighted[tile_rows(k), :] = (tile * scale[k : k + 1, :]).astype(bf16)


def backward_kernel(place, coords, w0, w1, w2, w3, other, pattern, own, s1, s2, s3, source, acc):
    x, z, c, y, _ = place_of(place)
    for r, block in enumerate((w0, w1, w2, w3)):
        base = c * (COL_TILES // 2) + (x ^ r) * OWN
        far = (1 - c) * (COL_TILES // 2) + (x ^ r) * OWN
        for k in range(OWN):
            source[base + k] = block[tile_rows(k), :]
            source[far + k] = other[r, tile_rows(k), :]
    tile_products(coords, pattern, source, acc, False)
    for s, out in enumerate((own, s1, s2, s3)):
        base = (y ^ s) * OWN
        for k in range(OWN):
            out[tile_rows(k), :] = acc[base + k].astype(out.dtype)


def backward(place, coords, blocks, other, pattern):
    outs = [shape(CHUNK, TILE)] + [shape(CHUNK, TILE, dtype=bf16)] * 3
    return call(
        backward_kernel,
        "backward",
        tuple(outs),
        [SMEM, SMEM] + [VMEM] * 6,
        scratch=[pltpu.VMEM((COL_TILES, K, TILE), bf16), pltpu.VMEM((ROW_TILES, K, TILE), f32)],
        limit=20,
        flops=6 * 10**9,
        moved=12 * MIB,
    )(place, coords, *blocks, other, pattern)


def image_kernel(last, place, own, r1, r2, r3, inv, image, gram, *scaled):
    x, z, c, y, _ = place_of(place)
    inv_own = inv[pl.ds(pl.multiple_of(y * OWN, OWN), OWN), :]
    total = jnp.zeros((K, K), f32)
    for k in range(OWN):
        at = tile_rows(k)
        tile = (own[at, :] + r1[at, :].astype(f32)) + (r2[at, :].astype(f32) + r3[at, :].astype(f32))
        tile = tile * inv_own[k : k + 1, :]
        image[at, :] = tile
        if not last:
            scaled[0][at, :] = (tile * inv_own[k : k + 1, :]).astype(bf16)
        total += lax.dot_general(
            tile, tile, (((1,), (1,)), ((), ())), precision=HIGHEST, preferred_element_type=f32
        )
    gram[...] = total / TOTAL_DOCS


def inverse_factor_kernel(gram, out):
    work = jnp.concatenate([gram[...], jnp.eye(K, dtype=f32)], axis=1)
    rows = lax.broadcasted_iota(jnp.int32, (K, 1), 0)
    for k in range(K):
        pivot = work[k : k + 1, :]
        ratio = jnp.where(rows > k, work[:, k : k + 1] / pivot[:, k : k + 1], 0.0)
        work = work - ratio * pivot
    diagonal = lax.broadcasted_iota(jnp.int32, (K, K), 0) == lax.broadcasted_iota(jnp.int32, (K, K), 1)
    pivots = jnp.sum(jnp.where(diagonal, work[:, :K], 0.0), axis=1, keepdims=True)
    out[...] = work[:, K:] / jnp.sqrt(pivots)


def solve_kernel(factor, image, out):
    for k in range(OWN):
        out[:, k * TILE : (k + 1) * TILE] = jnp.dot(
            factor[...], image[tile_rows(k), :], precision=HIGHEST, preferred_element_type=f32
        )


def swapped(values, axis):
    return [swap(value, axis, s + 1) for s, value in enumerate(values)]


def body(start_vectors, bucket_weight, tile_count, tile_coords, patterns):
    place = jnp.stack([lax.axis_index(a) for a in DOC_BKT] + [tile_count[0, 0]]).astype(jnp.int32)
    coords = tile_coords.reshape(2 * SLOTS)
    weight = bucket_weight.reshape(COL_TILES, TILE)
    chunk = shape(CHUNK, TILE)
    chunk_b = shape(CHUNK, TILE, dtype=bf16)

    block = call(cast_kernel, "cast", chunk_b, [VMEM])(start_vectors)
    blocks = [block] + [swap(block, BKT, s) for s in (1, 2, 3)]
    pattern, doc_part, size_part = prep(place, coords, weight, patterns.reshape(SLOTS, TILE, TILE))
    degrees = [doc_part] + [swap(doc_part, BKT, s) for s in (1, 2, 3)]
    inv = scale = factor = None
    for sweep in range(ITERS):
        first, last = sweep == 0, sweep == ITERS - 1
        outs = forward(first, place, coords, blocks, degrees, size_part, pattern)
        if first:
            keep, send, inv = outs
        else:
            keep, send = outs
        own, *parts = halves(keep, swap(send, CORE, 1))
        parts = swapped(parts, X)
        part = call(total_kernel, "total", shape(*own.shape, dtype=bf16), [VMEM] * 4)(own, *parts)
        parts = [part] + [swap(part, Z, s) for s in (1, 2, 3)]
        if first:
            weighted, scale = call(
                functools.partial(weigh_kernel, True), "weigh", (chunk_b, shape(OWN, TILE)), [SMEM] + [VMEM] * 5
            )(place, *parts, weight)
        else:
            weighted = call(functools.partial(weigh_kernel, False), "weigh", chunk_b, [SMEM] + [VMEM] * 6)(
                place, *parts, scale, factor
            )
        mine = [weighted] + [swap(weighted, X, s) for s in (1, 2, 3)]
        other = swap(jnp.stack(mine), CORE, 1)
        own, *parts = backward(place, coords, mine, other, pattern)
        outs = (chunk, shape(K, K)) + (() if last else (chunk_b,))
        outs = call(functools.partial(image_kernel, last), "image", outs, [SMEM] + [VMEM] * 5)(
            place, own, *swapped(parts, BKT), inv
        )
        image, gram = outs[:2]
        if not last:
            blocks = [outs[2]] + [swap(outs[2], BKT, s) for s in (1, 2, 3)]
        for axis, mask in ((CORE, 1), (BKT, 1), (BKT, 3), (X, 1), (X, 3), (Z, 1), (Z, 3)):
            gram = gram + swap(gram, axis, mask)
        factor = call(inverse_factor_kernel, "inverse_factor", shape(K, K), [VMEM])(gram)
    return call(solve_kernel, "solve", shape(K, OWN * TILE), [VMEM] * 2)(factor, image)


def solution(mesh):
    split = Mesh(mesh.devices.reshape(4, 4, 2, mesh.shape[BKT]), DOC_BKT)
    in_specs = (
        P(None, DOC_BKT),
        P(BKT),
        P(DOC, BKT),
        P(DOC, BKT, None, None),
        P(DOC, BKT, None, None, None),
    )
    return jax.shard_map(body, mesh=split, in_specs=in_specs, out_specs=P(None, DOC_BKT), check_vma=False)
```

time: 583 us -> 225 us (0.39); the launches traced: 574 us -> 225 us
  blocking collectives: 223 us -> 0 us
  other arithmetic: 152 us -> 0.21 us
  matrix products: 93.5 us -> 0 us
  waiting for transfers between devices: 23.9 us -> 106 us
  local copies, waits for them, and re-layouts: 55.2 us -> 8.53 us
  Pallas kernels: 0 us -> 46 us
  starting transfers between devices: 25.7 us -> 63.2 us
    all_to_all x6 -> x0, blocking collectives: 122 us -> none  [the longest x3 70.3 us: sum_at_owner(): lax.all_to_all(blocks, axis, split_axis=0, concat_axis=0, tiled=True)]
    ppermute x0 -> x51, waiting for transfers between devices: none -> 106 us  [swap(): return lax.ppermute(value, axis, [(i, i ^ mask) for i in range(size)])]
    scatter-add x4 -> x0, other arithmetic: 105 us -> none  [the longest x2 52.3 us: body(): row_terms = jnp.zeros((vector_count, row_tiles, tile_size), jnp.float32)....]
    psum x8 -> x0, blocking collectives: 100 us -> none  [over_axes(): return functools.reduce(lax.psum, axes, shard)]
    dot_general x14 -> x0, matrix products: 91.9 us -> none  [the longest x1 28.9 us: body(): jnp.einsum('tij,tj->ti', pattern_f, slot_weight, precision=highest)]
    ppermute x0 -> x51, starting transfers between devices: none -> 63.2 us  [swap(): return lax.ppermute(value, axis, [(i, i ^ mask) for i in range(size)])]
    pallas_call x0 -> x17, Pallas kernels: none -> 46 us  [the longest x2 14.7 us: backward(): call(backward_kernel, 'backward', tuple(outs), [SMEM, SMEM] + [VMEM] * 6,...]
    convert_element_type x4 -> x0, local copies, waits for them, and re-layouts: 26.4 us -> none  [the longest x2 13.2 us: body(): picked = jnp.einsum('rt,kri->kti', row_pick_b, band_vecs.reshape(vector_c...]
  transfers between devices with their start and end apart: 4 -> 51, of which waited for: 1 -> 41; matrix products, arithmetic and copies ran while one was open for 14% -> 0% of each run, Pallas kernels for 0% -> 5%
where the time goes in v1:
time: 225 us
  waiting for transfers between devices  106 us (47%)
  starting transfers between devices  63.2 us (28%)
  Pallas kernels  46 us (20%)
  local copies, waits for them, and re-layouts  8.53 us (4%)
    ppermute x51, waiting for transfers between devices, swap(): return lax.ppermute(value, axis, [(i, i ^ mask) for i in range(size)])  106 us
    ppermute x51, starting transfers between devices, swap(): return lax.ppermute(value, axis, [(i, i ^ mask) for i in range(size)])  63.2 us
    pallas_call x2, Pallas kernels, backward(): call(backward_kernel, 'backward', tuple(outs), [SMEM, SMEM] + [VMEM] * 6,...  14.7 us
    pallas_call x2, Pallas kernels, body(): call(inverse_factor_kernel, 'inverse_factor', shape(K, K), [VMEM])(gram)  10.9 us
    pallas_call x2, Pallas kernels, forward(): call(functools.partial(forward_kernel, first), 'forward', tuple(outs), [S...  8.52 us
    unnamed x9, local copies, waits for them, and re-layouts  8.29 us
    pallas_call x1, Pallas kernels, prep(): pl.pallas_call(prep_kernel, grid=(SLOTS // PREP_STEP,), out_shape=(shape(...  6.24 us
  transfers between devices with their start and end apart: 51, of which 41 were waited for; matrix products, arithmetic and copies ran while one was open for 0% of the time, Pallas kernels for 5%

profile of v1, /device:TPU:0, one launch (start us, length us, event | category | flops | bytes accessed | tf_op | source)
XLA Modules:
  0.0 225.1 jit_solution(15582018035726951273)
XLA Ops:
  1.0 3.2 %collective-permute-start.2 = (bf16[512,128]{1,0:T(8,128)(2,1)S(1)}, bf16[512,128]{1,0:T(8,128)(2,1)S(1)}, u32[]{:S(2)}, u32[]{:S(2)}) collective-permute-start(bf16[512,128]{1,0:T(8,128)(2,1)S(1)} %cast.1.refs_2_), channel_id=1, source_target_pairs={{0,3},{1,2},{2,1},{3,0},{4,7},{5,6},{6,5},{7,4},{8,11},{9,10},{10,... | collective-permute-start | bytes 393224 | tf_op jit(solution)/shard_map/ppermute | solution.py:55
  6.9 5.8 %copy-done = s32[1,1,256,128,128]{4,3,2,1,0:T(8,128)S(1)} copy-done((s32[1,1,256,128,128]{4,3,2,1,0:T(8,128)S(1)}, s32[1,1,256,128,128]{4,3,2,1,0:T(8,128)}, u32[]{:S(2)}) %copy-start) | copy-done | bytes 16777240
  13.4 6.2 %prep.1 = (bf16[256,128,128]{2,1,0:T(8,128)(2,1)S(1)}, f32[32,128]{1,0:T(8,128)S(1)}, f32[64,128]{1,0:T(8,128)S(1)}) custom-call(s32[5]{0:T(128)S(1)} %stack.49.place.refs_0_, s32[512]{0:T(512)S(1)} %reshape.9.coords.refs_1_, f32[64,128]{1,0:T(8,128)S(1)} %bitcast.20, s32[256,128,128]{2,1,0:T(8,128)S(1)} %bitcast.18), custom_call_target="tpu_custom_call" | custom-call | flops 1000000000 | bytes 25165824 | tf_op jit(solution)/shard_map/prep/pallas_call | solution.py:120
  19.6 3.2 %collective-permute-start.5 = (f32[32,128]{1,0:T(8,128)S(1)}, f32[32,128]{1,0:T(8,128)S(1)}, u32[]{:S(2)}, u32[]{:S(2)}) collective-permute-start(f32[32,128]{1,0:T(8,128)S(1)} %get-tuple-element.35.refs_6_), channel_id=1, source_target_pairs={{0,3},{1,2},{2,1},{3,0},{4,7},{5,6},{6,5},{7,4},{8,11},{9,10},{10,... | collective-permute-start | bytes 49160 | tf_op jit(solution)/shard_map/ppermute | solution.py:55
  25.1 2.9 %collective-permute-done.4.refs_8_ = f32[32,128]{1,0:T(8,128)S(1)} collective-permute-done((f32[32,128]{1,0:T(8,128)S(1)}, f32[32,128]{1,0:T(8,128)S(1)}, u32[]{:S(2)}, u32[]{:S(2)}) %collective-permute-start.4) | collective-permute-done | bytes 16416 | tf_op jit(solution)/shard_map/ppermute | solution.py:55
  28.4 4.3 %forward.2 = (f32[4,528,128]{2,1,0:T(8,128)S(1)}, bf16[4,528,128]{2,1,0:T(8,128)(2,1)S(1)}, f32[32,128]{1,0:T(8,128)S(1)}) custom-call(s32[5]{0:T(128)S(1)} %stack.49.place.refs_0_, s32[512]{0:T(512)S(1)} %reshape.9.coords.refs_1_, bf16[512,128]{1,0:T(8,128)(2,1)S(1)} %cast.1.refs_2_, bf16[512,128]{1,0:T(8,128)(2,1)S(1)} %collective-permute-done.refs_3_, ...), custom_call_target="tpu_custom_call" | custom-call | flops 6000000000 | bytes 12582912 | tf_op jit(solution)/shard_map/forward/pallas_call | solution.py:195
  41.2 4.7 %collective-permute-done.8.r2 = bf16[528,128]{1,0:T(8,128)(2,1)S(1)} collective-permute-done((bf16[528,128]{1,0:T(8,128)(2,1)S(1)}, bf16[528,128]{1,0:T(8,128)(2,1)S(1)}, u32[]{:S(2)}, u32[]{:S(2)}) %collective-permute-start.8) | collective-permute-done | bytes 135200 | tf_op jit(solution)/shard_map/ppermute | solution.py:55
  48.2 4.1 %collective-permute-start.12 = (bf16[528,128]{1,0:T(8,128)(2,1)S(1)}, bf16[528,128]{1,0:T(8,128)(2,1)S(1)}, u32[]{:S(2)}, u32[]{:S(2)}) collective-permute-start(bf16[528,128]{1,0:T(8,128)(2,1)S(1)} %total.2.refs_1_), channel_id=1, source_target_pairs={{0,24},{8,16},{16,8},{24,0},{1,25},{9,17},{17,9},{25,1},{2,26},{10... | collective-permute-start | bytes 405512 | tf_op jit(solution)/shard_map/ppermute | solution.py:55
  53.3 4.4 %collective-permute-done.12.refs_4_ = bf16[528,128]{1,0:T(8,128)(2,1)S(1)} collective-permute-done((bf16[528,128]{1,0:T(8,128)(2,1)S(1)}, bf16[528,128]{1,0:T(8,128)(2,1)S(1)}, u32[]{:S(2)}, u32[]{:S(2)}) %collective-permute-start.12) | collective-permute-done | bytes 135200 | tf_op jit(solution)/shard_map/ppermute | solution.py:55
  61.7 3.1 %collective-permute-start.13 = (bf16[512,128]{1,0:T(8,128)(2,1)S(1)}, bf16[512,128]{1,0:T(8,128)(2,1)S(1)}, u32[]{:S(2)}, u32[]{:S(2)}) collective-permute-start(bf16[512,128]{1,0:T(8,128)(2,1)S(1)} %get-tuple-element.44.w0), channel_id=1, source_target_pairs={{0,32},{32,0},{64,96},{96,64},{1,33},{33,1},{65,97},{97,65},{2,34}... | collective-permute-start | bytes 393224 | tf_op jit(solution)/shard_map/ppermute | solution.py:55
  64.8 3.5 %collective-permute-done.15.w3 = bf16[512,128]{1,0:T(8,128)(2,1)S(1)} collective-permute-done((bf16[512,128]{1,0:T(8,128)(2,1)S(1)}, bf16[512,128]{1,0:T(8,128)(2,1)S(1)}, u32[]{:S(2)}, u32[]{:S(2)}) %collective-permute-start.15) | collective-permute-done | bytes 131104 | tf_op jit(solution)/shard_map/ppermute | solution.py:55
  71.2 7.3 %backward.2 = (f32[512,128]{1,0:T(8,128)S(1)}, bf16[512,128]{1,0:T(8,128)(2,1)S(1)}, bf16[512,128]{1,0:T(8,128)(2,1)S(1)}, bf16[512,128]{1,0:T(8,128)(2,1)S(1)}) custom-call(s32[5]{0:T(128)S(1)} %stack.49.place.refs_0_, s32[512]{0:T(512)S(1)} %reshape.9.coords.refs_1_, bf16[512,128]{1,0:T(8,128)(2,1)S(1)} %get-tuple-element.44.w0, ...), custom_call_target="tpu_custom_call" | custom-call | flops 6000000000 | bytes 12582912 | tf_op jit(solution)/shard_map/backward/pallas_call | solution.py:258
  79.0 4.1 %collective-permute-start.18 = (bf16[512,128]{1,0:T(8,128)(2,1)S(1)}, bf16[512,128]{1,0:T(8,128)(2,1)S(1)}, u32[]{:S(2)}, u32[]{:S(2)}) collective-permute-start(bf16[512,128]{1,0:T(8,128)(2,1)S(1)} %get-tuple-element.47), channel_id=1, source_target_pairs={{0,2},{1,3},{2,0},{3,1},{4,6},{5,7},{6,4},{7,5},{8,10},{9,11},{10,... | collective-permute-start | bytes 393224 | tf_op jit(solution)/shard_map/ppermute | solution.py:55
  84.9 4.6 %collective-permute-done.18.r2 = bf16[512,128]{1,0:T(8,128)(2,1)S(1)} collective-permute-done((bf16[512,128]{1,0:T(8,128)(2,1)S(1)}, bf16[512,128]{1,0:T(8,128)(2,1)S(1)}, u32[]{:S(2)}, u32[]{:S(2)}) %collective-permute-start.18) | collective-permute-done | bytes 131104 | tf_op jit(solution)/shard_map/ppermute | solution.py:55
  94.2 3.1 %collective-permute-start.20 = (bf16[512,128]{1,0:T(8,128)(2,1)S(1)}, bf16[512,128]{1,0:T(8,128)(2,1)S(1)}, u32[]{:S(2)}, u32[]{:S(2)}) collective-permute-start(bf16[512,128]{1,0:T(8,128)(2,1)S(1)} %get-tuple-element.50.refs_2_), channel_id=1, source_target_pairs={{0,1},{1,0},{2,3},{3,2},{4,5},{5,4},{6,7},{7,6},{8,9},{9,8},{10,11... | collective-permute-start | bytes 393224 | tf_op jit(solution)/shard_map/ppermute | solution.py:55
  97.4 4.8 %collective-permute-done.22.refs_5_ = bf16[512,128]{1,0:T(8,128)(2,1)S(1)} collective-permute-done((bf16[512,128]{1,0:T(8,128)(2,1)S(1)}, bf16[512,128]{1,0:T(8,128)(2,1)S(1)}, u32[]{:S(2)}, u32[]{:S(2)}) %collective-permute-start.22) | collective-permute-done | bytes 131104 | tf_op jit(solution)/shard_map/ppermute | solution.py:55
  102.8 4.2 %forward.3 = (f32[4,512,128]{2,1,0:T(8,128)S(1)}, bf16[4,512,128]{2,1,0:T(8,128)(2,1)S(1)}) custom-call(s32[5]{0:T(128)S(1)} %stack.49.place.refs_0_, s32[512]{0:T(512)S(1)} %reshape.9.coords.refs_1_, bf16[512,128]{1,0:T(8,128)(2,1)S(1)} %get-tuple-element.50.refs_2_, bf16[512,128]{1,0:T(8,128)(2,1)S(1)} %collective-permute-done.20.refs_3_, ...), custom_call_target="tpu_custom_call" | custom-call | flops 6000000000 | bytes 12582912 | tf_op jit(solution)/shard_map/forward/pallas_call | solution.py:195
  115.5 2.8 %collective-permute-done.25.r2 = bf16[512,128]{1,0:T(8,128)(2,1)S(1)} collective-permute-done((bf16[512,128]{1,0:T(8,128)(2,1)S(1)}, bf16[512,128]{1,0:T(8,128)(2,1)S(1)}, u32[]{:S(2)}, u32[]{:S(2)}) %collective-permute-start.25) | collective-permute-done | bytes 131104 | tf_op jit(solution)/shard_map/ppermute | solution.py:55
  126.0 3.9 %collective-permute-done.31 = f32[64,64]{1,0:T(8,128)S(1)} collective-permute-done((f32[64,64]{1,0:T(8,128)S(1)}, f32[64,64]{1,0:T(8,128)S(1)}, u32[]{:S(2)}, u32[]{:S(2)}) %collective-permute-start.31) | collective-permute-done | bytes 16416 | tf_op jit(solution)/shard_map/ppermute | solution.py:55
  131.2 3.9 %collective-permute-done.32 = f32[64,64]{1,0:T(8,128)S(1)} collective-permute-done((f32[64,64]{1,0:T(8,128)S(1)}, f32[64,64]{1,0:T(8,128)S(1)}, u32[]{:S(2)}, u32[]{:S(2)}) %collective-permute-start.32) | collective-permute-done | bytes 16416 | tf_op jit(solution)/shard_map/ppermute | solution.py:55
  135.1 3.9 %collective-permute-done.33 = f32[64,64]{1,0:T(8,128)S(1)} collective-permute-done((f32[64,64]{1,0:T(8,128)S(1)}, f32[64,64]{1,0:T(8,128)S(1)}, u32[]{:S(2)}, u32[]{:S(2)}) %collective-permute-start.33) | collective-permute-done | bytes 16416 | tf_op jit(solution)/shard_map/ppermute | solution.py:55
  141.0 3.2 %collective-permute-done.34 = f32[64,64]{1,0:T(8,128)S(1)} collective-permute-done((f32[64,64]{1,0:T(8,128)S(1)}, f32[64,64]{1,0:T(8,128)S(1)}, u32[]{:S(2)}, u32[]{:S(2)}) %collective-permute-start.34) | collective-permute-done | bytes 16416 | tf_op jit(solution)/shard_map/ppermute | solution.py:55
  144.7 3.4 %collective-permute-done.35 = f32[64,64]{1,0:T(8,128)S(1)} collective-permute-done((f32[64,64]{1,0:T(8,128)S(1)}, f32[64,64]{1,0:T(8,128)S(1)}, u32[]{:S(2)}, u32[]{:S(2)}) %collective-permute-start.35) | collective-permute-done | bytes 16416 | tf_op jit(solution)/shard_map/ppermute | solution.py:55
  153.2 5.5 %inverse_factor.2.refs_6_ = f32[64,64]{1,0:T(8,128)S(1)} custom-call(f32[64,64]{1,0:T(8,128)S(1)} %add.48.gram), custom_call_target="tpu_custom_call" | custom-call | tf_op jit(solution)/shard_map/inverse_factor/pallas_call | solution.py:353
  170.2 7.3 %backward.3 = (f32[512,128]{1,0:T(8,128)S(1)}, bf16[512,128]{1,0:T(8,128)(2,1)S(1)}, bf16[512,128]{1,0:T(8,128)(2,1)S(1)}, bf16[512,128]{1,0:T(8,128)(2,1)S(1)}) custom-call(s32[5]{0:T(128)S(1)} %stack.49.place.refs_0_, s32[512]{0:T(512)S(1)} %reshape.9.coords.refs_1_, bf16[512,128]{1,0:T(8,128)(2,1)S(1)} %weigh.3.w0, ...), custom_call_target="tpu_custom_call" | custom-call | flops 6000000000 | bytes 12582912 | tf_op jit(solution)/shard_map/backward/pallas_call | solution.py:258
  183.9 2.8 %collective-permute-done.42.r2 = bf16[512,128]{1,0:T(8,128)(2,1)S(1)} collective-permute-done((bf16[512,128]{1,0:T(8,128)(2,1)S(1)}, bf16[512,128]{1,0:T(8,128)(2,1)S(1)}, u32[]{:S(2)}, u32[]{:S(2)}) %collective-permute-start.42) | collective-permute-done | bytes 131104 | tf_op jit(solution)/shard_map/ppermute | solution.py:55
  191.4 3.9 %collective-permute-done.45 = f32[64,64]{1,0:T(8,128)S(1)} collective-permute-done((f32[64,64]{1,0:T(8,128)S(1)}, f32[64,64]{1,0:T(8,128)S(1)}, u32[]{:S(2)}, u32[]{:S(2)}) %collective-permute-start.45) | collective-permute-done | bytes 16416 | tf_op jit(solution)/shard_map/ppermute | solution.py:55
  197.3 3.2 %collective-permute-done.46 = f32[64,64]{1,0:T(8,128)S(1)} collective-permute-done((f32[64,64]{1,0:T(8,128)S(1)}, f32[64,64]{1,0:T(8,128)S(1)}, u32[]{:S(2)}, u32[]{:S(2)}) %collective-permute-start.46) | collective-permute-done | bytes 16416 | tf_op jit(solution)/shard_map/ppermute | solution.py:55
  201.1 3.3 %collective-permute-done.47 = f32[64,64]{1,0:T(8,128)S(1)} collective-permute-done((f32[64,64]{1,0:T(8,128)S(1)}, f32[64,64]{1,0:T(8,128)S(1)}, u32[]{:S(2)}, u32[]{:S(2)}) %collective-permute-start.47) | collective-permute-done | bytes 16416 | tf_op jit(solution)/shard_map/ppermute | solution.py:55
  206.3 3.2 %collective-permute-done.48 = f32[64,64]{1,0:T(8,128)S(1)} collective-permute-done((f32[64,64]{1,0:T(8,128)S(1)}, f32[64,64]{1,0:T(8,128)S(1)}, u32[]{:S(2)}, u32[]{:S(2)}) %collective-permute-start.48) | collective-permute-done | bytes 16416 | tf_op jit(solution)/shard_map/ppermute | solution.py:55
  209.5 3.9 %collective-permute-done.49 = f32[64,64]{1,0:T(8,128)S(1)} collective-permute-done((f32[64,64]{1,0:T(8,128)S(1)}, f32[64,64]{1,0:T(8,128)S(1)}, u32[]{:S(2)}, u32[]{:S(2)}) %collective-permute-start.49) | collective-permute-done | bytes 16416 | tf_op jit(solution)/shard_map/ppermute | solution.py:55
  218.5 5.5 %inverse_factor.3.factor = f32[64,64]{1,0:T(8,128)S(1)} custom-call(f32[64,64]{1,0:T(8,128)S(1)} %add.55.gram), custom_call_target="tpu_custom_call" | custom-call | tf_op jit(solution)/shard_map/inverse_factor/pallas_call | solution.py:353
  (114 shorter events, 91.0 us)
Async XLA Ops:
  1.0 27.4 %collective-permute-start.2 = (bf16[512,128]{1,0:T(8,128)(2,1)S(1)}, bf16[512,128]{1,0:T(8,128)(2,1)S(1)}, u32[]{:S(2)}, u32[]{:S(2)}) collective-permute-start(bf16[512,128]{1,0:T(8,128)(2,1)S(1)} %cast.1.refs_2_), channel_id=1, source_target_pairs={{0,3},{1,2},{2,1},{3,0},{4,7},{5,6},{6,5},{7,4},{8,11},{9,10},{10,... | collective-permute-start | bytes 393224 | tf_op jit(solution)/shard_map/ppermute | solution.py:55
  4.1 24.3 %collective-permute-start.1 = (bf16[512,128]{1,0:T(8,128)(2,1)S(1)}, bf16[512,128]{1,0:T(8,128)(2,1)S(1)}, u32[]{:S(2)}, u32[]{:S(2)}) collective-permute-start(bf16[512,128]{1,0:T(8,128)(2,1)S(1)} %cast.1.refs_2_), channel_id=1, source_target_pairs={{0,2},{1,3},{2,0},{3,1},{4,6},{5,7},{6,4},{7,5},{8,10},{9,11},{10,... | collective-permute-start | bytes 393224 | tf_op jit(solution)/shard_map/ppermute | solution.py:55
  4.8 23.6 %collective-permute-start = (bf16[512,128]{1,0:T(8,128)(2,1)S(1)}, bf16[512,128]{1,0:T(8,128)(2,1)S(1)}, u32[]{:S(2)}, u32[]{:S(2)}) collective-permute-start(bf16[512,128]{1,0:T(8,128)(2,1)S(1)} %cast.1.refs_2_), channel_id=1, source_target_pairs={{0,1},{1,0},{2,3},{3,2},{4,5},{5,4},{6,7},{7,6},{8,9},{9,8},{10,11... | collective-permute-start | bytes 393224 | tf_op jit(solution)/shard_map/ppermute | solution.py:55
  22.8 5.2 %collective-permute-start.4 = (f32[32,128]{1,0:T(8,128)S(1)}, f32[32,128]{1,0:T(8,128)S(1)}, u32[]{:S(2)}, u32[]{:S(2)}) collective-permute-start(f32[32,128]{1,0:T(8,128)S(1)} %get-tuple-element.35.refs_6_), channel_id=1, source_target_pairs={{0,2},{1,3},{2,0},{3,1},{4,6},{5,7},{6,4},{7,5},{8,10},{9,11},{10,... | collective-permute-start | bytes 49160 | tf_op jit(solution)/shard_map/ppermute | solution.py:55
  34.9 6.3 %collective-permute-start.7 = (bf16[528,128]{1,0:T(8,128)(2,1)S(1)}, bf16[528,128]{1,0:T(8,128)(2,1)S(1)}, u32[]{:S(2)}, u32[]{:S(2)}) collective-permute-start(bf16[528,128]{1,0:T(8,128)(2,1)S(1)} %get-tuple-element.41), channel_id=1, source_target_pairs={{0,32},{32,0},{64,96},{96,64},{1,33},{33,1},{65,97},{97,65},{2,34}... | collective-permute-start | bytes 405512 | tf_op jit(solution)/shard_map/ppermute | solution.py:55
  36.5 9.3 %collective-permute-start.8 = (bf16[528,128]{1,0:T(8,128)(2,1)S(1)}, bf16[528,128]{1,0:T(8,128)(2,1)S(1)}, u32[]{:S(2)}, u32[]{:S(2)}) collective-permute-start(bf16[528,128]{1,0:T(8,128)(2,1)S(1)} %get-tuple-element.42), channel_id=1, source_target_pairs={{0,64},{32,96},{64,0},{96,32},{1,65},{33,97},{65,1},{97,33},{2,66}... | collective-permute-start | bytes 405512 | tf_op jit(solution)/shard_map/ppermute | solution.py:55
  39.3 8.9 %collective-permute-start.9 = (bf16[528,128]{1,0:T(8,128)(2,1)S(1)}, bf16[528,128]{1,0:T(8,128)(2,1)S(1)}, u32[]{:S(2)}, u32[]{:S(2)}) collective-permute-start(bf16[528,128]{1,0:T(8,128)(2,1)S(1)} %get-tuple-element.43), channel_id=1, source_target_pairs={{0,96},{32,64},{64,32},{96,0},{1,97},{33,65},{65,33},{97,1},{2,98}... | collective-permute-start | bytes 405512 | tf_op jit(solution)/shard_map/ppermute | solution.py:55
  48.2 9.5 %collective-permute-start.12 = (bf16[528,128]{1,0:T(8,128)(2,1)S(1)}, bf16[528,128]{1,0:T(8,128)(2,1)S(1)}, u32[]{:S(2)}, u32[]{:S(2)}) collective-permute-start(bf16[528,128]{1,0:T(8,128)(2,1)S(1)} %total.2.refs_1_), channel_id=1, source_target_pairs={{0,24},{8,16},{16,8},{24,0},{1,25},{9,17},{17,9},{25,1},{2,26},{10... | collective-permute-start | bytes 405512 | tf_op jit(solution)/shard_map/ppermute | solution.py:55
  52.3 7.6 %collective-permute-start.11 = (bf16[528,128]{1,0:T(8,128)(2,1)S(1)}, bf16[528,128]{1,0:T(8,128)(2,1)S(1)}, u32[]{:S(2)}, u32[]{:S(2)}) collective-permute-start(bf16[528,128]{1,0:T(8,128)(2,1)S(1)} %total.2.refs_1_), channel_id=1, source_target_pairs={{0,16},{8,24},{16,0},{24,8},{1,17},{9,25},{17,1},{25,9},{2,18},{10... | collective-permute-start | bytes 405512 | tf_op jit(solution)/shard_map/ppermute | solution.py:55
  52.3 7.6 %collective-permute-start.10 = (bf16[528,128]{1,0:T(8,128)(2,1)S(1)}, bf16[528,128]{1,0:T(8,128)(2,1)S(1)}, u32[]{:S(2)}, u32[]{:S(2)}) collective-permute-start(bf16[528,128]{1,0:T(8,128)(2,1)S(1)} %total.2.refs_1_), channel_id=1, source_target_pairs={{0,8},{8,0},{16,24},{24,16},{1,9},{9,1},{17,25},{25,17},{2,10},{10... | collective-permute-start | bytes 405512 | tf_op jit(solution)/shard_map/ppermute | solution.py:55
  60.6 7.7 %collective-permute-start.15 = (bf16[512,128]{1,0:T(8,128)(2,1)S(1)}, bf16[512,128]{1,0:T(8,128)(2,1)S(1)}, u32[]{:S(2)}, u32[]{:S(2)}) collective-permute-start(bf16[512,128]{1,0:T(8,128)(2,1)S(1)} %get-tuple-element.44.w0), channel_id=1, source_target_pairs={{0,96},{32,64},{64,32},{96,0},{1,97},{33,65},{65,33},{97,1},{2,98}... | collective-permute-start | bytes 393224 | tf_op jit(solution)/shard_map/ppermute | solution.py:55
  61.2 7.0 %collective-permute-start.14 = (bf16[512,128]{1,0:T(8,128)(2,1)S(1)}, bf16[512,128]{1,0:T(8,128)(2,1)S(1)}, u32[]{:S(2)}, u32[]{:S(2)}) collective-permute-start(bf16[512,128]{1,0:T(8,128)(2,1)S(1)} %get-tuple-element.44.w0), channel_id=1, source_target_pairs={{0,64},{32,96},{64,0},{96,32},{1,65},{33,97},{65,1},{97,33},{2,66}... | collective-permute-start | bytes 393224 | tf_op jit(solution)/shard_map/ppermute | solution.py:55
  61.7 7.4 %collective-permute-start.13 = (bf16[512,128]{1,0:T(8,128)(2,1)S(1)}, bf16[512,128]{1,0:T(8,128)(2,1)S(1)}, u32[]{:S(2)}, u32[]{:S(2)}) collective-permute-start(bf16[512,128]{1,0:T(8,128)(2,1)S(1)} %get-tuple-element.44.w0), channel_id=1, source_target_pairs={{0,32},{32,0},{64,96},{96,64},{1,33},{33,1},{65,97},{97,65},{2,34}... | collective-permute-start | bytes 393224 | tf_op jit(solution)/shard_map/ppermute | solution.py:55
  78.5 6.4 %collective-permute-start.17 = (bf16[512,128]{1,0:T(8,128)(2,1)S(1)}, bf16[512,128]{1,0:T(8,128)(2,1)S(1)}, u32[]{:S(2)}, u32[]{:S(2)}) collective-permute-start(bf16[512,128]{1,0:T(8,128)(2,1)S(1)} %get-tuple-element.46), channel_id=1, source_target_pairs={{0,1},{1,0},{2,3},{3,2},{4,5},{5,4},{6,7},{7,6},{8,9},{9,8},{10,11... | collective-permute-start | bytes 393224 | tf_op jit(solution)/shard_map/ppermute | solution.py:55
  79.0 10.6 %collective-permute-start.18 = (bf16[512,128]{1,0:T(8,128)(2,1)S(1)}, bf16[512,128]{1,0:T(8,128)(2,1)S(1)}, u32[]{:S(2)}, u32[]{:S(2)}) collective-permute-start(bf16[512,128]{1,0:T(8,128)(2,1)S(1)} %get-tuple-element.47), channel_id=1, source_target_pairs={{0,2},{1,3},{2,0},{3,1},{4,6},{5,7},{6,4},{7,5},{8,10},{9,11},{10,... | collective-permute-start | bytes 393224 | tf_op jit(solution)/shard_map/ppermute | solution.py:55
  83.1 8.7 %collective-permute-start.19 = (bf16[512,128]{1,0:T(8,128)(2,1)S(1)}, bf16[512,128]{1,0:T(8,128)(2,1)S(1)}, u32[]{:S(2)}, u32[]{:S(2)}) collective-permute-start(bf16[512,128]{1,0:T(8,128)(2,1)S(1)} %get-tuple-element.48), channel_id=1, source_target_pairs={{0,3},{1,2},{2,1},{3,0},{4,7},{5,6},{6,5},{7,4},{8,11},{9,10},{10,... | collective-permute-start | bytes 393224 | tf_op jit(solution)/shard_map/ppermute | solution.py:55
  93.3 8.9 %collective-permute-start.22 = (bf16[512,128]{1,0:T(8,128)(2,1)S(1)}, bf16[512,128]{1,0:T(8,128)(2,1)S(1)}, u32[]{:S(2)}, u32[]{:S(2)}) collective-permute-start(bf16[512,128]{1,0:T(8,128)(2,1)S(1)} %get-tuple-element.50.refs_2_), channel_id=1, source_target_pairs={{0,3},{1,2},{2,1},{3,0},{4,7},{5,6},{6,5},{7,4},{8,11},{9,10},{10,... | collective-permute-start | bytes 393224 | tf_op jit(solution)/shard_map/ppermute | solution.py:55
  93.5 8.7 %collective-permute-start.21 = (bf16[512,128]{1,0:T(8,128)(2,1)S(1)}, bf16[512,128]{1,0:T(8,128)(2,1)S(1)}, u32[]{:S(2)}, u32[]{:S(2)}) collective-permute-start(bf16[512,128]{1,0:T(8,128)(2,1)S(1)} %get-tuple-element.50.refs_2_), channel_id=1, source_target_pairs={{0,2},{1,3},{2,0},{3,1},{4,6},{5,7},{6,4},{7,5},{8,10},{9,11},{10,... | collective-permute-start | bytes 393224 | tf_op jit(solution)/shard_map/ppermute | solution.py:55
  94.2 8.5 %collective-permute-start.20 = (bf16[512,128]{1,0:T(8,128)(2,1)S(1)}, bf16[512,128]{1,0:T(8,128)(2,1)S(1)}, u32[]{:S(2)}, u32[]{:S(2)}) collective-permute-start(bf16[512,128]{1,0:T(8,128)(2,1)S(1)} %get-tuple-element.50.refs_2_), channel_id=1, source_target_pairs={{0,1},{1,0},{2,3},{3,2},{4,5},{5,4},{6,7},{7,6},{8,9},{9,8},{10,11... | collective-permute-start | bytes 393224 | tf_op jit(solution)/shard_map/ppermute | solution.py:55
  109.1 6.4 %collective-permute-start.24 = (bf16[512,128]{1,0:T(8,128)(2,1)S(1)}, bf16[512,128]{1,0:T(8,128)(2,1)S(1)}, u32[]{:S(2)}, u32[]{:S(2)}) collective-permute-start(bf16[512,128]{1,0:T(8,128)(2,1)S(1)} %get-tuple-element.54), channel_id=1, source_target_pairs={{0,32},{32,0},{64,96},{96,64},{1,33},{33,1},{65,97},{97,65},{2,34}... | collective-permute-start | bytes 393224 | tf_op jit(solution)/shard_map/ppermute | solution.py:55
  109.8 8.5 %collective-permute-start.25 = (bf16[512,128]{1,0:T(8,128)(2,1)S(1)}, bf16[512,128]{1,0:T(8,128)(2,1)S(1)}, u32[]{:S(2)}, u32[]{:S(2)}) collective-permute-start(bf16[512,128]{1,0:T(8,128)(2,1)S(1)} %get-tuple-element.55), channel_id=1, source_target_pairs={{0,64},{32,96},{64,0},{96,32},{1,65},{33,97},{65,1},{97,33},{2,66}... | collective-permute-start | bytes 393224 | tf_op jit(solution)/shard_map/ppermute | solution.py:55
  111.9 8.7 %collective-permute-start.26 = (bf16[512,128]{1,0:T(8,128)(2,1)S(1)}, bf16[512,128]{1,0:T(8,128)(2,1)S(1)}, u32[]{:S(2)}, u32[]{:S(2)}) collective-permute-start(bf16[512,128]{1,0:T(8,128)(2,1)S(1)} %get-tuple-element.56), channel_id=1, source_target_pairs={{0,96},{32,64},{64,32},{96,0},{1,97},{33,65},{65,33},{97,1},{2,98}... | collective-permute-start | bytes 393224 | tf_op jit(solution)/shard_map/ppermute | solution.py:55
  120.6 38.0 %collective-permute-start.29 = (bf16[512,128]{1,0:T(8,128)(2,1)S(1)}, bf16[512,128]{1,0:T(8,128)(2,1)S(1)}, u32[]{:S(2)}, u32[]{:S(2)}) collective-permute-start(bf16[512,128]{1,0:T(8,128)(2,1)S(1)} %total.3.refs_1_), channel_id=1, source_target_pairs={{0,24},{8,16},{16,8},{24,0},{1,25},{9,17},{17,9},{25,1},{2,26},{10... | collective-permute-start | bytes 393224 | tf_op jit(solution)/shard_map/ppermute | solution.py:55
  123.3 35.3 %collective-permute-start.28 = (bf16[512,128]{1,0:T(8,128)(2,1)S(1)}, bf16[512,128]{1,0:T(8,128)(2,1)S(1)}, u32[]{:S(2)}, u32[]{:S(2)}) collective-permute-start(bf16[512,128]{1,0:T(8,128)(2,1)S(1)} %total.3.refs_1_), channel_id=1, source_target_pairs={{0,16},{8,24},{16,0},{24,8},{1,17},{9,25},{17,1},{25,9},{2,18},{10... | collective-permute-start | bytes 393224 | tf_op jit(solution)/shard_map/ppermute | solution.py:55
  123.3 35.3 %collective-permute-start.27 = (bf16[512,128]{1,0:T(8,128)(2,1)S(1)}, bf16[512,128]{1,0:T(8,128)(2,1)S(1)}, u32[]{:S(2)}, u32[]{:S(2)}) collective-permute-start(bf16[512,128]{1,0:T(8,128)(2,1)S(1)} %total.3.refs_1_), channel_id=1, source_target_pairs={{0,8},{8,0},{16,24},{24,16},{1,9},{9,1},{17,25},{25,17},{2,10},{10... | collective-permute-start | bytes 393224 | tf_op jit(solution)/shard_map/ppermute | solution.py:55
  130.0 5.1 %collective-permute-start.32 = (f32[64,64]{1,0:T(8,128)S(1)}, f32[64,64]{1,0:T(8,128)S(1)}, u32[]{:S(2)}, u32[]{:S(2)}) collective-permute-start(f32[64,64]{1,0:T(8,128)S(1)} %add.43), channel_id=1, source_target_pairs={{0,3},{1,2},{2,1},{3,0},{4,7},{5,6},{6,5},{7,4},{8,11},{9,10},{10,... | collective-permute-start | bytes 49160 | tf_op jit(solution)/shard_map/ppermute | solution.py:55
  159.6 6.3 %collective-permute-start.39 = (bf16[512,128]{1,0:T(8,128)(2,1)S(1)}, bf16[512,128]{1,0:T(8,128)(2,1)S(1)}, u32[]{:S(2)}, u32[]{:S(2)}) collective-permute-start(bf16[512,128]{1,0:T(8,128)(2,1)S(1)} %weigh.3.w0), channel_id=1, source_target_pairs={{0,96},{32,64},{64,32},{96,0},{1,97},{33,65},{65,33},{97,1},{2,98}... | collective-permute-start | bytes 393224 | tf_op jit(solution)/shard_map/ppermute | solution.py:55
  161.6 6.5 %collective-permute-start.38 = (bf16[512,128]{1,0:T(8,128)(2,1)S(1)}, bf16[512,128]{1,0:T(8,128)(2,1)S(1)}, u32[]{:S(2)}, u32[]{:S(2)}) collective-permute-start(bf16[512,128]{1,0:T(8,128)(2,1)S(1)} %weigh.3.w0), channel_id=1, source_target_pairs={{0,64},{32,96},{64,0},{96,32},{1,65},{33,97},{65,1},{97,33},{2,66}... | collective-permute-start | bytes 393224 | tf_op jit(solution)/shard_map/ppermute | solution.py:55
  161.6 6.5 %collective-permute-start.37 = (bf16[512,128]{1,0:T(8,128)(2,1)S(1)}, bf16[512,128]{1,0:T(8,128)(2,1)S(1)}, u32[]{:S(2)}, u32[]{:S(2)}) collective-permute-start(bf16[512,128]{1,0:T(8,128)(2,1)S(1)} %weigh.3.w0), channel_id=1, source_target_pairs={{0,32},{32,0},{64,96},{96,64},{1,33},{33,1},{65,97},{97,65},{2,34}... | collective-permute-start | bytes 393224 | tf_op jit(solution)/shard_map/ppermute | solution.py:55
  177.5 6.4 %collective-permute-start.41 = (bf16[512,128]{1,0:T(8,128)(2,1)S(1)}, bf16[512,128]{1,0:T(8,128)(2,1)S(1)}, u32[]{:S(2)}, u32[]{:S(2)}) collective-permute-start(bf16[512,128]{1,0:T(8,128)(2,1)S(1)} %get-tuple-element.60), channel_id=1, source_target_pairs={{0,1},{1,0},{2,3},{3,2},{4,5},{5,4},{6,7},{7,6},{8,9},{9,8},{10,11... | collective-permute-start | bytes 393224 | tf_op jit(solution)/shard_map/ppermute | solution.py:55
  177.6 9.2 %collective-permute-start.42 = (bf16[512,128]{1,0:T(8,128)(2,1)S(1)}, bf16[512,128]{1,0:T(8,128)(2,1)S(1)}, u32[]{:S(2)}, u32[]{:S(2)}) collective-permute-start(bf16[512,128]{1,0:T(8,128)(2,1)S(1)} %get-tuple-element.61), channel_id=1, source_target_pairs={{0,2},{1,3},{2,0},{3,1},{4,6},{5,7},{6,4},{7,5},{8,10},{9,11},{10,... | collective-permute-start | bytes 393224 | tf_op jit(solution)/shard_map/ppermute | solution.py:55
  180.3 8.7 %collective-permute-start.43 = (bf16[512,128]{1,0:T(8,128)(2,1)S(1)}, bf16[512,128]{1,0:T(8,128)(2,1)S(1)}, u32[]{:S(2)}, u32[]{:S(2)}) collective-permute-start(bf16[512,128]{1,0:T(8,128)(2,1)S(1)} %get-tuple-element.62), channel_id=1, source_target_pairs={{0,3},{1,2},{2,1},{3,0},{4,7},{5,6},{6,5},{7,4},{8,11},{9,10},{10,... | collective-permute-start | bytes 393224 | tf_op jit(solution)/shard_map/ppermute | solution.py:55
  (23 other events, 107.4 us)

commit v2 on v1

v2 whole, which is shorter than its diff:
```python
import functools

import jax
import jax.numpy as jnp
from jax import lax
from jax.experimental import pallas as pl
from jax.experimental.pallas import tpu as pltpu
from jax.sharding import Mesh
from jax.sharding import PartitionSpec as P

ITERS = 2
K = 64
TILE = 128
SLOTS = 256
ROW_TILES = 32
COL_TILES = 64
TOTAL_DOCS = 131072
OWN = 8
CHUNK = OWN * K
COUNT_ROWS = 16
PACKED = 96
TURN = 16
PIVOTS = 8
UNROLL = 32
PREP_STEP = 32
MIB = 1 << 20
PREP_LIMIT = 32 * MIB

X, Z, CORE, BKT = "doc_0", "doc_1", "doc_2", "bkt"
DOC = (X, Z, CORE)
DOC_BKT = (X, Z, CORE, BKT)

f32 = jnp.float32
bf16 = jnp.bfloat16
SMEM = pl.BlockSpec(memory_space=pltpu.SMEM)
VMEM = pl.BlockSpec(memory_space=pltpu.VMEM)
HIGHEST = lax.Precision.HIGHEST


def shape(*lengths, dtype=f32):
    return jax.ShapeDtypeStruct(lengths, dtype)


def call(kernel, name, out_shape, in_specs, scratch=(), limit=8, flops=0, moved=0):
    return pl.pallas_call(
        kernel,
        out_shape=out_shape,
        in_specs=in_specs,
        out_specs=jax.tree.map(lambda _: VMEM, out_shape),
        scratch_shapes=list(scratch),
        compiler_params=pltpu.CompilerParams(vmem_limit_bytes=limit * MIB),
        cost_estimate=pl.CostEstimate(flops=flops, bytes_accessed=moved, transcendentals=0),
        name=name,
    )


def swap(value, axis, mask):
    size = lax.axis_size(axis)
    return lax.ppermute(value, axis, [(i, i ^ mask) for i in range(size)])


def place_of(place):
    return place[0], place[1], place[2], place[3], place[4]


def tile_rows(k):
    return slice(k * K, (k + 1) * K)


def split3(value):
    high = value.astype(bf16)
    rest = value - high.astype(f32)
    middle = rest.astype(bf16)
    return high, middle, (rest - middle.astype(f32)).astype(bf16)


def pack_gram(gram):
    high, middle, low = (term.astype(f32) for term in split3(gram))
    top = jnp.concatenate([high, middle], axis=1)
    bottom = jnp.concatenate([low[: K // 2], low[K // 2 :]], axis=1)
    return jnp.concatenate([top, bottom], axis=0).astype(bf16)


def unpack_gram(packed):
    packed = packed.astype(f32)
    low = jnp.concatenate([packed[K:, :K], packed[K:, K:]], axis=0)
    return (packed[:K, :K] + packed[:K, K:]) + low


def prep_kernel(
    place, coords, weight, pattern_hbm,
    pattern, doc_part, size_part,
    raw, split, doc_acc, size_acc, sems,
):
    steps = SLOTS // PREP_STEP

    def fetch(step):
        at = pl.ds(step * PREP_STEP, PREP_STEP)
        return pltpu.make_async_copy(pattern_hbm.at[at], raw.at[at], sems.at[step])

    for step in range(steps):
        fetch(step).start()
    doc_acc[...] = jnp.zeros_like(doc_acc)
    size_acc[...] = jnp.zeros_like(size_acc)
    rows = lax.broadcasted_iota(jnp.int32, split.shape, 1)
    terms = jnp.zeros(split.shape, f32)
    for i, term in enumerate(split3(weight[...])):
        terms = jnp.where(rows == i, jnp.broadcast_to(term.astype(f32)[:, None, :], split.shape), terms)
    split[...] = terms.astype(bf16)
    count = place[4]

    def block(step, carry):
        fetch(step).wait()
        products, sums = [], []
        for u in range(PREP_STEP):
            slot = step * PREP_STEP + u
            tile = jnp.where(slot < count, raw[slot], 0).astype(f32)
            sums.append(jnp.sum(tile.reshape(TILE // 8, 8, TILE), axis=0))
            tile = tile.astype(bf16)
            pattern[slot] = tile
            products.append(
                lax.dot_general(
                    split[coords[2 * slot + 1]], tile, (((1,), (1,)), ((), ())), preferred_element_type=f32
                )
            )
        for u in range(PREP_STEP):
            slot = step * PREP_STEP + u
            doc_acc[coords[2 * slot]] += products[u]
            size_acc[coords[2 * slot + 1]] += sums[u]
        return carry

    lax.fori_loop(0, steps, block, 0)
    doc_part[...] = jnp.sum(doc_acc[...], axis=1)
    size_part[...] = jnp.sum(size_acc[...], axis=1)


def pack_kernel(vectors, doc_part, payload):
    for k in range(OWN):
        payload[tile_rows(k), :] = vectors[:, k * TILE : (k + 1) * TILE].astype(bf16)
    for i, term in enumerate(split3(doc_part[...])):
        payload[CHUNK + i * ROW_TILES : CHUNK + (i + 1) * ROW_TILES, :] = term


def prep(place, coords, weight, patterns):
    return pl.pallas_call(
        prep_kernel,
        out_shape=(
            shape(SLOTS, TILE, TILE, dtype=bf16),
            shape(ROW_TILES, TILE),
            shape(COL_TILES, TILE),
        ),
        in_specs=[SMEM, SMEM, VMEM, pl.BlockSpec(memory_space=pltpu.HBM)],
        out_specs=(VMEM, VMEM, VMEM),
        scratch_shapes=[
            pltpu.VMEM((SLOTS, TILE, TILE), jnp.int32),
            pltpu.VMEM((COL_TILES, 16, TILE), bf16),
            pltpu.VMEM((ROW_TILES, 16, TILE), f32),
            pltpu.VMEM((COL_TILES, 8, TILE), f32),
            pltpu.SemaphoreType.DMA((SLOTS // PREP_STEP,)),
        ],
        compiler_params=pltpu.CompilerParams(vmem_limit_bytes=PREP_LIMIT),
        cost_estimate=pl.CostEstimate(flops=10**9, bytes_accessed=24 * MIB, transcendentals=0),
        name="prep",
    )(place, coords, weight, patterns)


def turn_kernel(pattern, turned):
    def group(g, carry):
        for u in range(TURN):
            slot = g * TURN + u
            turned[slot] = pattern[slot].T
        return carry

    lax.fori_loop(0, SLOTS // TURN, group, 0)


def tile_products(coords, pattern, source, acc, read, write):
    acc[...] = jnp.zeros_like(acc)

    def group(g, carry):
        products = []
        for u in range(UNROLL):
            slot = g * UNROLL + u
            products.append(
                jnp.dot(source[coords[2 * slot + read]], pattern[slot], preferred_element_type=f32)
            )
        for u in range(UNROLL):
            slot = g * UNROLL + u
            acc[coords[2 * slot + write]] += products[u]
        return carry

    lax.fori_loop(0, SLOTS // UNROLL, group, 0)


def forward_kernel(first, place, coords, b0, b1, b2, b3, pattern, *refs):
    if first:
        sizes, _, keep, send, inv, source, acc = refs
    else:
        keep, send, gram, source, acc = refs
    x, z, c, y, _ = place_of(place)
    blocks = (b0, b1, b2, b3)
    if first:
        terms = [block[CHUNK + i * ROW_TILES : CHUNK + (i + 1) * ROW_TILES, :].astype(f32) for block in blocks for i in range(3)]
        parts = [(terms[3 * s] + terms[3 * s + 1]) + terms[3 * s + 2] for s in range(4)]
        inv[...] = 1.0 / jnp.sqrt(jnp.maximum((parts[0] + parts[1]) + (parts[2] + parts[3]), 1.0))
    for s, block in enumerate(blocks):
        base = (y ^ s) * OWN
        for k in range(OWN):
            tile = block[tile_rows(k), :]
            if first:
                tile = (tile.astype(f32) * inv[pl.ds(base + k, 1), :]).astype(bf16)
            source[base + k] = tile
    tile_products(coords, pattern, source, acc, 0, 1)
    for out, half in ((keep, c), (send, 1 - c)):
        for r in range(4):
            base = half * (COL_TILES // 2) + (x ^ r) * OWN
            for k in range(OWN):
                at = r * CHUNK + k * K
                out[at : at + K, :] = acc[base + k].astype(out.dtype)
            if first:
                counts = jnp.concatenate(
                    [sizes[pl.ds(pl.multiple_of(base, OWN), OWN), :], jnp.zeros((COUNT_ROWS - OWN, TILE), f32)], axis=0
                )
                at = 4 * CHUNK + r * COUNT_ROWS
                out[at : at + COUNT_ROWS, :] = counts.astype(out.dtype)
    if not first:
        parts = [unpack_gram(block[CHUNK : CHUNK + PACKED, :]) for block in blocks]
        gram[...] = (parts[0] + parts[1]) + (parts[2] + parts[3])
        send[4 * CHUNK : 4 * CHUNK + PACKED, :] = pack_gram(gram[...])


def forward(first, place, coords, blocks, pattern, *sizes):
    extra = 4 * COUNT_ROWS
    outs = (
        shape(4 * CHUNK + (extra if first else 0), TILE),
        shape(4 * CHUNK + (extra if first else PACKED), TILE, dtype=bf16),
        shape(ROW_TILES, TILE) if first else shape(K, K),
    )
    return call(
        functools.partial(forward_kernel, first),
        "forward",
        outs,
        [SMEM, SMEM] + [VMEM] * (5 + len(sizes)),
        scratch=[pltpu.VMEM((ROW_TILES, K, TILE), bf16), pltpu.VMEM((COL_TILES, K, TILE), f32)],
        limit=20,
        flops=6 * 10**9,
        moved=12 * MIB,
    )(place, coords, *blocks, pattern, *sizes)


def halves_kernel(first, *refs):
    if first:
        keep, arrived, own, s1, s2, s3 = refs
    else:
        keep, gram, arrived, own, s1, s2, s3, gram_out = refs
        gram_out[...] = gram[...] + unpack_gram(arrived[4 * CHUNK : 4 * CHUNK + PACKED, :])
        packed = pack_gram(gram_out[...])
    for r, out in enumerate((own, s1, s2, s3)):
        at = slice(r * CHUNK, (r + 1) * CHUNK)
        out[:CHUNK, :] = (keep[at, :] + arrived[at, :].astype(f32)).astype(out.dtype)
        if first:
            at = slice(4 * CHUNK + r * COUNT_ROWS, 4 * CHUNK + (r + 1) * COUNT_ROWS)
            out[CHUNK:, :] = (keep[at, :] + arrived[at, :].astype(f32)).astype(out.dtype)
        elif r:
            out[CHUNK:, :] = packed


def halves(first, *args):
    rows = CHUNK + (COUNT_ROWS if first else PACKED)
    outs = [shape(rows if first else CHUNK, TILE)] + [shape(rows, TILE, dtype=bf16)] * 3
    if not first:
        outs.append(shape(K, K))
    return call(functools.partial(halves_kernel, first), "halves", tuple(outs), [VMEM] * len(args), moved=3 * MIB)(*args)


def add4(own, r1, r2, r3, at):
    return (own[at, :].astype(f32) + r1[at, :].astype(f32)) + (r2[at, :].astype(f32) + r3[at, :].astype(f32))


def add_grams(gram, *refs):
    parts = [unpack_gram(ref[CHUNK : CHUNK + PACKED, :]) for ref in refs]
    return (gram[...] + parts[0]) + (parts[1] + parts[2])


def total_kernel(first, *refs):
    if first:
        own, r1, r2, r3, out = refs
        out[...] = add4(own, r1, r2, r3, slice(None)).astype(bf16)
    else:
        own, r1, r2, r3, gram, out, gram_out = refs
        out[:CHUNK, :] = add4(own, r1, r2, r3, slice(0, CHUNK)).astype(bf16)
        gram_out[...] = add_grams(gram, r1, r2, r3)
        out[CHUNK:, :] = pack_gram(gram_out[...])


def total(first, *args):
    rows = CHUNK + (COUNT_ROWS if first else PACKED)
    outs = (shape(rows, TILE, dtype=bf16),) + (() if first else (shape(K, K),))
    return call(functools.partial(total_kernel, first), "total", outs, [VMEM] * len(args))(*args)


def inverse_factor(gram):
    work = jnp.concatenate([gram, jnp.eye(K, dtype=f32)], axis=1)
    below = lax.broadcasted_iota(jnp.int32, (K, 1), 0)
    for k in range(0, K, PIVOTS):
        cols = [jnp.broadcast_to(work[:, k + j : k + j + 1], (K, 2 * K)) for j in range(PIVOTS)]
        rows = [work[k + j : k + j + 1, :] for j in range(PIVOTS)]
        for j in range(PIVOTS):
            inverse = 1.0 / cols[j][k + j : k + j + 1, :]
            row = rows[j] * inverse
            for i in range(j + 1, PIVOTS):
                factor = cols[j][k + i : k + i + 1, :]
                rows[i] = rows[i] - factor * row
                cols[i] = cols[i] - cols[j] * (factor * inverse)
            work = work - jnp.where(below > k + j, cols[j], 0.0) * row
    diagonal = lax.broadcasted_iota(jnp.int32, (K, K), 0) == lax.broadcasted_iota(jnp.int32, (K, K), 1)
    pivots = jnp.sum(jnp.where(diagonal, work[:, :K], 0.0), axis=1, keepdims=True)
    return work[:, K:] / jnp.sqrt(pivots)


def weigh_kernel(first, *refs):
    if first:
        place, p0, p1, p2, p3, weight, weighted, scale = refs
        x, z, c, y, _ = place_of(place)
        base = pl.multiple_of(c * (COL_TILES // 2) + x * OWN, OWN)
        counts = add4(p0, p1, p2, p3, slice(CHUNK, CHUNK + COUNT_ROWS))[:OWN]
        scale[...] = weight[pl.ds(base, OWN), :] / jnp.maximum(counts, 1.0)
    else:
        p0, p1, p2, p3, gram, scale, weighted = refs
        factor = inverse_factor(add_grams(gram, p1, p2, p3))
    for k in range(OWN):
        tile = add4(p0, p1, p2, p3, tile_rows(k))
        if not first:
            tile = jnp.dot(factor, tile, precision=HIGHEST, preferred_element_type=f32)
        weighted[tile_rows(k), :] = (tile * scale[k : k + 1, :]).astype(bf16)


def backward_kernel(place, coords, w0, w1, w2, w3, other, turned, own, s1, s2, s3, source, acc):
    x, z, c, y, _ = place_of(place)
    for r, block in enumerate((w0, w1, w2, w3)):
        base = c * (COL_TILES // 2) + (x ^ r) * OWN
        far = (1 - c) * (COL_TILES // 2) + (x ^ r) * OWN
        for k in range(OWN):
            source[base + k] = block[tile_rows(k), :]
            source[far + k] = other[r, tile_rows(k), :]
    tile_products(coords, turned, source, acc, 1, 0)
    for s, out in enumerate((own, s1, s2, s3)):
        base = (y ^ s) * OWN
        for k in range(OWN):
            out[tile_rows(k), :] = acc[base + k].astype(out.dtype)


def backward(place, coords, blocks, other, turned):
    outs = [shape(CHUNK, TILE)] + [shape(CHUNK, TILE, dtype=bf16)] * 3
    return call(
        backward_kernel,
        "backward",
        tuple(outs),
        [SMEM, SMEM] + [VMEM] * 6,
        scratch=[pltpu.VMEM((COL_TILES, K, TILE), bf16), pltpu.VMEM((ROW_TILES, K, TILE), f32)],
        limit=20,
        flops=6 * 10**9,
        moved=12 * MIB,
    )(place, coords, *blocks, other, turned)


def image_kernel(last, place, own, r1, r2, r3, inv, *refs):
    x, z, c, y, _ = place_of(place)
    inv_own = inv[pl.ds(pl.multiple_of(y * OWN, OWN), OWN), :]
    gram = jnp.zeros((K, K), f32)
    for k in range(OWN):
        at = tile_rows(k)
        tile = add4(own, r1, r2, r3, at) * inv_own[k : k + 1, :]
        if last:
            refs[0][at, :] = tile
        else:
            refs[0][at, :] = (tile * inv_own[k : k + 1, :]).astype(bf16)
        gram += lax.dot_general(
            tile, tile, (((1,), (1,)), ((), ())), precision=HIGHEST, preferred_element_type=f32
        )
    gram = gram / TOTAL_DOCS
    if last:
        image, keep, send, whole = refs
        whole[...] = gram
        for out, half in ((keep, c), (send, 1 - c)):
            rows = whole[pl.ds(pl.multiple_of(half * (K // 2), K // 2), K // 2), :]
            out[...] = jnp.concatenate([rows[: K // 4], rows[K // 4 :]], axis=1)
    else:
        refs[0][CHUNK:, :] = pack_gram(gram)


def sum_kernel(parts, out):
    out[...] = jnp.sum(parts[...], axis=0)


def solve_kernel(place, half, other, image, out, whole):
    c = place[2]
    for ref, at in ((half, c), (other, 1 - c)):
        rows = jnp.concatenate([ref[:, :K], ref[:, K:]], axis=0)
        whole[pl.ds(pl.multiple_of(at * (K // 2), K // 2), K // 2), :] = rows
    factor = inverse_factor(whole[...])
    for k in range(OWN):
        out[:, k * TILE : (k + 1) * TILE] = jnp.dot(
            factor, image[tile_rows(k), :], precision=HIGHEST, preferred_element_type=f32
        )


def spread(value, axis):
    return [value] + [swap(value, axis, s) for s in (1, 2, 3)]


def swapped(values, axis):
    return [swap(value, axis, s + 1) for s, value in enumerate(values)]


def body(start_vectors, bucket_weight, tile_count, tile_coords, patterns):
    place = jnp.stack([lax.axis_index(a) for a in DOC_BKT] + [tile_count[0, 0]]).astype(jnp.int32)
    coords = tile_coords.reshape(2 * SLOTS)
    weight = bucket_weight.reshape(COL_TILES, TILE)
    chunk_b = shape(CHUNK, TILE, dtype=bf16)

    pattern, doc_part, sizes = prep(place, coords, weight, patterns.reshape(SLOTS, TILE, TILE))
    payload = call(pack_kernel, "pack", shape(CHUNK + PACKED, TILE, dtype=bf16), [VMEM] * 2)(start_vectors, doc_part)
    turned = call(turn_kernel, "turn", shape(SLOTS, TILE, TILE, dtype=bf16), [VMEM], limit=4, moved=16 * MIB)(pattern)
    inv = scale = None
    for sweep in range(ITERS):
        first, last = sweep == 0, sweep == ITERS - 1
        blocks = spread(payload, BKT)
        if first:
            keep, send, inv = forward(True, place, coords, blocks, pattern, sizes, turned)
            own, *parts = halves(True, keep, swap(send, CORE, 1))
            (part,) = total(True, own, *swapped(parts, X))
            weighted, scale = call(
                functools.partial(weigh_kernel, True), "weigh", (chunk_b, shape(OWN, TILE)), [SMEM] + [VMEM] * 5
            )(place, *spread(part, Z), weight)
        else:
            keep, send, gram = forward(False, place, coords, blocks, pattern)
            own, *parts, gram = halves(False, keep, gram, swap(send, CORE, 1))
            part, gram = total(False, own, *swapped(parts, X), gram)
            weighted = call(functools.partial(weigh_kernel, False), "weigh", chunk_b, [VMEM] * 6)(
                *spread(part, Z), gram, scale
            )
        mine = spread(weighted, X)
        other = swap(jnp.stack(mine), CORE, 1)
        own, *parts = backward(place, coords, mine, other, turned)
        if not last:
            outs = shape(CHUNK + PACKED, TILE, dtype=bf16)
            scratch = ()
        else:
            outs = (shape(CHUNK, TILE), shape(K // 4, TILE), shape(K // 4, TILE))
            scratch = (pltpu.VMEM((K, K), f32),)
        outs = call(functools.partial(image_kernel, last), "image", outs, [SMEM] + [VMEM] * 5, scratch=scratch)(
            place, own, *swapped(parts, BKT), inv
        )
        if not last:
            payload = outs
    image, keep, send = outs
    half = keep + swap(send, CORE, 1)
    others = (X, Z, BKT)
    copies = jnp.broadcast_to(half, (lax.axis_size(others), *half.shape))
    parts = lax.all_to_all(copies, others, split_axis=0, concat_axis=0, tiled=True)
    half = call(sum_kernel, "sum", shape(K // 4, TILE), [VMEM])(parts)
    return call(
        solve_kernel,
        "solve",
        shape(K, OWN * TILE),
        [SMEM] + [VMEM] * 3,
        scratch=[pltpu.VMEM((K, K), f32)],
    )(place, half, swap(half, CORE, 1), image)


def solution(mesh):
    split = Mesh(mesh.devices.reshape(4, 4, 2, mesh.shape[BKT]), DOC_BKT)
    in_specs = (
        P(None, DOC_BKT),
        P(BKT),
        P(DOC, BKT),
        P(DOC, BKT, None, None),
        P(DOC, BKT, None, None, None),
    )
    return jax.shard_map(body, mesh=split, in_specs=in_specs, out_specs=P(None, DOC_BKT), check_vma=False)
```

time: 225 us -> 181 us (0.80)
  waiting for transfers between devices: 106 us -> 73.7 us
  blocking collectives: 0 us -> 21 us
  starting transfers between devices: 63.2 us -> 45.4 us
  Pallas kernels: 46 us -> 36.8 us
  local copies, waits for them, and re-layouts: 8.53 us -> 1.84 us
    ppermute x51 -> x36, waiting for transfers between devices: 106 us -> 73.7 us  [swap(): return lax.ppermute(value, axis, [(i, i ^ mask) for i in range(size)])]
    all_to_all x0 -> x1, blocking collectives: none -> 21 us  [body(): lax.all_to_all(copies, others, split_axis=0, concat_axis=0, tiled=True)]
    ppermute x51 -> x36, starting transfers between devices: 63.2 us -> 45.4 us  [swap(): return lax.ppermute(value, axis, [(i, i ^ mask) for i in range(size)])]
    unnamed x9 -> x7, local copies, waits for them, and re-layouts: 8.29 us -> 1.57 us
    pallas_call x2, Pallas kernels: 14.7 us -> 8.29 us  [backward(): call(backward_kernel, 'backward', tuple(outs), [SMEM, SMEM] + [VMEM] * 6,...]
    pallas_call x12, Pallas kernels: 28.1 us -> 25.6 us  [the longest x2 8.63 us: forward(): call(functools.partial(forward_kernel, first), 'forward', outs, [SMEM, SM...]
  transfers between devices with their start and end apart: 51 -> 36, of which waited for: 41 -> 30; matrix products, arithmetic and copies ran while one was open for 0% -> 0% of each run, Pallas kernels for 5% -> 2%
where the time goes in v2:
time: 181 us; the launch traced here: 180 us
  waiting for transfers between devices  73.7 us (41%)
  starting transfers between devices  45.4 us (25%)
  Pallas kernels  36.8 us (20%)
  blocking collectives  21 us (12%)
  local copies, waits for them, and re-layouts  1.84 us (1%)
    ppermute x36, waiting for transfers between devices, swap(): return lax.ppermute(value, axis, [(i, i ^ mask) for i in range(size)])  73.7 us
    ppermute x36, starting transfers between devices, swap(): return lax.ppermute(value, axis, [(i, i ^ mask) for i in range(size)])  45.4 us
    all_to_all x1, blocking collectives, body(): lax.all_to_all(copies, others, split_axis=0, concat_axis=0, tiled=True)  21 us
    pallas_call x2, Pallas kernels, forward(): call(functools.partial(forward_kernel, first), 'forward', outs, [SMEM, SM...  8.63 us
    pallas_call x2, Pallas kernels, backward(): call(backward_kernel, 'backward', tuple(outs), [SMEM, SMEM] + [VMEM] * 6,...  8.29 us
    pallas_call x1, Pallas kernels, prep(): pl.pallas_call(prep_kernel, out_shape=(shape(SLOTS, TILE, TILE, dtype=bf1...  7.72 us
  transfers between devices with their start and end apart: 36, of which 30 were waited for; matrix products, arithmetic and copies ran while one was open for 0% of the time, Pallas kernels for 2%

profile of v2, /device:TPU:0, one launch (start us, length us, event | category | flops | bytes accessed | tf_op | source)
XLA Modules:
  0.0 179.9 jit_solution(14255513889445431605)
XLA Ops:
  2.5 7.7 %prep.1 = (bf16[256,128,128]{2,1,0:T(8,128)(2,1)S(1)}, f32[32,128]{1,0:T(8,128)S(1)}, f32[64,128]{1,0:T(8,128)S(1)}) custom-call(s32[5]{0:T(128)S(1)} %stack.49.place.refs_0_, s32[512]{0:T(512)S(1)} %reshape.9.coords, f32[64,128]{1,0:T(8,128)S(1)} %bitcast.19, s32[256,128,128]{2,1,0:T(8,128)} %bitcast.28), custom_call_target="tpu_custom_call" | custom-call | flops 1000000000 | bytes 25165824 | tf_op jit(solution)/shard_map/prep/pallas_call | solution.py:145
  10.2 3.2 %collective-permute-start.2 = (bf16[608,128]{1,0:T(8,128)(2,1)S(1)}, bf16[608,128]{1,0:T(8,128)(2,1)S(1)}, u32[]{:S(2)}, u32[]{:S(2)}) collective-permute-start(bf16[608,128]{1,0:T(8,128)(2,1)S(1)} %pack.1.b0), channel_id=1, source_target_pairs={{0,3},{1,2},{2,1},{3,0},{4,7},{5,6},{6,5},{7,4},{8,11},{9,10},{10,... | collective-permute-start | bytes 466952 | tf_op jit(solution)/shard_map/ppermute | solution.py:59
  14.4 3.0 %turn.1.refs_1_.turned = bf16[256,128,128]{2,1,0:T(8,128)(2,1)S(1)} custom-call(bf16[256,128,128]{2,1,0:T(8,128)(2,1)S(1)} %get-tuple-element.39.pattern), custom_call_target="tpu_custom_call" | custom-call | bytes 16777216 | tf_op jit(solution)/shard_map/turn/pallas_call | solution.py:424
  17.4 2.6 %collective-permute-done.2.b3 = bf16[608,128]{1,0:T(8,128)(2,1)S(1)} collective-permute-done((bf16[608,128]{1,0:T(8,128)(2,1)S(1)}, bf16[608,128]{1,0:T(8,128)(2,1)S(1)}, u32[]{:S(2)}, u32[]{:S(2)}) %collective-permute-start.2) | collective-permute-done | bytes 155680 | tf_op jit(solution)/shard_map/ppermute | solution.py:59
  21.9 4.3 %forward.2 = (f32[2112,128]{1,0:T(8,128)S(1)}, bf16[2112,128]{1,0:T(8,128)(2,1)S(1)}, f32[32,128]{1,0:T(8,128)S(1)}) custom-call(s32[5]{0:T(128)S(1)} %stack.49.place.refs_0_, s32[512]{0:T(512)S(1)} %reshape.9.coords, bf16[608,128]{1,0:T(8,128)(2,1)S(1)} %pack.1.b0, bf16[608,128]{1,0:T(8,128)(2,1)S(1)} %collective-permute-done.b1, ...), custom_call_target="tpu_custom_call" | custom-call | flops 6000000000 | bytes 12582912 | tf_op jit(solution)/shard_map/forward/pallas_call | solution.py:239
  29.9 2.7 %collective-permute-start.5 = (bf16[528,128]{1,0:T(8,128)(2,1)S(1)}, bf16[528,128]{1,0:T(8,128)(2,1)S(1)}, u32[]{:S(2)}, u32[]{:S(2)}) collective-permute-start(bf16[528,128]{1,0:T(8,128)(2,1)S(1)} %get-tuple-element.45), channel_id=1, source_target_pairs={{0,64},{32,96},{64,0},{96,32},{1,65},{33,97},{65,1},{97,33},{2,66}... | collective-permute-start | bytes 405512 | tf_op jit(solution)/shard_map/ppermute | solution.py:59
  34.7 4.5 %collective-permute-done.5.refs_2_ = bf16[528,128]{1,0:T(8,128)(2,1)S(1)} collective-permute-done((bf16[528,128]{1,0:T(8,128)(2,1)S(1)}, bf16[528,128]{1,0:T(8,128)(2,1)S(1)}, u32[]{:S(2)}, u32[]{:S(2)}) %collective-permute-start.5) | collective-permute-done | bytes 135200 | tf_op jit(solution)/shard_map/ppermute | solution.py:59
  39.2 2.3 %collective-permute-done.6.refs_3_ = bf16[528,128]{1,0:T(8,128)(2,1)S(1)} collective-permute-done((bf16[528,128]{1,0:T(8,128)(2,1)S(1)}, bf16[528,128]{1,0:T(8,128)(2,1)S(1)}, u32[]{:S(2)}, u32[]{:S(2)}) %collective-permute-start.6) | collective-permute-done | bytes 135200 | tf_op jit(solution)/shard_map/ppermute | solution.py:59
  41.6 4.1 %collective-permute-start.9 = (bf16[528,128]{1,0:T(8,128)(2,1)S(1)}, bf16[528,128]{1,0:T(8,128)(2,1)S(1)}, u32[]{:S(2)}, u32[]{:S(2)}) collective-permute-start(bf16[528,128]{1,0:T(8,128)(2,1)S(1)} %total.2.refs_1_), channel_id=1, source_target_pairs={{0,24},{8,16},{16,8},{24,0},{1,25},{9,17},{17,9},{25,1},{2,26},{10... | collective-permute-start | bytes 405512 | tf_op jit(solution)/shard_map/ppermute | solution.py:59
  46.6 4.4 %collective-permute-done.9.refs_4_ = bf16[528,128]{1,0:T(8,128)(2,1)S(1)} collective-permute-done((bf16[528,128]{1,0:T(8,128)(2,1)S(1)}, bf16[528,128]{1,0:T(8,128)(2,1)S(1)}, u32[]{:S(2)}, u32[]{:S(2)}) %collective-permute-start.9) | collective-permute-done | bytes 135200 | tf_op jit(solution)/shard_map/ppermute | solution.py:59
  51.1 2.2 %collective-permute-done.8.refs_3_ = bf16[528,128]{1,0:T(8,128)(2,1)S(1)} collective-permute-done((bf16[528,128]{1,0:T(8,128)(2,1)S(1)}, bf16[528,128]{1,0:T(8,128)(2,1)S(1)}, u32[]{:S(2)}, u32[]{:S(2)}) %collective-permute-start.8) | collective-permute-done | bytes 135200 | tf_op jit(solution)/shard_map/ppermute | solution.py:59
  55.0 3.1 %collective-permute-start.10 = (bf16[512,128]{1,0:T(8,128)(2,1)S(1)}, bf16[512,128]{1,0:T(8,128)(2,1)S(1)}, u32[]{:S(2)}, u32[]{:S(2)}) collective-permute-start(bf16[512,128]{1,0:T(8,128)(2,1)S(1)} %get-tuple-element.47.w0), channel_id=1, source_target_pairs={{0,32},{32,0},{64,96},{96,64},{1,33},{33,1},{65,97},{97,65},{2,34}... | collective-permute-start | bytes 393224 | tf_op jit(solution)/shard_map/ppermute | solution.py:59
  58.1 3.5 %collective-permute-done.12.w3 = bf16[512,128]{1,0:T(8,128)(2,1)S(1)} collective-permute-done((bf16[512,128]{1,0:T(8,128)(2,1)S(1)}, bf16[512,128]{1,0:T(8,128)(2,1)S(1)}, u32[]{:S(2)}, u32[]{:S(2)}) %collective-permute-start.12) | collective-permute-done | bytes 131104 | tf_op jit(solution)/shard_map/ppermute | solution.py:59
  64.5 4.1 %backward.2 = (f32[512,128]{1,0:T(8,128)S(1)}, bf16[512,128]{1,0:T(8,128)(2,1)S(1)}, bf16[512,128]{1,0:T(8,128)(2,1)S(1)}, bf16[512,128]{1,0:T(8,128)(2,1)S(1)}) custom-call(s32[5]{0:T(128)S(1)} %stack.49.place.refs_0_, s32[512]{0:T(512)S(1)} %reshape.9.coords, bf16[512,128]{1,0:T(8,128)(2,1)S(1)} %get-tuple-element.47.w0, ...), custom_call_target="tpu_custom_call" | custom-call | flops 6000000000 | bytes 12582912 | tf_op jit(solution)/shard_map/backward/pallas_call | solution.py:355
  69.8 2.9 %collective-permute-start.15 = (bf16[512,128]{1,0:T(8,128)(2,1)S(1)}, bf16[512,128]{1,0:T(8,128)(2,1)S(1)}, u32[]{:S(2)}, u32[]{:S(2)}) collective-permute-start(bf16[512,128]{1,0:T(8,128)(2,1)S(1)} %get-tuple-element.50), channel_id=1, source_target_pairs={{0,2},{1,3},{2,0},{3,1},{4,6},{5,7},{6,4},{7,5},{8,10},{9,11},{10,... | collective-permute-start | bytes 393224 | tf_op jit(solution)/shard_map/ppermute | solution.py:59
  75.1 4.0 %collective-permute-done.15.r2 = bf16[512,128]{1,0:T(8,128)(2,1)S(1)} collective-permute-done((bf16[512,128]{1,0:T(8,128)(2,1)S(1)}, bf16[512,128]{1,0:T(8,128)(2,1)S(1)}, u32[]{:S(2)}, u32[]{:S(2)}) %collective-permute-start.15) | collective-permute-done | bytes 131104 | tf_op jit(solution)/shard_map/ppermute | solution.py:59
  79.1 2.2 %collective-permute-done.16.r3 = bf16[512,128]{1,0:T(8,128)(2,1)S(1)} collective-permute-done((bf16[512,128]{1,0:T(8,128)(2,1)S(1)}, bf16[512,128]{1,0:T(8,128)(2,1)S(1)}, u32[]{:S(2)}, u32[]{:S(2)}) %collective-permute-start.16) | collective-permute-done | bytes 131104 | tf_op jit(solution)/shard_map/ppermute | solution.py:59
  83.9 2.7 %collective-permute-start.17 = (bf16[608,128]{1,0:T(8,128)(2,1)S(1)}, bf16[608,128]{1,0:T(8,128)(2,1)S(1)}, u32[]{:S(2)}, u32[]{:S(2)}) collective-permute-start(bf16[608,128]{1,0:T(8,128)(2,1)S(1)} %image.2.b0), channel_id=1, source_target_pairs={{0,1},{1,0},{2,3},{3,2},{4,5},{5,4},{6,7},{7,6},{8,9},{9,8},{10,11... | collective-permute-start | bytes 466952 | tf_op jit(solution)/shard_map/ppermute | solution.py:59
  86.7 5.9 %collective-permute-done.19.b3 = bf16[608,128]{1,0:T(8,128)(2,1)S(1)} collective-permute-done((bf16[608,128]{1,0:T(8,128)(2,1)S(1)}, bf16[608,128]{1,0:T(8,128)(2,1)S(1)}, u32[]{:S(2)}, u32[]{:S(2)}) %collective-permute-start.19) | collective-permute-done | bytes 155680 | tf_op jit(solution)/shard_map/ppermute | solution.py:59
  93.2 4.3 %forward.3 = (f32[2048,128]{1,0:T(8,128)S(1)}, bf16[2144,128]{1,0:T(8,128)(2,1)S(1)}, f32[64,64]{1,0:T(8,128)S(1)}) custom-call(s32[5]{0:T(128)S(1)} %stack.49.place.refs_0_, s32[512]{0:T(512)S(1)} %reshape.9.coords, bf16[608,128]{1,0:T(8,128)(2,1)S(1)} %image.2.b0, bf16[608,128]{1,0:T(8,128)(2,1)S(1)} %collective-permute-done.17.b1, ...), custom_call_target="tpu_custom_call" | custom-call | flops 6000000000 | bytes 12582912 | tf_op jit(solution)/shard_map/forward/pallas_call | solution.py:239
  106.7 3.3 %collective-permute-done.22.refs_2_ = bf16[608,128]{1,0:T(8,128)(2,1)S(1)} collective-permute-done((bf16[608,128]{1,0:T(8,128)(2,1)S(1)}, bf16[608,128]{1,0:T(8,128)(2,1)S(1)}, u32[]{:S(2)}, u32[]{:S(2)}) %collective-permute-start.22) | collective-permute-done | bytes 155680 | tf_op jit(solution)/shard_map/ppermute | solution.py:59
  110.0 2.5 %collective-permute-done.23.refs_3_ = bf16[608,128]{1,0:T(8,128)(2,1)S(1)} collective-permute-done((bf16[608,128]{1,0:T(8,128)(2,1)S(1)}, bf16[608,128]{1,0:T(8,128)(2,1)S(1)}, u32[]{:S(2)}, u32[]{:S(2)}) %collective-permute-start.23) | collective-permute-done | bytes 155680 | tf_op jit(solution)/shard_map/ppermute | solution.py:59
  112.8 2.7 %collective-permute-start.26 = (bf16[608,128]{1,0:T(8,128)(2,1)S(1)}, bf16[608,128]{1,0:T(8,128)(2,1)S(1)}, u32[]{:S(2)}, u32[]{:S(2)}) collective-permute-start(bf16[608,128]{1,0:T(8,128)(2,1)S(1)} %get-tuple-element.61.refs_0_), channel_id=1, source_target_pairs={{0,24},{8,16},{16,8},{24,0},{1,25},{9,17},{17,9},{25,1},{2,26},{10... | collective-permute-start | bytes 466952 | tf_op jit(solution)/shard_map/ppermute | solution.py:59
  117.0 4.7 %collective-permute-done.26.refs_3_ = bf16[608,128]{1,0:T(8,128)(2,1)S(1)} collective-permute-done((bf16[608,128]{1,0:T(8,128)(2,1)S(1)}, bf16[608,128]{1,0:T(8,128)(2,1)S(1)}, u32[]{:S(2)}, u32[]{:S(2)}) %collective-permute-start.26) | collective-permute-done | bytes 155680 | tf_op jit(solution)/shard_map/ppermute | solution.py:59
  130.0 2.3 %collective-permute-done.29.w3 = bf16[512,128]{1,0:T(8,128)(2,1)S(1)} collective-permute-done((bf16[512,128]{1,0:T(8,128)(2,1)S(1)}, bf16[512,128]{1,0:T(8,128)(2,1)S(1)}, u32[]{:S(2)}, u32[]{:S(2)}) %collective-permute-start.29) | collective-permute-done | bytes 131104 | tf_op jit(solution)/shard_map/ppermute | solution.py:59
  136.4 4.1 %backward.3 = (f32[512,128]{1,0:T(8,128)S(1)}, bf16[512,128]{1,0:T(8,128)(2,1)S(1)}, bf16[512,128]{1,0:T(8,128)(2,1)S(1)}, bf16[512,128]{1,0:T(8,128)(2,1)S(1)}) custom-call(s32[5]{0:T(128)S(1)} %stack.49.place.refs_0_, s32[512]{0:T(512)S(1)} %reshape.9.coords, bf16[512,128]{1,0:T(8,128)(2,1)S(1)} %weigh.3.w0, ...), custom_call_target="tpu_custom_call" | custom-call | flops 6000000000 | bytes 12582912 | tf_op jit(solution)/shard_map/backward/pallas_call | solution.py:355
  140.7 2.5 %collective-permute-start.32 = (bf16[512,128]{1,0:T(8,128)(2,1)S(1)}, bf16[512,128]{1,0:T(8,128)(2,1)S(1)}, u32[]{:S(2)}, u32[]{:S(2)}) collective-permute-start(bf16[512,128]{1,0:T(8,128)(2,1)S(1)} %get-tuple-element.66), channel_id=1, source_target_pairs={{0,2},{1,3},{2,0},{3,1},{4,6},{5,7},{6,4},{7,5},{8,10},{9,11},{10,... | collective-permute-start | bytes 393224 | tf_op jit(solution)/shard_map/ppermute | solution.py:59
  143.1 2.2 %collective-permute-start.33 = (bf16[512,128]{1,0:T(8,128)(2,1)S(1)}, bf16[512,128]{1,0:T(8,128)(2,1)S(1)}, u32[]{:S(2)}, u32[]{:S(2)}) collective-permute-start(bf16[512,128]{1,0:T(8,128)(2,1)S(1)} %get-tuple-element.67), channel_id=1, source_target_pairs={{0,3},{1,2},{2,1},{3,0},{4,7},{5,6},{6,5},{7,4},{8,11},{9,10},{10,... | collective-permute-start | bytes 393224 | tf_op jit(solution)/shard_map/ppermute | solution.py:59
  147.0 2.6 %collective-permute-done.32.r2 = bf16[512,128]{1,0:T(8,128)(2,1)S(1)} collective-permute-done((bf16[512,128]{1,0:T(8,128)(2,1)S(1)}, bf16[512,128]{1,0:T(8,128)(2,1)S(1)}, u32[]{:S(2)}, u32[]{:S(2)}) %collective-permute-start.32) | collective-permute-done | bytes 131104 | tf_op jit(solution)/shard_map/ppermute | solution.py:59
  149.5 2.2 %collective-permute-done.33.r3 = bf16[512,128]{1,0:T(8,128)(2,1)S(1)} collective-permute-done((bf16[512,128]{1,0:T(8,128)(2,1)S(1)}, bf16[512,128]{1,0:T(8,128)(2,1)S(1)}, u32[]{:S(2)}, u32[]{:S(2)}) %collective-permute-start.33) | collective-permute-done | bytes 131104 | tf_op jit(solution)/shard_map/ppermute | solution.py:59
  154.2 21.0 %all_to_all.5.parts = f32[64,16,128]{2,1,0:T(8,128)S(1)} all-to-all(f32[64,16,128]{2,1,0:T(8,128)S(1)} %broadcast_in_dim.3), channel_id=1, replica_groups=mesh['doc_0'=4,'doc_1'=4,'doc_2'=2,'bkt'=4] {'doc_0','doc_1','bkt'}, dimensions={0} | all-to-all | bytes 1048576 | tf_op jit(solution)/shard_map/all_to_all | solution.py:461
  176.5 3.4 %solve.1 = f32[64,1024]{1,0:T(8,128)} custom-call(s32[5]{0:T(128)S(1)} %stack.49.place.refs_0_, f32[16,128]{1,0:T(8,128)S(1)} %sum.1.half, f32[16,128]{1,0:T(8,128)S(1)} %collective-permute-done.35.other, f32[512,128]{1,0:T(8,128)S(1)} %get-tuple-element.70.image), custom_call_target="tpu_custom_call" | custom-call | tf_op jit(solution)/shard_map/solve/pallas_call | solution.py:463
  (71 shorter events, 51.6 us)
Async XLA Ops:
  10.2 9.8 %collective-permute-start.2 = (bf16[608,128]{1,0:T(8,128)(2,1)S(1)}, bf16[608,128]{1,0:T(8,128)(2,1)S(1)}, u32[]{:S(2)}, u32[]{:S(2)}) collective-permute-start(bf16[608,128]{1,0:T(8,128)(2,1)S(1)} %pack.1.b0), channel_id=1, source_target_pairs={{0,3},{1,2},{2,1},{3,0},{4,7},{5,6},{6,5},{7,4},{8,11},{9,10},{10,... | collective-permute-start | bytes 466952 | tf_op jit(solution)/shard_map/ppermute | solution.py:59
  13.4 8.5 %collective-permute-start.1 = (bf16[608,128]{1,0:T(8,128)(2,1)S(1)}, bf16[608,128]{1,0:T(8,128)(2,1)S(1)}, u32[]{:S(2)}, u32[]{:S(2)}) collective-permute-start(bf16[608,128]{1,0:T(8,128)(2,1)S(1)} %pack.1.b0), channel_id=1, source_target_pairs={{0,2},{1,3},{2,0},{3,1},{4,6},{5,7},{6,4},{7,5},{8,10},{9,11},{10,... | collective-permute-start | bytes 466952 | tf_op jit(solution)/shard_map/ppermute | solution.py:59
  14.0 7.8 %collective-permute-start = (bf16[608,128]{1,0:T(8,128)(2,1)S(1)}, bf16[608,128]{1,0:T(8,128)(2,1)S(1)}, u32[]{:S(2)}, u32[]{:S(2)}) collective-permute-start(bf16[608,128]{1,0:T(8,128)(2,1)S(1)} %pack.1.b0), channel_id=1, source_target_pairs={{0,1},{1,0},{2,3},{3,2},{4,5},{5,4},{6,7},{7,6},{8,9},{9,8},{10,11... | collective-permute-start | bytes 466952 | tf_op jit(solution)/shard_map/ppermute | solution.py:59
  26.2 2.0 %collective-permute-start.3 = (bf16[2112,128]{1,0:T(8,128)(2,1)S(1)}, bf16[2112,128]{1,0:T(8,128)(2,1)S(1)}, u32[]{:S(2)}, u32[]{:S(2)}) collective-permute-start(bf16[2112,128]{1,0:T(8,128)(2,1)S(1)} %get-tuple-element.42), channel_id=1, source_target_pairs={{0,4},{4,0},{1,5},{5,1},{2,6},{6,2},{3,7},{7,3},{8,12},{12,8},{9,1... | collective-permute-start | bytes 1622024 | tf_op jit(solution)/shard_map/ppermute | solution.py:59
  28.3 6.4 %collective-permute-start.4 = (bf16[528,128]{1,0:T(8,128)(2,1)S(1)}, bf16[528,128]{1,0:T(8,128)(2,1)S(1)}, u32[]{:S(2)}, u32[]{:S(2)}) collective-permute-start(bf16[528,128]{1,0:T(8,128)(2,1)S(1)} %get-tuple-element.44), channel_id=1, source_target_pairs={{0,32},{32,0},{64,96},{96,64},{1,33},{33,1},{65,97},{97,65},{2,34}... | collective-permute-start | bytes 405512 | tf_op jit(solution)/shard_map/ppermute | solution.py:59
  29.9 9.3 %collective-permute-start.5 = (bf16[528,128]{1,0:T(8,128)(2,1)S(1)}, bf16[528,128]{1,0:T(8,128)(2,1)S(1)}, u32[]{:S(2)}, u32[]{:S(2)}) collective-permute-start(bf16[528,128]{1,0:T(8,128)(2,1)S(1)} %get-tuple-element.45), channel_id=1, source_target_pairs={{0,64},{32,96},{64,0},{96,32},{1,65},{33,97},{65,1},{97,33},{2,66}... | collective-permute-start | bytes 405512 | tf_op jit(solution)/shard_map/ppermute | solution.py:59
  32.6 8.9 %collective-permute-start.6 = (bf16[528,128]{1,0:T(8,128)(2,1)S(1)}, bf16[528,128]{1,0:T(8,128)(2,1)S(1)}, u32[]{:S(2)}, u32[]{:S(2)}) collective-permute-start(bf16[528,128]{1,0:T(8,128)(2,1)S(1)} %get-tuple-element.46), channel_id=1, source_target_pairs={{0,96},{32,64},{64,32},{96,0},{1,97},{33,65},{65,33},{97,1},{2,98}... | collective-permute-start | bytes 405512 | tf_op jit(solution)/shard_map/ppermute | solution.py:59
  41.6 9.5 %collective-permute-start.9 = (bf16[528,128]{1,0:T(8,128)(2,1)S(1)}, bf16[528,128]{1,0:T(8,128)(2,1)S(1)}, u32[]{:S(2)}, u32[]{:S(2)}) collective-permute-start(bf16[528,128]{1,0:T(8,128)(2,1)S(1)} %total.2.refs_1_), channel_id=1, source_target_pairs={{0,24},{8,16},{16,8},{24,0},{1,25},{9,17},{17,9},{25,1},{2,26},{10... | collective-permute-start | bytes 405512 | tf_op jit(solution)/shard_map/ppermute | solution.py:59
  45.7 7.6 %collective-permute-start.8 = (bf16[528,128]{1,0:T(8,128)(2,1)S(1)}, bf16[528,128]{1,0:T(8,128)(2,1)S(1)}, u32[]{:S(2)}, u32[]{:S(2)}) collective-permute-start(bf16[528,128]{1,0:T(8,128)(2,1)S(1)} %total.2.refs_1_), channel_id=1, source_target_pairs={{0,16},{8,24},{16,0},{24,8},{1,17},{9,25},{17,1},{25,9},{2,18},{10... | collective-permute-start | bytes 405512 | tf_op jit(solution)/shard_map/ppermute | solution.py:59
  45.7 7.6 %collective-permute-start.7 = (bf16[528,128]{1,0:T(8,128)(2,1)S(1)}, bf16[528,128]{1,0:T(8,128)(2,1)S(1)}, u32[]{:S(2)}, u32[]{:S(2)}) collective-permute-start(bf16[528,128]{1,0:T(8,128)(2,1)S(1)} %total.2.refs_1_), channel_id=1, source_target_pairs={{0,8},{8,0},{16,24},{24,16},{1,9},{9,1},{17,25},{25,17},{2,10},{10... | collective-permute-start | bytes 405512 | tf_op jit(solution)/shard_map/ppermute | solution.py:59
  53.9 7.7 %collective-permute-start.12 = (bf16[512,128]{1,0:T(8,128)(2,1)S(1)}, bf16[512,128]{1,0:T(8,128)(2,1)S(1)}, u32[]{:S(2)}, u32[]{:S(2)}) collective-permute-start(bf16[512,128]{1,0:T(8,128)(2,1)S(1)} %get-tuple-element.47.w0), channel_id=1, source_target_pairs={{0,96},{32,64},{64,32},{96,0},{1,97},{33,65},{65,33},{97,1},{2,98}... | collective-permute-start | bytes 393224 | tf_op jit(solution)/shard_map/ppermute | solution.py:59
  54.6 7.0 %collective-permute-start.11 = (bf16[512,128]{1,0:T(8,128)(2,1)S(1)}, bf16[512,128]{1,0:T(8,128)(2,1)S(1)}, u32[]{:S(2)}, u32[]{:S(2)}) collective-permute-start(bf16[512,128]{1,0:T(8,128)(2,1)S(1)} %get-tuple-element.47.w0), channel_id=1, source_target_pairs={{0,64},{32,96},{64,0},{96,32},{1,65},{33,97},{65,1},{97,33},{2,66}... | collective-permute-start | bytes 393224 | tf_op jit(solution)/shard_map/ppermute | solution.py:59
  55.0 7.4 %collective-permute-start.10 = (bf16[512,128]{1,0:T(8,128)(2,1)S(1)}, bf16[512,128]{1,0:T(8,128)(2,1)S(1)}, u32[]{:S(2)}, u32[]{:S(2)}) collective-permute-start(bf16[512,128]{1,0:T(8,128)(2,1)S(1)} %get-tuple-element.47.w0), channel_id=1, source_target_pairs={{0,32},{32,0},{64,96},{96,64},{1,33},{33,1},{65,97},{97,65},{2,34}... | collective-permute-start | bytes 393224 | tf_op jit(solution)/shard_map/ppermute | solution.py:59
  68.7 6.4 %collective-permute-start.14 = (bf16[512,128]{1,0:T(8,128)(2,1)S(1)}, bf16[512,128]{1,0:T(8,128)(2,1)S(1)}, u32[]{:S(2)}, u32[]{:S(2)}) collective-permute-start(bf16[512,128]{1,0:T(8,128)(2,1)S(1)} %get-tuple-element.49), channel_id=1, source_target_pairs={{0,1},{1,0},{2,3},{3,2},{4,5},{5,4},{6,7},{7,6},{8,9},{9,8},{10,11... | collective-permute-start | bytes 393224 | tf_op jit(solution)/shard_map/ppermute | solution.py:59
  69.8 9.3 %collective-permute-start.15 = (bf16[512,128]{1,0:T(8,128)(2,1)S(1)}, bf16[512,128]{1,0:T(8,128)(2,1)S(1)}, u32[]{:S(2)}, u32[]{:S(2)}) collective-permute-start(bf16[512,128]{1,0:T(8,128)(2,1)S(1)} %get-tuple-element.50), channel_id=1, source_target_pairs={{0,2},{1,3},{2,0},{3,1},{4,6},{5,7},{6,4},{7,5},{8,10},{9,11},{10,... | collective-permute-start | bytes 393224 | tf_op jit(solution)/shard_map/ppermute | solution.py:59
  72.7 8.7 %collective-permute-start.16 = (bf16[512,128]{1,0:T(8,128)(2,1)S(1)}, bf16[512,128]{1,0:T(8,128)(2,1)S(1)}, u32[]{:S(2)}, u32[]{:S(2)}) collective-permute-start(bf16[512,128]{1,0:T(8,128)(2,1)S(1)} %get-tuple-element.51), channel_id=1, source_target_pairs={{0,3},{1,2},{2,1},{3,0},{4,7},{5,6},{6,5},{7,4},{8,11},{9,10},{10,... | collective-permute-start | bytes 393224 | tf_op jit(solution)/shard_map/ppermute | solution.py:59
  82.5 10.0 %collective-permute-start.19 = (bf16[608,128]{1,0:T(8,128)(2,1)S(1)}, bf16[608,128]{1,0:T(8,128)(2,1)S(1)}, u32[]{:S(2)}, u32[]{:S(2)}) collective-permute-start(bf16[608,128]{1,0:T(8,128)(2,1)S(1)} %image.2.b0), channel_id=1, source_target_pairs={{0,3},{1,2},{2,1},{3,0},{4,7},{5,6},{6,5},{7,4},{8,11},{9,10},{10,... | collective-permute-start | bytes 466952 | tf_op jit(solution)/shard_map/ppermute | solution.py:59
  83.3 9.2 %collective-permute-start.18 = (bf16[608,128]{1,0:T(8,128)(2,1)S(1)}, bf16[608,128]{1,0:T(8,128)(2,1)S(1)}, u32[]{:S(2)}, u32[]{:S(2)}) collective-permute-start(bf16[608,128]{1,0:T(8,128)(2,1)S(1)} %image.2.b0), channel_id=1, source_target_pairs={{0,2},{1,3},{2,0},{3,1},{4,6},{5,7},{6,4},{7,5},{8,10},{9,11},{10,... | collective-permute-start | bytes 466952 | tf_op jit(solution)/shard_map/ppermute | solution.py:59
  83.9 9.2 %collective-permute-start.17 = (bf16[608,128]{1,0:T(8,128)(2,1)S(1)}, bf16[608,128]{1,0:T(8,128)(2,1)S(1)}, u32[]{:S(2)}, u32[]{:S(2)}) collective-permute-start(bf16[608,128]{1,0:T(8,128)(2,1)S(1)} %image.2.b0), channel_id=1, source_target_pairs={{0,1},{1,0},{2,3},{3,2},{4,5},{5,4},{6,7},{7,6},{8,9},{9,8},{10,11... | collective-permute-start | bytes 466952 | tf_op jit(solution)/shard_map/ppermute | solution.py:59
  97.5 2.0 %collective-permute-start.20 = (bf16[2144,128]{1,0:T(8,128)(2,1)S(1)}, bf16[2144,128]{1,0:T(8,128)(2,1)S(1)}, u32[]{:S(2)}, u32[]{:S(2)}) collective-permute-start(bf16[2144,128]{1,0:T(8,128)(2,1)S(1)} %get-tuple-element.55), channel_id=1, source_target_pairs={{0,4},{4,0},{1,5},{5,1},{2,6},{6,2},{3,7},{7,3},{8,12},{12,8},{9,1... | collective-permute-start | bytes 1646600 | tf_op jit(solution)/shard_map/ppermute | solution.py:59
  99.7 6.9 %collective-permute-start.21 = (bf16[608,128]{1,0:T(8,128)(2,1)S(1)}, bf16[608,128]{1,0:T(8,128)(2,1)S(1)}, u32[]{:S(2)}, u32[]{:S(2)}) collective-permute-start(bf16[608,128]{1,0:T(8,128)(2,1)S(1)} %get-tuple-element.57), channel_id=1, source_target_pairs={{0,32},{32,0},{64,96},{96,64},{1,33},{33,1},{65,97},{97,65},{2,34}... | collective-permute-start | bytes 466952 | tf_op jit(solution)/shard_map/ppermute | solution.py:59
  100.5 9.6 %collective-permute-start.22 = (bf16[608,128]{1,0:T(8,128)(2,1)S(1)}, bf16[608,128]{1,0:T(8,128)(2,1)S(1)}, u32[]{:S(2)}, u32[]{:S(2)}) collective-permute-start(bf16[608,128]{1,0:T(8,128)(2,1)S(1)} %get-tuple-element.58), channel_id=1, source_target_pairs={{0,64},{32,96},{64,0},{96,32},{1,65},{33,97},{65,1},{97,33},{2,66}... | collective-permute-start | bytes 466952 | tf_op jit(solution)/shard_map/ppermute | solution.py:59
  102.6 10.0 %collective-permute-start.23 = (bf16[608,128]{1,0:T(8,128)(2,1)S(1)}, bf16[608,128]{1,0:T(8,128)(2,1)S(1)}, u32[]{:S(2)}, u32[]{:S(2)}) collective-permute-start(bf16[608,128]{1,0:T(8,128)(2,1)S(1)} %get-tuple-element.59), channel_id=1, source_target_pairs={{0,96},{32,64},{64,32},{96,0},{1,97},{33,65},{65,33},{97,1},{2,98}... | collective-permute-start | bytes 466952 | tf_op jit(solution)/shard_map/ppermute | solution.py:59
  112.8 8.9 %collective-permute-start.26 = (bf16[608,128]{1,0:T(8,128)(2,1)S(1)}, bf16[608,128]{1,0:T(8,128)(2,1)S(1)}, u32[]{:S(2)}, u32[]{:S(2)}) collective-permute-start(bf16[608,128]{1,0:T(8,128)(2,1)S(1)} %get-tuple-element.61.refs_0_), channel_id=1, source_target_pairs={{0,24},{8,16},{16,8},{24,0},{1,25},{9,17},{17,9},{25,1},{2,26},{10... | collective-permute-start | bytes 466952 | tf_op jit(solution)/shard_map/ppermute | solution.py:59
  115.5 8.2 %collective-permute-start.25 = (bf16[608,128]{1,0:T(8,128)(2,1)S(1)}, bf16[608,128]{1,0:T(8,128)(2,1)S(1)}, u32[]{:S(2)}, u32[]{:S(2)}) collective-permute-start(bf16[608,128]{1,0:T(8,128)(2,1)S(1)} %get-tuple-element.61.refs_0_), channel_id=1, source_target_pairs={{0,16},{8,24},{16,0},{24,8},{1,17},{9,25},{17,1},{25,9},{2,18},{10... | collective-permute-start | bytes 466952 | tf_op jit(solution)/shard_map/ppermute | solution.py:59
  115.5 8.2 %collective-permute-start.24 = (bf16[608,128]{1,0:T(8,128)(2,1)S(1)}, bf16[608,128]{1,0:T(8,128)(2,1)S(1)}, u32[]{:S(2)}, u32[]{:S(2)}) collective-permute-start(bf16[608,128]{1,0:T(8,128)(2,1)S(1)} %get-tuple-element.61.refs_0_), channel_id=1, source_target_pairs={{0,8},{8,0},{16,24},{24,16},{1,9},{9,1},{17,25},{25,17},{2,10},{10... | collective-permute-start | bytes 466952 | tf_op jit(solution)/shard_map/ppermute | solution.py:59
  125.9 6.4 %collective-permute-start.29 = (bf16[512,128]{1,0:T(8,128)(2,1)S(1)}, bf16[512,128]{1,0:T(8,128)(2,1)S(1)}, u32[]{:S(2)}, u32[]{:S(2)}) collective-permute-start(bf16[512,128]{1,0:T(8,128)(2,1)S(1)} %weigh.3.w0), channel_id=1, source_target_pairs={{0,96},{32,64},{64,32},{96,0},{1,97},{33,65},{65,33},{97,1},{2,98}... | collective-permute-start | bytes 393224 | tf_op jit(solution)/shard_map/ppermute | solution.py:59
  127.8 6.5 %collective-permute-start.28 = (bf16[512,128]{1,0:T(8,128)(2,1)S(1)}, bf16[512,128]{1,0:T(8,128)(2,1)S(1)}, u32[]{:S(2)}, u32[]{:S(2)}) collective-permute-start(bf16[512,128]{1,0:T(8,128)(2,1)S(1)} %weigh.3.w0), channel_id=1, source_target_pairs={{0,64},{32,96},{64,0},{96,32},{1,65},{33,97},{65,1},{97,33},{2,66}... | collective-permute-start | bytes 393224 | tf_op jit(solution)/shard_map/ppermute | solution.py:59
  127.8 6.5 %collective-permute-start.27 = (bf16[512,128]{1,0:T(8,128)(2,1)S(1)}, bf16[512,128]{1,0:T(8,128)(2,1)S(1)}, u32[]{:S(2)}, u32[]{:S(2)}) collective-permute-start(bf16[512,128]{1,0:T(8,128)(2,1)S(1)} %weigh.3.w0), channel_id=1, source_target_pairs={{0,32},{32,0},{64,96},{96,64},{1,33},{33,1},{65,97},{97,65},{2,34}... | collective-permute-start | bytes 393224 | tf_op jit(solution)/shard_map/ppermute | solution.py:59
  140.6 6.4 %collective-permute-start.31 = (bf16[512,128]{1,0:T(8,128)(2,1)S(1)}, bf16[512,128]{1,0:T(8,128)(2,1)S(1)}, u32[]{:S(2)}, u32[]{:S(2)}) collective-permute-start(bf16[512,128]{1,0:T(8,128)(2,1)S(1)} %get-tuple-element.65), channel_id=1, source_target_pairs={{0,1},{1,0},{2,3},{3,2},{4,5},{5,4},{6,7},{7,6},{8,9},{9,8},{10,11... | collective-permute-start | bytes 393224 | tf_op jit(solution)/shard_map/ppermute | solution.py:59
  140.7 8.9 %collective-permute-start.32 = (bf16[512,128]{1,0:T(8,128)(2,1)S(1)}, bf16[512,128]{1,0:T(8,128)(2,1)S(1)}, u32[]{:S(2)}, u32[]{:S(2)}) collective-permute-start(bf16[512,128]{1,0:T(8,128)(2,1)S(1)} %get-tuple-element.66), channel_id=1, source_target_pairs={{0,2},{1,3},{2,0},{3,1},{4,6},{5,7},{6,4},{7,5},{8,10},{9,11},{10,... | collective-permute-start | bytes 393224 | tf_op jit(solution)/shard_map/ppermute | solution.py:59
  143.1 8.7 %collective-permute-start.33 = (bf16[512,128]{1,0:T(8,128)(2,1)S(1)}, bf16[512,128]{1,0:T(8,128)(2,1)S(1)}, u32[]{:S(2)}, u32[]{:S(2)}) collective-permute-start(bf16[512,128]{1,0:T(8,128)(2,1)S(1)} %get-tuple-element.67), channel_id=1, source_target_pairs={{0,3},{1,2},{2,1},{3,0},{4,7},{5,6},{6,5},{7,4},{8,11},{9,10},{10,... | collective-permute-start | bytes 393224 | tf_op jit(solution)/shard_map/ppermute | solution.py:59
  (7 other events, 46.3 us)

commit v3 on v2

--- a/solution.py
+++ b/solution.py
@@ -19,9 +19,10 @@
 CHUNK = OWN * K
 COUNT_ROWS = 16
 PACKED = 96
-TURN = 16
+TURN = 32
+SEND = (1, 2, 3)
 PIVOTS = 8
-UNROLL = 32
+UNROLL = 128
 PREP_STEP = 32
 MIB = 1 << 20
 PREP_LIMIT = 32 * MIB
@@ -72,6 +73,14 @@
     rest = value - high.astype(f32)
     middle = rest.astype(bf16)
     return high, middle, (rest - middle.astype(f32)).astype(bf16)
+
+
+def times(factor, value):
+    f_high, f_low, _ = split3(factor)
+    v_high, v_low, _ = split3(value)
+    both = jnp.dot(jnp.concatenate([f_high, f_low], axis=0), v_high, preferred_element_type=f32)
+    low = jnp.dot(f_high, v_low, preferred_element_type=f32)
+    return both[:K] + (both[K:] + low)
 
 
 def pack_gram(gram):
@@ -250,12 +259,12 @@
 
 def halves_kernel(first, *refs):
     if first:
-        keep, arrived, own, s1, s2, s3 = refs
+        keep, arrived, own, *sent = refs
     else:
-        keep, gram, arrived, own, s1, s2, s3, gram_out = refs
+        keep, gram, arrived, own, *sent, gram_out = refs
         gram_out[...] = gram[...] + unpack_gram(arrived[4 * CHUNK : 4 * CHUNK + PACKED, :])
         packed = pack_gram(gram_out[...])
-    for r, out in enumerate((own, s1, s2, s3)):
+    for r, out in ((0, own), *zip(SEND, sent)):
         at = slice(r * CHUNK, (r + 1) * CHUNK)
         out[:CHUNK, :] = (keep[at, :] + arrived[at, :].astype(f32)).astype(out.dtype)
         if first:
@@ -331,11 +340,12 @@
     for k in range(OWN):
         tile = add4(p0, p1, p2, p3, tile_rows(k))
         if not first:
-            tile = jnp.dot(factor, tile, precision=HIGHEST, preferred_element_type=f32)
+            tile = times(factor, tile)
         weighted[tile_rows(k), :] = (tile * scale[k : k + 1, :]).astype(bf16)
 
 
 def backward_kernel(place, coords, w0, w1, w2, w3, other, turned, own, s1, s2, s3, source, acc):
+    sent = (s1, s2, s3)
     x, z, c, y, _ = place_of(place)
     for r, block in enumerate((w0, w1, w2, w3)):
         base = c * (COL_TILES // 2) + (x ^ r) * OWN
@@ -344,7 +354,7 @@
             source[base + k] = block[tile_rows(k), :]
             source[far + k] = other[r, tile_rows(k), :]
     tile_products(coords, turned, source, acc, 1, 0)
-    for s, out in enumerate((own, s1, s2, s3)):
+    for s, out in ((0, own), *zip(SEND, sent)):
         base = (y ^ s) * OWN
         for k in range(OWN):
             out[tile_rows(k), :] = acc[base + k].astype(out.dtype)
@@ -400,9 +410,7 @@
         whole[pl.ds(pl.multiple_of(at * (K // 2), K // 2), K // 2), :] = rows
     factor = inverse_factor(whole[...])
     for k in range(OWN):
-        out[:, k * TILE : (k + 1) * TILE] = jnp.dot(
-            factor, image[tile_rows(k), :], precision=HIGHEST, preferred_element_type=f32
-        )
+        out[:, k * TILE : (k + 1) * TILE] = times(factor, image[tile_rows(k), :])
 
 
 def spread(value, axis):
@@ -410,7 +418,8 @@
 
 
 def swapped(values, axis):
-    return [swap(value, axis, s + 1) for s, value in enumerate(values)]
+    arrived = {s: swap(value, axis, s) for s, value in zip(SEND, values)}
+    return [arrived[s] for s in (3, 2, 1)]
 
 
 def body(start_vectors, bucket_weight, tile_count, tile_coords, patterns):

time: 181 us -> 170 us (0.939)
  waiting for transfers between devices: 73.7 us -> 68.8 us
  Pallas kernels: 36.8 us -> 32.6 us
  starting transfers between devices: 45.4 us -> 43 us
    ppermute x36, waiting for transfers between devices: 73.7 us -> 68.8 us  [swap(): return lax.ppermute(value, axis, [(i, i ^ mask) for i in range(size)])]
    ppermute x36, starting transfers between devices: 45.4 us -> 43 us  [swap(): return lax.ppermute(value, axis, [(i, i ^ mask) for i in range(size)])]
    pallas_call x2, Pallas kernels: 8.29 us -> 6.47 us  [backward(): call(backward_kernel, 'backward', tuple(outs), [SMEM, SMEM] + [VMEM] * 6,...]
  transfers between devices with their start and end apart: 36 -> 36, of which waited for: 30 -> 27; matrix products, arithmetic and copies ran while one was open for 0% -> 0% of each run, Pallas kernels for 2% -> 2%
where the time goes in v3:
time: 170 us; the launch traced here: 169 us
  waiting for transfers between devices  68.8 us (40%)
  starting transfers between devices  43 us (25%)
  Pallas kernels  32.6 us (19%)
  blocking collectives  21.3 us (13%)
  local copies, waits for them, and re-layouts  1.84 us (1%)
    ppermute x36, waiting for transfers between devices, swap(): return lax.ppermute(value, axis, [(i, i ^ mask) for i in range(size)])  68.8 us
    ppermute x36, starting transfers between devices, swap(): return lax.ppermute(value, axis, [(i, i ^ mask) for i in range(size)])  43 us
    all_to_all x1, blocking collectives, body(): lax.all_to_all(copies, others, split_axis=0, concat_axis=0, tiled=True)  21.3 us
    pallas_call x1, Pallas kernels, prep(): pl.pallas_call(prep_kernel, out_shape=(shape(SLOTS, TILE, TILE, dtype=bf1...  7.71 us
    pallas_call x2, Pallas kernels, forward(): call(functools.partial(forward_kernel, first), 'forward', outs, [SMEM, SM...  6.87 us
    pallas_call x2, Pallas kernels, backward(): call(backward_kernel, 'backward', tuple(outs), [SMEM, SMEM] + [VMEM] * 6,...  6.47 us
  transfers between devices with their start and end apart: 36, of which 27 were waited for; matrix products, arithmetic and copies ran while one was open for 0% of the time, Pallas kernels for 2%

profile of v3, /device:TPU:0, one launch (start us, length us, event | category | flops | bytes accessed | tf_op | source)
XLA Modules:
  0.0 168.6 jit_solution(1271829835809109217)
XLA Ops:
  2.5 7.7 %prep.1 = (bf16[256,128,128]{2,1,0:T(8,128)(2,1)S(1)}, f32[32,128]{1,0:T(8,128)S(1)}, f32[64,128]{1,0:T(8,128)S(1)}) custom-call(s32[5]{0:T(128)S(1)} %stack.49.place.refs_0_, s32[512]{0:T(512)S(1)} %reshape.9.coords, f32[64,128]{1,0:T(8,128)S(1)} %bitcast.19, s32[256,128,128]{2,1,0:T(8,128)} %bitcast.28), custom_call_target="tpu_custom_call" | custom-call | flops 1000000000 | bytes 25165824 | tf_op jit(solution)/shard_map/prep/pallas_call | solution.py:154
  10.2 3.2 %collective-permute-start.2 = (bf16[608,128]{1,0:T(8,128)(2,1)S(1)}, bf16[608,128]{1,0:T(8,128)(2,1)S(1)}, u32[]{:S(2)}, u32[]{:S(2)}) collective-permute-start(bf16[608,128]{1,0:T(8,128)(2,1)S(1)} %pack.1.b0), channel_id=1, source_target_pairs={{0,3},{1,2},{2,1},{3,0},{4,7},{5,6},{6,5},{7,4},{8,11},{9,10},{10,... | collective-permute-start | bytes 466952 | tf_op jit(solution)/shard_map/ppermute | solution.py:60
  14.4 2.6 %turn.1.refs_1_.turned = bf16[256,128,128]{2,1,0:T(8,128)(2,1)S(1)} custom-call(bf16[256,128,128]{2,1,0:T(8,128)(2,1)S(1)} %get-tuple-element.39.pattern), custom_call_target="tpu_custom_call" | custom-call | bytes 16777216 | tf_op jit(solution)/shard_map/turn/pallas_call | solution.py:433
  17.0 3.0 %collective-permute-done.2.b3 = bf16[608,128]{1,0:T(8,128)(2,1)S(1)} collective-permute-done((bf16[608,128]{1,0:T(8,128)(2,1)S(1)}, bf16[608,128]{1,0:T(8,128)(2,1)S(1)}, u32[]{:S(2)}, u32[]{:S(2)}) %collective-permute-start.2) | collective-permute-done | bytes 155680 | tf_op jit(solution)/shard_map/ppermute | solution.py:60
  21.9 3.4 %forward.2 = (f32[2112,128]{1,0:T(8,128)S(1)}, bf16[2112,128]{1,0:T(8,128)(2,1)S(1)}, f32[32,128]{1,0:T(8,128)S(1)}) custom-call(s32[5]{0:T(128)S(1)} %stack.49.place.refs_0_, s32[512]{0:T(512)S(1)} %reshape.9.coords, bf16[608,128]{1,0:T(8,128)(2,1)S(1)} %pack.1.b0, bf16[608,128]{1,0:T(8,128)(2,1)S(1)} %collective-permute-done.b1, ...), custom_call_target="tpu_custom_call" | custom-call | flops 6000000000 | bytes 12582912 | tf_op jit(solution)/shard_map/forward/pallas_call | solution.py:248
  27.4 2.9 %collective-permute-start.4 = (bf16[528,128]{1,0:T(8,128)(2,1)S(1)}, bf16[528,128]{1,0:T(8,128)(2,1)S(1)}, u32[]{:S(2)}, u32[]{:S(2)}) collective-permute-start(bf16[528,128]{1,0:T(8,128)(2,1)S(1)} %get-tuple-element.44), channel_id=1, source_target_pairs={{0,96},{32,64},{64,32},{96,0},{1,97},{33,65},{65,33},{97,1},{2,98}... | collective-permute-start | bytes 405512 | tf_op jit(solution)/shard_map/ppermute | solution.py:60
  31.6 4.7 %collective-permute-done.4.refs_1_ = bf16[528,128]{1,0:T(8,128)(2,1)S(1)} collective-permute-done((bf16[528,128]{1,0:T(8,128)(2,1)S(1)}, bf16[528,128]{1,0:T(8,128)(2,1)S(1)}, u32[]{:S(2)}, u32[]{:S(2)}) %collective-permute-start.4) | collective-permute-done | bytes 135200 | tf_op jit(solution)/shard_map/ppermute | solution.py:60
  38.3 4.1 %collective-permute-start.9 = (bf16[528,128]{1,0:T(8,128)(2,1)S(1)}, bf16[528,128]{1,0:T(8,128)(2,1)S(1)}, u32[]{:S(2)}, u32[]{:S(2)}) collective-permute-start(bf16[528,128]{1,0:T(8,128)(2,1)S(1)} %total.2.refs_1_), channel_id=1, source_target_pairs={{0,24},{8,16},{16,8},{24,0},{1,25},{9,17},{17,9},{25,1},{2,26},{10... | collective-permute-start | bytes 405512 | tf_op jit(solution)/shard_map/ppermute | solution.py:60
  43.4 3.7 %collective-permute-done.9.refs_4_ = bf16[528,128]{1,0:T(8,128)(2,1)S(1)} collective-permute-done((bf16[528,128]{1,0:T(8,128)(2,1)S(1)}, bf16[528,128]{1,0:T(8,128)(2,1)S(1)}, u32[]{:S(2)}, u32[]{:S(2)}) %collective-permute-start.9) | collective-permute-done | bytes 135200 | tf_op jit(solution)/shard_map/ppermute | solution.py:60
  47.0 2.3 %collective-permute-done.8.refs_3_ = bf16[528,128]{1,0:T(8,128)(2,1)S(1)} collective-permute-done((bf16[528,128]{1,0:T(8,128)(2,1)S(1)}, bf16[528,128]{1,0:T(8,128)(2,1)S(1)}, u32[]{:S(2)}, u32[]{:S(2)}) %collective-permute-start.8) | collective-permute-done | bytes 135200 | tf_op jit(solution)/shard_map/ppermute | solution.py:60
  49.9 2.8 %collective-permute-start.12 = (bf16[512,128]{1,0:T(8,128)(2,1)S(1)}, bf16[512,128]{1,0:T(8,128)(2,1)S(1)}, u32[]{:S(2)}, u32[]{:S(2)}) collective-permute-start(bf16[512,128]{1,0:T(8,128)(2,1)S(1)} %get-tuple-element.47.w0), channel_id=1, source_target_pairs={{0,96},{32,64},{64,32},{96,0},{1,97},{33,65},{65,33},{97,1},{2,98}... | collective-permute-start | bytes 393224 | tf_op jit(solution)/shard_map/ppermute | solution.py:60
  54.1 2.6 %collective-permute-done.12.w3 = bf16[512,128]{1,0:T(8,128)(2,1)S(1)} collective-permute-done((bf16[512,128]{1,0:T(8,128)(2,1)S(1)}, bf16[512,128]{1,0:T(8,128)(2,1)S(1)}, u32[]{:S(2)}, u32[]{:S(2)}) %collective-permute-start.12) | collective-permute-done | bytes 131104 | tf_op jit(solution)/shard_map/ppermute | solution.py:60
  56.7 2.5 %collective-permute-done.11.w2 = bf16[512,128]{1,0:T(8,128)(2,1)S(1)} collective-permute-done((bf16[512,128]{1,0:T(8,128)(2,1)S(1)}, bf16[512,128]{1,0:T(8,128)(2,1)S(1)}, u32[]{:S(2)}, u32[]{:S(2)}) %collective-permute-start.11) | collective-permute-done | bytes 131104 | tf_op jit(solution)/shard_map/ppermute | solution.py:60
  61.3 3.2 %backward.2 = (f32[512,128]{1,0:T(8,128)S(1)}, bf16[512,128]{1,0:T(8,128)(2,1)S(1)}, bf16[512,128]{1,0:T(8,128)(2,1)S(1)}, bf16[512,128]{1,0:T(8,128)(2,1)S(1)}) custom-call(s32[5]{0:T(128)S(1)} %stack.49.place.refs_0_, s32[512]{0:T(512)S(1)} %reshape.9.coords, bf16[512,128]{1,0:T(8,128)(2,1)S(1)} %get-tuple-element.47.w0, ...), custom_call_target="tpu_custom_call" | custom-call | flops 6000000000 | bytes 12582912 | tf_op jit(solution)/shard_map/backward/pallas_call | solution.py:365
  64.6 2.6 %collective-permute-start.14 = (bf16[512,128]{1,0:T(8,128)(2,1)S(1)}, bf16[512,128]{1,0:T(8,128)(2,1)S(1)}, u32[]{:S(2)}, u32[]{:S(2)}) collective-permute-start(bf16[512,128]{1,0:T(8,128)(2,1)S(1)} %get-tuple-element.49), channel_id=1, source_target_pairs={{0,3},{1,2},{2,1},{3,0},{4,7},{5,6},{6,5},{7,4},{8,11},{9,10},{10,... | collective-permute-start | bytes 393224 | tf_op jit(solution)/shard_map/ppermute | solution.py:60
  68.7 4.7 %collective-permute-done.14.r1 = bf16[512,128]{1,0:T(8,128)(2,1)S(1)} collective-permute-done((bf16[512,128]{1,0:T(8,128)(2,1)S(1)}, bf16[512,128]{1,0:T(8,128)(2,1)S(1)}, u32[]{:S(2)}, u32[]{:S(2)}) %collective-permute-start.14) | collective-permute-done | bytes 131104 | tf_op jit(solution)/shard_map/ppermute | solution.py:60
  76.2 2.4 %collective-permute-start.19 = (bf16[608,128]{1,0:T(8,128)(2,1)S(1)}, bf16[608,128]{1,0:T(8,128)(2,1)S(1)}, u32[]{:S(2)}, u32[]{:S(2)}) collective-permute-start(bf16[608,128]{1,0:T(8,128)(2,1)S(1)} %image.2.b0), channel_id=1, source_target_pairs={{0,3},{1,2},{2,1},{3,0},{4,7},{5,6},{6,5},{7,4},{8,11},{9,10},{10,... | collective-permute-start | bytes 466952 | tf_op jit(solution)/shard_map/ppermute | solution.py:60
  80.4 4.7 %collective-permute-done.19.b3 = bf16[608,128]{1,0:T(8,128)(2,1)S(1)} collective-permute-done((bf16[608,128]{1,0:T(8,128)(2,1)S(1)}, bf16[608,128]{1,0:T(8,128)(2,1)S(1)}, u32[]{:S(2)}, u32[]{:S(2)}) %collective-permute-start.19) | collective-permute-done | bytes 155680 | tf_op jit(solution)/shard_map/ppermute | solution.py:60
  86.5 3.4 %forward.3 = (f32[2048,128]{1,0:T(8,128)S(1)}, bf16[2144,128]{1,0:T(8,128)(2,1)S(1)}, f32[64,64]{1,0:T(8,128)S(1)}) custom-call(s32[5]{0:T(128)S(1)} %stack.49.place.refs_0_, s32[512]{0:T(512)S(1)} %reshape.9.coords, bf16[608,128]{1,0:T(8,128)(2,1)S(1)} %image.2.b0, bf16[608,128]{1,0:T(8,128)(2,1)S(1)} %collective-permute-done.17.b1, ...), custom_call_target="tpu_custom_call" | custom-call | flops 6000000000 | bytes 12582912 | tf_op jit(solution)/shard_map/forward/pallas_call | solution.py:248
  92.1 2.0 %collective-permute-start.21 = (bf16[608,128]{1,0:T(8,128)(2,1)S(1)}, bf16[608,128]{1,0:T(8,128)(2,1)S(1)}, u32[]{:S(2)}, u32[]{:S(2)}) collective-permute-start(bf16[608,128]{1,0:T(8,128)(2,1)S(1)} %get-tuple-element.57), channel_id=1, source_target_pairs={{0,96},{32,64},{64,32},{96,0},{1,97},{33,65},{65,33},{97,1},{2,98}... | collective-permute-start | bytes 466952 | tf_op jit(solution)/shard_map/ppermute | solution.py:60
  96.3 6.5 %collective-permute-done.21.refs_1_ = bf16[608,128]{1,0:T(8,128)(2,1)S(1)} collective-permute-done((bf16[608,128]{1,0:T(8,128)(2,1)S(1)}, bf16[608,128]{1,0:T(8,128)(2,1)S(1)}, u32[]{:S(2)}, u32[]{:S(2)}) %collective-permute-start.21) | collective-permute-done | bytes 155680 | tf_op jit(solution)/shard_map/ppermute | solution.py:60
  103.7 2.6 %collective-permute-start.26 = (bf16[608,128]{1,0:T(8,128)(2,1)S(1)}, bf16[608,128]{1,0:T(8,128)(2,1)S(1)}, u32[]{:S(2)}, u32[]{:S(2)}) collective-permute-start(bf16[608,128]{1,0:T(8,128)(2,1)S(1)} %get-tuple-element.61.refs_0_), channel_id=1, source_target_pairs={{0,24},{8,16},{16,8},{24,0},{1,25},{9,17},{17,9},{25,1},{2,26},{10... | collective-permute-start | bytes 466952 | tf_op jit(solution)/shard_map/ppermute | solution.py:60
  107.9 4.4 %collective-permute-done.26.refs_3_ = bf16[608,128]{1,0:T(8,128)(2,1)S(1)} collective-permute-done((bf16[608,128]{1,0:T(8,128)(2,1)S(1)}, bf16[608,128]{1,0:T(8,128)(2,1)S(1)}, u32[]{:S(2)}, u32[]{:S(2)}) %collective-permute-start.26) | collective-permute-done | bytes 155680 | tf_op jit(solution)/shard_map/ppermute | solution.py:60
  114.2 2.0 %weigh.3.w0 = bf16[512,128]{1,0:T(8,128)(2,1)S(1)} custom-call(bf16[608,128]{1,0:T(8,128)(2,1)S(1)} %get-tuple-element.61.refs_0_, bf16[608,128]{1,0:T(8,128)(2,1)S(1)} %collective-permute-done.24.refs_1_, bf16[608,128]{1,0:T(8,128)(2,1)S(1)} %collective-permute-done.25.refs_2_, bf16[608,128]{1,0:T(8,128)(2,1)S(1)} %collective-permute-done.26.refs_3_, ...), custom_call_target="tpu_custom_call" | custom-call | tf_op jit(solution)/shard_map/weigh/pallas_call | solution.py:449
  116.2 2.1 %collective-permute-start.29 = (bf16[512,128]{1,0:T(8,128)(2,1)S(1)}, bf16[512,128]{1,0:T(8,128)(2,1)S(1)}, u32[]{:S(2)}, u32[]{:S(2)}) collective-permute-start(bf16[512,128]{1,0:T(8,128)(2,1)S(1)} %weigh.3.w0), channel_id=1, source_target_pairs={{0,96},{32,64},{64,32},{96,0},{1,97},{33,65},{65,33},{97,1},{2,98}... | collective-permute-start | bytes 393224 | tf_op jit(solution)/shard_map/ppermute | solution.py:60
  120.4 2.1 %collective-permute-done.29.w3 = bf16[512,128]{1,0:T(8,128)(2,1)S(1)} collective-permute-done((bf16[512,128]{1,0:T(8,128)(2,1)S(1)}, bf16[512,128]{1,0:T(8,128)(2,1)S(1)}, u32[]{:S(2)}, u32[]{:S(2)}) %collective-permute-start.29) | collective-permute-done | bytes 131104 | tf_op jit(solution)/shard_map/ppermute | solution.py:60
  122.5 2.3 %collective-permute-done.28.w2 = bf16[512,128]{1,0:T(8,128)(2,1)S(1)} collective-permute-done((bf16[512,128]{1,0:T(8,128)(2,1)S(1)}, bf16[512,128]{1,0:T(8,128)(2,1)S(1)}, u32[]{:S(2)}, u32[]{:S(2)}) %collective-permute-start.28) | collective-permute-done | bytes 131104 | tf_op jit(solution)/shard_map/ppermute | solution.py:60
  126.8 3.2 %backward.3 = (f32[512,128]{1,0:T(8,128)S(1)}, bf16[512,128]{1,0:T(8,128)(2,1)S(1)}, bf16[512,128]{1,0:T(8,128)(2,1)S(1)}, bf16[512,128]{1,0:T(8,128)(2,1)S(1)}) custom-call(s32[5]{0:T(128)S(1)} %stack.49.place.refs_0_, s32[512]{0:T(512)S(1)} %reshape.9.coords, bf16[512,128]{1,0:T(8,128)(2,1)S(1)} %weigh.3.w0, ...), custom_call_target="tpu_custom_call" | custom-call | flops 6000000000 | bytes 12582912 | tf_op jit(solution)/shard_map/backward/pallas_call | solution.py:365
  130.1 2.3 %collective-permute-start.31 = (bf16[512,128]{1,0:T(8,128)(2,1)S(1)}, bf16[512,128]{1,0:T(8,128)(2,1)S(1)}, u32[]{:S(2)}, u32[]{:S(2)}) collective-permute-start(bf16[512,128]{1,0:T(8,128)(2,1)S(1)} %get-tuple-element.65), channel_id=1, source_target_pairs={{0,3},{1,2},{2,1},{3,0},{4,7},{5,6},{6,5},{7,4},{8,11},{9,10},{10,... | collective-permute-start | bytes 393224 | tf_op jit(solution)/shard_map/ppermute | solution.py:60
  134.3 4.9 %collective-permute-done.31.r1 = bf16[512,128]{1,0:T(8,128)(2,1)S(1)} collective-permute-done((bf16[512,128]{1,0:T(8,128)(2,1)S(1)}, bf16[512,128]{1,0:T(8,128)(2,1)S(1)}, u32[]{:S(2)}, u32[]{:S(2)}) %collective-permute-start.31) | collective-permute-done | bytes 131104 | tf_op jit(solution)/shard_map/ppermute | solution.py:60
  142.7 21.3 %all_to_all.5.parts = f32[64,16,128]{2,1,0:T(8,128)S(1)} all-to-all(f32[64,16,128]{2,1,0:T(8,128)S(1)} %broadcast_in_dim.3), channel_id=1, replica_groups=mesh['doc_0'=4,'doc_1'=4,'doc_2'=2,'bkt'=4] {'doc_0','doc_1','bkt'}, dimensions={0} | all-to-all | bytes 1048576 | tf_op jit(solution)/shard_map/all_to_all | solution.py:470
  165.3 3.2 %solve.1 = f32[64,1024]{1,0:T(8,128)} custom-call(s32[5]{0:T(128)S(1)} %stack.49.place.refs_0_, f32[16,128]{1,0:T(8,128)S(1)} %sum.1.half, f32[16,128]{1,0:T(8,128)S(1)} %collective-permute-done.35.other, f32[512,128]{1,0:T(8,128)S(1)} %get-tuple-element.70.image), custom_call_target="tpu_custom_call" | custom-call | tf_op jit(solution)/shard_map/solve/pallas_call | solution.py:472
  (71 shorter events, 42.3 us)
Async XLA Ops:
  10.2 9.8 %collective-permute-start.2 = (bf16[608,128]{1,0:T(8,128)(2,1)S(1)}, bf16[608,128]{1,0:T(8,128)(2,1)S(1)}, u32[]{:S(2)}, u32[]{:S(2)}) collective-permute-start(bf16[608,128]{1,0:T(8,128)(2,1)S(1)} %pack.1.b0), channel_id=1, source_target_pairs={{0,3},{1,2},{2,1},{3,0},{4,7},{5,6},{6,5},{7,4},{8,11},{9,10},{10,... | collective-permute-start | bytes 466952 | tf_op jit(solution)/shard_map/ppermute | solution.py:60
  13.4 8.5 %collective-permute-start.1 = (bf16[608,128]{1,0:T(8,128)(2,1)S(1)}, bf16[608,128]{1,0:T(8,128)(2,1)S(1)}, u32[]{:S(2)}, u32[]{:S(2)}) collective-permute-start(bf16[608,128]{1,0:T(8,128)(2,1)S(1)} %pack.1.b0), channel_id=1, source_target_pairs={{0,2},{1,3},{2,0},{3,1},{4,6},{5,7},{6,4},{7,5},{8,10},{9,11},{10,... | collective-permute-start | bytes 466952 | tf_op jit(solution)/shard_map/ppermute | solution.py:60
  14.0 7.8 %collective-permute-start = (bf16[608,128]{1,0:T(8,128)(2,1)S(1)}, bf16[608,128]{1,0:T(8,128)(2,1)S(1)}, u32[]{:S(2)}, u32[]{:S(2)}) collective-permute-start(bf16[608,128]{1,0:T(8,128)(2,1)S(1)} %pack.1.b0), channel_id=1, source_target_pairs={{0,1},{1,0},{2,3},{3,2},{4,5},{5,4},{6,7},{7,6},{8,9},{9,8},{10,11... | collective-permute-start | bytes 466952 | tf_op jit(solution)/shard_map/ppermute | solution.py:60
  25.3 2.0 %collective-permute-start.3 = (bf16[2112,128]{1,0:T(8,128)(2,1)S(1)}, bf16[2112,128]{1,0:T(8,128)(2,1)S(1)}, u32[]{:S(2)}, u32[]{:S(2)}) collective-permute-start(bf16[2112,128]{1,0:T(8,128)(2,1)S(1)} %get-tuple-element.42), channel_id=1, source_target_pairs={{0,4},{4,0},{1,5},{5,1},{2,6},{6,2},{3,7},{7,3},{8,12},{12,8},{9,1... | collective-permute-start | bytes 1622024 | tf_op jit(solution)/shard_map/ppermute | solution.py:60
  27.4 8.9 %collective-permute-start.4 = (bf16[528,128]{1,0:T(8,128)(2,1)S(1)}, bf16[528,128]{1,0:T(8,128)(2,1)S(1)}, u32[]{:S(2)}, u32[]{:S(2)}) collective-permute-start(bf16[528,128]{1,0:T(8,128)(2,1)S(1)} %get-tuple-element.44), channel_id=1, source_target_pairs={{0,96},{32,64},{64,32},{96,0},{1,97},{33,65},{65,33},{97,1},{2,98}... | collective-permute-start | bytes 405512 | tf_op jit(solution)/shard_map/ppermute | solution.py:60
  30.3 8.0 %collective-permute-start.5 = (bf16[528,128]{1,0:T(8,128)(2,1)S(1)}, bf16[528,128]{1,0:T(8,128)(2,1)S(1)}, u32[]{:S(2)}, u32[]{:S(2)}) collective-permute-start(bf16[528,128]{1,0:T(8,128)(2,1)S(1)} %get-tuple-element.45), channel_id=1, source_target_pairs={{0,64},{32,96},{64,0},{96,32},{1,65},{33,97},{65,1},{97,33},{2,66}... | collective-permute-start | bytes 405512 | tf_op jit(solution)/shard_map/ppermute | solution.py:60
  31.1 7.2 %collective-permute-start.6 = (bf16[528,128]{1,0:T(8,128)(2,1)S(1)}, bf16[528,128]{1,0:T(8,128)(2,1)S(1)}, u32[]{:S(2)}, u32[]{:S(2)}) collective-permute-start(bf16[528,128]{1,0:T(8,128)(2,1)S(1)} %get-tuple-element.46), channel_id=1, source_target_pairs={{0,32},{32,0},{64,96},{96,64},{1,33},{33,1},{65,97},{97,65},{2,34}... | collective-permute-start | bytes 405512 | tf_op jit(solution)/shard_map/ppermute | solution.py:60
  38.3 8.7 %collective-permute-start.9 = (bf16[528,128]{1,0:T(8,128)(2,1)S(1)}, bf16[528,128]{1,0:T(8,128)(2,1)S(1)}, u32[]{:S(2)}, u32[]{:S(2)}) collective-permute-start(bf16[528,128]{1,0:T(8,128)(2,1)S(1)} %total.2.refs_1_), channel_id=1, source_target_pairs={{0,24},{8,16},{16,8},{24,0},{1,25},{9,17},{17,9},{25,1},{2,26},{10... | collective-permute-start | bytes 405512 | tf_op jit(solution)/shard_map/ppermute | solution.py:60
  42.4 6.9 %collective-permute-start.8 = (bf16[528,128]{1,0:T(8,128)(2,1)S(1)}, bf16[528,128]{1,0:T(8,128)(2,1)S(1)}, u32[]{:S(2)}, u32[]{:S(2)}) collective-permute-start(bf16[528,128]{1,0:T(8,128)(2,1)S(1)} %total.2.refs_1_), channel_id=1, source_target_pairs={{0,16},{8,24},{16,0},{24,8},{1,17},{9,25},{17,1},{25,9},{2,18},{10... | collective-permute-start | bytes 405512 | tf_op jit(solution)/shard_map/ppermute | solution.py:60
  42.4 6.9 %collective-permute-start.7 = (bf16[528,128]{1,0:T(8,128)(2,1)S(1)}, bf16[528,128]{1,0:T(8,128)(2,1)S(1)}, u32[]{:S(2)}, u32[]{:S(2)}) collective-permute-start(bf16[528,128]{1,0:T(8,128)(2,1)S(1)} %total.2.refs_1_), channel_id=1, source_target_pairs={{0,8},{8,0},{16,24},{24,16},{1,9},{9,1},{17,25},{25,17},{2,10},{10... | collective-permute-start | bytes 405512 | tf_op jit(solution)/shard_map/ppermute | solution.py:60
  49.9 6.8 %collective-permute-start.12 = (bf16[512,128]{1,0:T(8,128)(2,1)S(1)}, bf16[512,128]{1,0:T(8,128)(2,1)S(1)}, u32[]{:S(2)}, u32[]{:S(2)}) collective-permute-start(bf16[512,128]{1,0:T(8,128)(2,1)S(1)} %get-tuple-element.47.w0), channel_id=1, source_target_pairs={{0,96},{32,64},{64,32},{96,0},{1,97},{33,65},{65,33},{97,1},{2,98}... | collective-permute-start | bytes 393224 | tf_op jit(solution)/shard_map/ppermute | solution.py:60
  52.8 6.5 %collective-permute-start.11 = (bf16[512,128]{1,0:T(8,128)(2,1)S(1)}, bf16[512,128]{1,0:T(8,128)(2,1)S(1)}, u32[]{:S(2)}, u32[]{:S(2)}) collective-permute-start(bf16[512,128]{1,0:T(8,128)(2,1)S(1)} %get-tuple-element.47.w0), channel_id=1, source_target_pairs={{0,64},{32,96},{64,0},{96,32},{1,65},{33,97},{65,1},{97,33},{2,66}... | collective-permute-start | bytes 393224 | tf_op jit(solution)/shard_map/ppermute | solution.py:60
  53.6 5.7 %collective-permute-start.10 = (bf16[512,128]{1,0:T(8,128)(2,1)S(1)}, bf16[512,128]{1,0:T(8,128)(2,1)S(1)}, u32[]{:S(2)}, u32[]{:S(2)}) collective-permute-start(bf16[512,128]{1,0:T(8,128)(2,1)S(1)} %get-tuple-element.47.w0), channel_id=1, source_target_pairs={{0,32},{32,0},{64,96},{96,64},{1,33},{33,1},{65,97},{97,65},{2,34}... | collective-permute-start | bytes 393224 | tf_op jit(solution)/shard_map/ppermute | solution.py:60
  64.6 8.8 %collective-permute-start.14 = (bf16[512,128]{1,0:T(8,128)(2,1)S(1)}, bf16[512,128]{1,0:T(8,128)(2,1)S(1)}, u32[]{:S(2)}, u32[]{:S(2)}) collective-permute-start(bf16[512,128]{1,0:T(8,128)(2,1)S(1)} %get-tuple-element.49), channel_id=1, source_target_pairs={{0,3},{1,2},{2,1},{3,0},{4,7},{5,6},{6,5},{7,4},{8,11},{9,10},{10,... | collective-permute-start | bytes 393224 | tf_op jit(solution)/shard_map/ppermute | solution.py:60
  67.1 7.9 %collective-permute-start.15 = (bf16[512,128]{1,0:T(8,128)(2,1)S(1)}, bf16[512,128]{1,0:T(8,128)(2,1)S(1)}, u32[]{:S(2)}, u32[]{:S(2)}) collective-permute-start(bf16[512,128]{1,0:T(8,128)(2,1)S(1)} %get-tuple-element.50), channel_id=1, source_target_pairs={{0,2},{1,3},{2,0},{3,1},{4,6},{5,7},{6,4},{7,5},{8,10},{9,11},{10,... | collective-permute-start | bytes 393224 | tf_op jit(solution)/shard_map/ppermute | solution.py:60
  67.8 7.2 %collective-permute-start.16 = (bf16[512,128]{1,0:T(8,128)(2,1)S(1)}, bf16[512,128]{1,0:T(8,128)(2,1)S(1)}, u32[]{:S(2)}, u32[]{:S(2)}) collective-permute-start(bf16[512,128]{1,0:T(8,128)(2,1)S(1)} %get-tuple-element.51), channel_id=1, source_target_pairs={{0,1},{1,0},{2,3},{3,2},{4,5},{5,4},{6,7},{7,6},{8,9},{9,8},{10,11... | collective-permute-start | bytes 393224 | tf_op jit(solution)/shard_map/ppermute | solution.py:60
  76.2 8.9 %collective-permute-start.19 = (bf16[608,128]{1,0:T(8,128)(2,1)S(1)}, bf16[608,128]{1,0:T(8,128)(2,1)S(1)}, u32[]{:S(2)}, u32[]{:S(2)}) collective-permute-start(bf16[608,128]{1,0:T(8,128)(2,1)S(1)} %image.2.b0), channel_id=1, source_target_pairs={{0,3},{1,2},{2,1},{3,0},{4,7},{5,6},{6,5},{7,4},{8,11},{9,10},{10,... | collective-permute-start | bytes 466952 | tf_op jit(solution)/shard_map/ppermute | solution.py:60
  78.6 7.9 %collective-permute-start.18 = (bf16[608,128]{1,0:T(8,128)(2,1)S(1)}, bf16[608,128]{1,0:T(8,128)(2,1)S(1)}, u32[]{:S(2)}, u32[]{:S(2)}) collective-permute-start(bf16[608,128]{1,0:T(8,128)(2,1)S(1)} %image.2.b0), channel_id=1, source_target_pairs={{0,2},{1,3},{2,0},{3,1},{4,6},{5,7},{6,4},{7,5},{8,10},{9,11},{10,... | collective-permute-start | bytes 466952 | tf_op jit(solution)/shard_map/ppermute | solution.py:60
  79.2 7.3 %collective-permute-start.17 = (bf16[608,128]{1,0:T(8,128)(2,1)S(1)}, bf16[608,128]{1,0:T(8,128)(2,1)S(1)}, u32[]{:S(2)}, u32[]{:S(2)}) collective-permute-start(bf16[608,128]{1,0:T(8,128)(2,1)S(1)} %image.2.b0), channel_id=1, source_target_pairs={{0,1},{1,0},{2,3},{3,2},{4,5},{5,4},{6,7},{7,6},{8,9},{9,8},{10,11... | collective-permute-start | bytes 466952 | tf_op jit(solution)/shard_map/ppermute | solution.py:60
  89.9 2.0 %collective-permute-start.20 = (bf16[2144,128]{1,0:T(8,128)(2,1)S(1)}, bf16[2144,128]{1,0:T(8,128)(2,1)S(1)}, u32[]{:S(2)}, u32[]{:S(2)}) collective-permute-start(bf16[2144,128]{1,0:T(8,128)(2,1)S(1)} %get-tuple-element.55), channel_id=1, source_target_pairs={{0,4},{4,0},{1,5},{5,1},{2,6},{6,2},{3,7},{7,3},{8,12},{12,8},{9,1... | collective-permute-start | bytes 1646600 | tf_op jit(solution)/shard_map/ppermute | solution.py:60
  92.1 10.7 %collective-permute-start.21 = (bf16[608,128]{1,0:T(8,128)(2,1)S(1)}, bf16[608,128]{1,0:T(8,128)(2,1)S(1)}, u32[]{:S(2)}, u32[]{:S(2)}) collective-permute-start(bf16[608,128]{1,0:T(8,128)(2,1)S(1)} %get-tuple-element.57), channel_id=1, source_target_pairs={{0,96},{32,64},{64,32},{96,0},{1,97},{33,65},{65,33},{97,1},{2,98}... | collective-permute-start | bytes 466952 | tf_op jit(solution)/shard_map/ppermute | solution.py:60
  94.2 8.6 %collective-permute-start.22 = (bf16[608,128]{1,0:T(8,128)(2,1)S(1)}, bf16[608,128]{1,0:T(8,128)(2,1)S(1)}, u32[]{:S(2)}, u32[]{:S(2)}) collective-permute-start(bf16[608,128]{1,0:T(8,128)(2,1)S(1)} %get-tuple-element.58), channel_id=1, source_target_pairs={{0,64},{32,96},{64,0},{96,32},{1,65},{33,97},{65,1},{97,33},{2,66}... | collective-permute-start | bytes 466952 | tf_op jit(solution)/shard_map/ppermute | solution.py:60
  95.0 8.5 %collective-permute-start.23 = (bf16[608,128]{1,0:T(8,128)(2,1)S(1)}, bf16[608,128]{1,0:T(8,128)(2,1)S(1)}, u32[]{:S(2)}, u32[]{:S(2)}) collective-permute-start(bf16[608,128]{1,0:T(8,128)(2,1)S(1)} %get-tuple-element.59), channel_id=1, source_target_pairs={{0,32},{32,0},{64,96},{96,64},{1,33},{33,1},{65,97},{97,65},{2,34}... | collective-permute-start | bytes 466952 | tf_op jit(solution)/shard_map/ppermute | solution.py:60
  103.7 8.6 %collective-permute-start.26 = (bf16[608,128]{1,0:T(8,128)(2,1)S(1)}, bf16[608,128]{1,0:T(8,128)(2,1)S(1)}, u32[]{:S(2)}, u32[]{:S(2)}) collective-permute-start(bf16[608,128]{1,0:T(8,128)(2,1)S(1)} %get-tuple-element.61.refs_0_), channel_id=1, source_target_pairs={{0,24},{8,16},{16,8},{24,0},{1,25},{9,17},{17,9},{25,1},{2,26},{10... | collective-permute-start | bytes 466952 | tf_op jit(solution)/shard_map/ppermute | solution.py:60
  106.3 7.9 %collective-permute-start.25 = (bf16[608,128]{1,0:T(8,128)(2,1)S(1)}, bf16[608,128]{1,0:T(8,128)(2,1)S(1)}, u32[]{:S(2)}, u32[]{:S(2)}) collective-permute-start(bf16[608,128]{1,0:T(8,128)(2,1)S(1)} %get-tuple-element.61.refs_0_), channel_id=1, source_target_pairs={{0,16},{8,24},{16,0},{24,8},{1,17},{9,25},{17,1},{25,9},{2,18},{10... | collective-permute-start | bytes 466952 | tf_op jit(solution)/shard_map/ppermute | solution.py:60
  106.3 7.9 %collective-permute-start.24 = (bf16[608,128]{1,0:T(8,128)(2,1)S(1)}, bf16[608,128]{1,0:T(8,128)(2,1)S(1)}, u32[]{:S(2)}, u32[]{:S(2)}) collective-permute-start(bf16[608,128]{1,0:T(8,128)(2,1)S(1)} %get-tuple-element.61.refs_0_), channel_id=1, source_target_pairs={{0,8},{8,0},{16,24},{24,16},{1,9},{9,1},{17,25},{25,17},{2,10},{10... | collective-permute-start | bytes 466952 | tf_op jit(solution)/shard_map/ppermute | solution.py:60
  116.2 6.3 %collective-permute-start.29 = (bf16[512,128]{1,0:T(8,128)(2,1)S(1)}, bf16[512,128]{1,0:T(8,128)(2,1)S(1)}, u32[]{:S(2)}, u32[]{:S(2)}) collective-permute-start(bf16[512,128]{1,0:T(8,128)(2,1)S(1)} %weigh.3.w0), channel_id=1, source_target_pairs={{0,96},{32,64},{64,32},{96,0},{1,97},{33,65},{65,33},{97,1},{2,98}... | collective-permute-start | bytes 393224 | tf_op jit(solution)/shard_map/ppermute | solution.py:60
  118.3 6.5 %collective-permute-start.28 = (bf16[512,128]{1,0:T(8,128)(2,1)S(1)}, bf16[512,128]{1,0:T(8,128)(2,1)S(1)}, u32[]{:S(2)}, u32[]{:S(2)}) collective-permute-start(bf16[512,128]{1,0:T(8,128)(2,1)S(1)} %weigh.3.w0), channel_id=1, source_target_pairs={{0,64},{32,96},{64,0},{96,32},{1,65},{33,97},{65,1},{97,33},{2,66}... | collective-permute-start | bytes 393224 | tf_op jit(solution)/shard_map/ppermute | solution.py:60
  119.0 5.7 %collective-permute-start.27 = (bf16[512,128]{1,0:T(8,128)(2,1)S(1)}, bf16[512,128]{1,0:T(8,128)(2,1)S(1)}, u32[]{:S(2)}, u32[]{:S(2)}) collective-permute-start(bf16[512,128]{1,0:T(8,128)(2,1)S(1)} %weigh.3.w0), channel_id=1, source_target_pairs={{0,32},{32,0},{64,96},{96,64},{1,33},{33,1},{65,97},{97,65},{2,34}... | collective-permute-start | bytes 393224 | tf_op jit(solution)/shard_map/ppermute | solution.py:60
  130.1 9.1 %collective-permute-start.31 = (bf16[512,128]{1,0:T(8,128)(2,1)S(1)}, bf16[512,128]{1,0:T(8,128)(2,1)S(1)}, u32[]{:S(2)}, u32[]{:S(2)}) collective-permute-start(bf16[512,128]{1,0:T(8,128)(2,1)S(1)} %get-tuple-element.65), channel_id=1, source_target_pairs={{0,3},{1,2},{2,1},{3,0},{4,7},{5,6},{6,5},{7,4},{8,11},{9,10},{10,... | collective-permute-start | bytes 393224 | tf_op jit(solution)/shard_map/ppermute | solution.py:60
  132.4 7.9 %collective-permute-start.32 = (bf16[512,128]{1,0:T(8,128)(2,1)S(1)}, bf16[512,128]{1,0:T(8,128)(2,1)S(1)}, u32[]{:S(2)}, u32[]{:S(2)}) collective-permute-start(bf16[512,128]{1,0:T(8,128)(2,1)S(1)} %get-tuple-element.66), channel_id=1, source_target_pairs={{0,2},{1,3},{2,0},{3,1},{4,6},{5,7},{6,4},{7,5},{8,10},{9,11},{10,... | collective-permute-start | bytes 393224 | tf_op jit(solution)/shard_map/ppermute | solution.py:60
  133.0 7.4 %collective-permute-start.33 = (bf16[512,128]{1,0:T(8,128)(2,1)S(1)}, bf16[512,128]{1,0:T(8,128)(2,1)S(1)}, u32[]{:S(2)}, u32[]{:S(2)}) collective-permute-start(bf16[512,128]{1,0:T(8,128)(2,1)S(1)} %get-tuple-element.67), channel_id=1, source_target_pairs={{0,1},{1,0},{2,3},{3,2},{4,5},{5,4},{6,7},{7,6},{8,9},{9,8},{10,11... | collective-permute-start | bytes 393224 | tf_op jit(solution)/shard_map/ppermute | solution.py:60
  (7 other events, 42.4 us)

commit v4 on v3

--- a/solution.py
+++ b/solution.py
@@ -390,25 +390,18 @@
         )
     gram = gram / TOTAL_DOCS
     if last:
-        image, keep, send, whole = refs
-        whole[...] = gram
-        for out, half in ((keep, c), (send, 1 - c)):
-            rows = whole[pl.ds(pl.multiple_of(half * (K // 2), K // 2), K // 2), :]
-            out[...] = jnp.concatenate([rows[: K // 4], rows[K // 4 :]], axis=1)
+        image, halves_beside = refs
+        halves_beside[...] = jnp.concatenate([gram[: K // 2], gram[K // 2 :]], axis=1)
     else:
         refs[0][CHUNK:, :] = pack_gram(gram)
 
 
-def sum_kernel(parts, out):
-    out[...] = jnp.sum(parts[...], axis=0)
-
-
-def solve_kernel(place, half, other, image, out, whole):
-    c = place[2]
-    for ref, at in ((half, c), (other, 1 - c)):
-        rows = jnp.concatenate([ref[:, :K], ref[:, K:]], axis=0)
-        whole[pl.ds(pl.multiple_of(at * (K // 2), K // 2), K // 2), :] = rows
-    factor = inverse_factor(whole[...])
+def sum_kernel(own, r1, r3, r2, out):
+    out[...] = (own[...] + r1[...]) + (r2[...] + r3[...])
+
+
+def solve_kernel(gram, image, out):
+    factor = inverse_factor(jnp.concatenate([gram[:, :K], gram[:, K:]], axis=0))
     for k in range(OWN):
         out[:, k * TILE : (k + 1) * TILE] = times(factor, image[tile_rows(k), :])
 
@@ -454,28 +447,20 @@
         own, *parts = backward(place, coords, mine, other, turned)
         if not last:
             outs = shape(CHUNK + PACKED, TILE, dtype=bf16)
-            scratch = ()
         else:
-            outs = (shape(CHUNK, TILE), shape(K // 4, TILE), shape(K // 4, TILE))
-            scratch = (pltpu.VMEM((K, K), f32),)
-        outs = call(functools.partial(image_kernel, last), "image", outs, [SMEM] + [VMEM] * 5, scratch=scratch)(
+            outs = (shape(CHUNK, TILE), shape(K // 2, 2 * K))
+        outs = call(functools.partial(image_kernel, last), "image", outs, [SMEM] + [VMEM] * 5)(
             place, own, *swapped(parts, BKT), inv
         )
         if not last:
             payload = outs
-    image, keep, send = outs
-    half = keep + swap(send, CORE, 1)
-    others = (X, Z, BKT)
-    copies = jnp.broadcast_to(half, (lax.axis_size(others), *half.shape))
-    parts = lax.all_to_all(copies, others, split_axis=0, concat_axis=0, tiled=True)
-    half = call(sum_kernel, "sum", shape(K // 4, TILE), [VMEM])(parts)
-    return call(
-        solve_kernel,
-        "solve",
-        shape(K, OWN * TILE),
-        [SMEM] + [VMEM] * 3,
-        scratch=[pltpu.VMEM((K, K), f32)],
-    )(place, half, swap(half, CORE, 1), image)
+    image, gram = outs
+    gram = gram + swap(gram, CORE, 1)
+    for axis in (BKT, X, Z):
+        gram = call(sum_kernel, "sum", shape(K // 2, 2 * K), [VMEM] * 4)(
+            gram, *[swap(gram, axis, s) for s in (1, 3, 2)]
+        )
+    return call(solve_kernel, "solve", shape(K, OWN * TILE), [VMEM] * 2)(gram, image)
 
 
 def solution(mesh):

time: 170 us -> 167 us (0.982)
  blocking collectives: 21.3 us -> 0 us
  starting transfers between devices: 43 us -> 53.6 us
  waiting for transfers between devices: 68.8 us -> 78.5 us
    all_to_all x1 -> x0, blocking collectives: 21.3 us -> none  [body(): lax.all_to_all(copies, others, split_axis=0, concat_axis=0, tiled=True)]
    ppermute x36 -> x44, starting transfers between devices: 43 us -> 53.6 us  [swap(): return lax.ppermute(value, axis, [(i, i ^ mask) for i in range(size)])]
    ppermute x36 -> x44, waiting for transfers between devices: 68.8 us -> 78.5 us  [swap(): return lax.ppermute(value, axis, [(i, i ^ mask) for i in range(size)])]
  transfers between devices with their start and end apart: 36 -> 44, of which waited for: 27 -> 33; matrix products, arithmetic and copies ran while one was open for 0% -> 0% of each run, Pallas kernels for 2% -> 2%
where the time goes in v4:
time: 167 us
  waiting for transfers between devices  78.5 us (47%)
  starting transfers between devices  53.6 us (32%)
  Pallas kernels  32 us (19%)
  local copies, waits for them, and re-layouts  1.81 us (1%)
    ppermute x44, waiting for transfers between devices, swap(): return lax.ppermute(value, axis, [(i, i ^ mask) for i in range(size)])  78.5 us
    ppermute x44, starting transfers between devices, swap(): return lax.ppermute(value, axis, [(i, i ^ mask) for i in range(size)])  53.6 us
    pallas_call x1, Pallas kernels, prep(): pl.pallas_call(prep_kernel, out_shape=(shape(SLOTS, TILE, TILE, dtype=bf1...  7.71 us
    pallas_call x2, Pallas kernels, forward(): call(functools.partial(forward_kernel, first), 'forward', outs, [SMEM, SM...  6.88 us
    pallas_call x2, Pallas kernels, backward(): call(backward_kernel, 'backward', tuple(outs), [SMEM, SMEM] + [VMEM] * 6,...  6.47 us
  transfers between devices with their start and end apart: 44, of which 33 were waited for; matrix products, arithmetic and copies ran while one was open for 0% of the time, Pallas kernels for 2%

profile of v4, /device:TPU:0, one launch (start us, length us, event | category | flops | bytes accessed | tf_op | source)
XLA Modules:
  0.0 166.9 jit_solution(1114010947062986214)
XLA Ops:
  2.5 7.7 %prep.1 = (bf16[256,128,128]{2,1,0:T(8,128)(2,1)S(1)}, f32[32,128]{1,0:T(8,128)S(1)}, f32[64,128]{1,0:T(8,128)S(1)}) custom-call(s32[5]{0:T(128)S(1)} %stack.49.place.refs_0_, s32[512]{0:T(512)S(1)} %reshape.9.coords, f32[64,128]{1,0:T(8,128)S(1)} %bitcast.19, s32[256,128,128]{2,1,0:T(8,128)} %bitcast.28), custom_call_target="tpu_custom_call" | custom-call | flops 1000000000 | bytes 25165824 | tf_op jit(solution)/shard_map/prep/pallas_call | solution.py:154
  10.2 3.2 %collective-permute-start.2 = (bf16[608,128]{1,0:T(8,128)(2,1)S(1)}, bf16[608,128]{1,0:T(8,128)(2,1)S(1)}, u32[]{:S(2)}, u32[]{:S(2)}) collective-permute-start(bf16[608,128]{1,0:T(8,128)(2,1)S(1)} %pack.1.b0), channel_id=1, source_target_pairs={{0,3},{1,2},{2,1},{3,0},{4,7},{5,6},{6,5},{7,4},{8,11},{9,10},{10,... | collective-permute-start | bytes 466952 | tf_op jit(solution)/shard_map/ppermute | solution.py:60
  14.4 2.6 %turn.1.refs_1_.turned = bf16[256,128,128]{2,1,0:T(8,128)(2,1)S(1)} custom-call(bf16[256,128,128]{2,1,0:T(8,128)(2,1)S(1)} %get-tuple-element.38.pattern), custom_call_target="tpu_custom_call" | custom-call | bytes 16777216 | tf_op jit(solution)/shard_map/turn/pallas_call | solution.py:426
  17.0 3.0 %collective-permute-done.2.b3 = bf16[608,128]{1,0:T(8,128)(2,1)S(1)} collective-permute-done((bf16[608,128]{1,0:T(8,128)(2,1)S(1)}, bf16[608,128]{1,0:T(8,128)(2,1)S(1)}, u32[]{:S(2)}, u32[]{:S(2)}) %collective-permute-start.2) | collective-permute-done | bytes 155680 | tf_op jit(solution)/shard_map/ppermute | solution.py:60
  21.9 3.4 %forward.2 = (f32[2112,128]{1,0:T(8,128)S(1)}, bf16[2112,128]{1,0:T(8,128)(2,1)S(1)}, f32[32,128]{1,0:T(8,128)S(1)}) custom-call(s32[5]{0:T(128)S(1)} %stack.49.place.refs_0_, s32[512]{0:T(512)S(1)} %reshape.9.coords, bf16[608,128]{1,0:T(8,128)(2,1)S(1)} %pack.1.b0, bf16[608,128]{1,0:T(8,128)(2,1)S(1)} %collective-permute-done.b1, ...), custom_call_target="tpu_custom_call" | custom-call | flops 6000000000 | bytes 12582912 | tf_op jit(solution)/shard_map/forward/pallas_call | solution.py:248
  27.4 2.8 %collective-permute-start.4 = (bf16[528,128]{1,0:T(8,128)(2,1)S(1)}, bf16[528,128]{1,0:T(8,128)(2,1)S(1)}, u32[]{:S(2)}, u32[]{:S(2)}) collective-permute-start(bf16[528,128]{1,0:T(8,128)(2,1)S(1)} %get-tuple-element.43), channel_id=1, source_target_pairs={{0,96},{32,64},{64,32},{96,0},{1,97},{33,65},{65,33},{97,1},{2,98}... | collective-permute-start | bytes 405512 | tf_op jit(solution)/shard_map/ppermute | solution.py:60
  31.6 4.7 %collective-permute-done.4.refs_1_ = bf16[528,128]{1,0:T(8,128)(2,1)S(1)} collective-permute-done((bf16[528,128]{1,0:T(8,128)(2,1)S(1)}, bf16[528,128]{1,0:T(8,128)(2,1)S(1)}, u32[]{:S(2)}, u32[]{:S(2)}) %collective-permute-start.4) | collective-permute-done | bytes 135200 | tf_op jit(solution)/shard_map/ppermute | solution.py:60
  38.3 4.1 %collective-permute-start.9 = (bf16[528,128]{1,0:T(8,128)(2,1)S(1)}, bf16[528,128]{1,0:T(8,128)(2,1)S(1)}, u32[]{:S(2)}, u32[]{:S(2)}) collective-permute-start(bf16[528,128]{1,0:T(8,128)(2,1)S(1)} %total.2.refs_1_), channel_id=1, source_target_pairs={{0,24},{8,16},{16,8},{24,0},{1,25},{9,17},{17,9},{25,1},{2,26},{10... | collective-permute-start | bytes 405512 | tf_op jit(solution)/shard_map/ppermute | solution.py:60
  43.4 3.6 %collective-permute-done.9.refs_4_ = bf16[528,128]{1,0:T(8,128)(2,1)S(1)} collective-permute-done((bf16[528,128]{1,0:T(8,128)(2,1)S(1)}, bf16[528,128]{1,0:T(8,128)(2,1)S(1)}, u32[]{:S(2)}, u32[]{:S(2)}) %collective-permute-start.9) | collective-permute-done | bytes 135200 | tf_op jit(solution)/shard_map/ppermute | solution.py:60
  47.0 2.3 %collective-permute-done.8.refs_3_ = bf16[528,128]{1,0:T(8,128)(2,1)S(1)} collective-permute-done((bf16[528,128]{1,0:T(8,128)(2,1)S(1)}, bf16[528,128]{1,0:T(8,128)(2,1)S(1)}, u32[]{:S(2)}, u32[]{:S(2)}) %collective-permute-start.8) | collective-permute-done | bytes 135200 | tf_op jit(solution)/shard_map/ppermute | solution.py:60
  49.9 2.8 %collective-permute-start.12 = (bf16[512,128]{1,0:T(8,128)(2,1)S(1)}, bf16[512,128]{1,0:T(8,128)(2,1)S(1)}, u32[]{:S(2)}, u32[]{:S(2)}) collective-permute-start(bf16[512,128]{1,0:T(8,128)(2,1)S(1)} %get-tuple-element.46.w0), channel_id=1, source_target_pairs={{0,96},{32,64},{64,32},{96,0},{1,97},{33,65},{65,33},{97,1},{2,98}... | collective-permute-start | bytes 393224 | tf_op jit(solution)/shard_map/ppermute | solution.py:60
  54.1 2.6 %collective-permute-done.12.w3 = bf16[512,128]{1,0:T(8,128)(2,1)S(1)} collective-permute-done((bf16[512,128]{1,0:T(8,128)(2,1)S(1)}, bf16[512,128]{1,0:T(8,128)(2,1)S(1)}, u32[]{:S(2)}, u32[]{:S(2)}) %collective-permute-start.12) | collective-permute-done | bytes 131104 | tf_op jit(solution)/shard_map/ppermute | solution.py:60
  56.7 2.5 %collective-permute-done.11.w2 = bf16[512,128]{1,0:T(8,128)(2,1)S(1)} collective-permute-done((bf16[512,128]{1,0:T(8,128)(2,1)S(1)}, bf16[512,128]{1,0:T(8,128)(2,1)S(1)}, u32[]{:S(2)}, u32[]{:S(2)}) %collective-permute-start.11) | collective-permute-done | bytes 131104 | tf_op jit(solution)/shard_map/ppermute | solution.py:60
  61.3 3.2 %backward.2 = (f32[512,128]{1,0:T(8,128)S(1)}, bf16[512,128]{1,0:T(8,128)(2,1)S(1)}, bf16[512,128]{1,0:T(8,128)(2,1)S(1)}, bf16[512,128]{1,0:T(8,128)(2,1)S(1)}) custom-call(s32[5]{0:T(128)S(1)} %stack.49.place.refs_0_, s32[512]{0:T(512)S(1)} %reshape.9.coords, bf16[512,128]{1,0:T(8,128)(2,1)S(1)} %get-tuple-element.46.w0, ...), custom_call_target="tpu_custom_call" | custom-call | flops 6000000000 | bytes 12582912 | tf_op jit(solution)/shard_map/backward/pallas_call | solution.py:365
  64.6 2.6 %collective-permute-start.14 = (bf16[512,128]{1,0:T(8,128)(2,1)S(1)}, bf16[512,128]{1,0:T(8,128)(2,1)S(1)}, u32[]{:S(2)}, u32[]{:S(2)}) collective-permute-start(bf16[512,128]{1,0:T(8,128)(2,1)S(1)} %get-tuple-element.48), channel_id=1, source_target_pairs={{0,3},{1,2},{2,1},{3,0},{4,7},{5,6},{6,5},{7,4},{8,11},{9,10},{10,... | collective-permute-start | bytes 393224 | tf_op jit(solution)/shard_map/ppermute | solution.py:60
  68.7 4.7 %collective-permute-done.14.r1 = bf16[512,128]{1,0:T(8,128)(2,1)S(1)} collective-permute-done((bf16[512,128]{1,0:T(8,128)(2,1)S(1)}, bf16[512,128]{1,0:T(8,128)(2,1)S(1)}, u32[]{:S(2)}, u32[]{:S(2)}) %collective-permute-start.14) | collective-permute-done | bytes 131104 | tf_op jit(solution)/shard_map/ppermute | solution.py:60
  76.2 2.4 %collective-permute-start.19 = (bf16[608,128]{1,0:T(8,128)(2,1)S(1)}, bf16[608,128]{1,0:T(8,128)(2,1)S(1)}, u32[]{:S(2)}, u32[]{:S(2)}) collective-permute-start(bf16[608,128]{1,0:T(8,128)(2,1)S(1)} %image.2.b0), channel_id=1, source_target_pairs={{0,3},{1,2},{2,1},{3,0},{4,7},{5,6},{6,5},{7,4},{8,11},{9,10},{10,... | collective-permute-start | bytes 466952 | tf_op jit(solution)/shard_map/ppermute | solution.py:60
  80.4 4.7 %collective-permute-done.19.b3 = bf16[608,128]{1,0:T(8,128)(2,1)S(1)} collective-permute-done((bf16[608,128]{1,0:T(8,128)(2,1)S(1)}, bf16[608,128]{1,0:T(8,128)(2,1)S(1)}, u32[]{:S(2)}, u32[]{:S(2)}) %collective-permute-start.19) | collective-permute-done | bytes 155680 | tf_op jit(solution)/shard_map/ppermute | solution.py:60
  86.5 3.4 %forward.3 = (f32[2048,128]{1,0:T(8,128)S(1)}, bf16[2144,128]{1,0:T(8,128)(2,1)S(1)}, f32[64,64]{1,0:T(8,128)S(1)}) custom-call(s32[5]{0:T(128)S(1)} %stack.49.place.refs_0_, s32[512]{0:T(512)S(1)} %reshape.9.coords, bf16[608,128]{1,0:T(8,128)(2,1)S(1)} %image.2.b0, bf16[608,128]{1,0:T(8,128)(2,1)S(1)} %collective-permute-done.17.b1, ...), custom_call_target="tpu_custom_call" | custom-call | flops 6000000000 | bytes 12582912 | tf_op jit(solution)/shard_map/forward/pallas_call | solution.py:248
  92.1 2.1 %collective-permute-start.21 = (bf16[608,128]{1,0:T(8,128)(2,1)S(1)}, bf16[608,128]{1,0:T(8,128)(2,1)S(1)}, u32[]{:S(2)}, u32[]{:S(2)}) collective-permute-start(bf16[608,128]{1,0:T(8,128)(2,1)S(1)} %get-tuple-element.56), channel_id=1, source_target_pairs={{0,96},{32,64},{64,32},{96,0},{1,97},{33,65},{65,33},{97,1},{2,98}... | collective-permute-start | bytes 466952 | tf_op jit(solution)/shard_map/ppermute | solution.py:60
  96.3 6.5 %collective-permute-done.21.refs_1_ = bf16[608,128]{1,0:T(8,128)(2,1)S(1)} collective-permute-done((bf16[608,128]{1,0:T(8,128)(2,1)S(1)}, bf16[608,128]{1,0:T(8,128)(2,1)S(1)}, u32[]{:S(2)}, u32[]{:S(2)}) %collective-permute-start.21) | collective-permute-done | bytes 155680 | tf_op jit(solution)/shard_map/ppermute | solution.py:60
  103.7 2.6 %collective-permute-start.26 = (bf16[608,128]{1,0:T(8,128)(2,1)S(1)}, bf16[608,128]{1,0:T(8,128)(2,1)S(1)}, u32[]{:S(2)}, u32[]{:S(2)}) collective-permute-start(bf16[608,128]{1,0:T(8,128)(2,1)S(1)} %get-tuple-element.60.refs_0_), channel_id=1, source_target_pairs={{0,24},{8,16},{16,8},{24,0},{1,25},{9,17},{17,9},{25,1},{2,26},{10... | collective-permute-start | bytes 466952 | tf_op jit(solution)/shard_map/ppermute | solution.py:60
  107.8 4.4 %collective-permute-done.26.refs_3_ = bf16[608,128]{1,0:T(8,128)(2,1)S(1)} collective-permute-done((bf16[608,128]{1,0:T(8,128)(2,1)S(1)}, bf16[608,128]{1,0:T(8,128)(2,1)S(1)}, u32[]{:S(2)}, u32[]{:S(2)}) %collective-permute-start.26) | collective-permute-done | bytes 155680 | tf_op jit(solution)/shard_map/ppermute | solution.py:60
  116.2 2.0 %collective-permute-start.29 = (bf16[512,128]{1,0:T(8,128)(2,1)S(1)}, bf16[512,128]{1,0:T(8,128)(2,1)S(1)}, u32[]{:S(2)}, u32[]{:S(2)}) collective-permute-start(bf16[512,128]{1,0:T(8,128)(2,1)S(1)} %weigh.3.w0), channel_id=1, source_target_pairs={{0,96},{32,64},{64,32},{96,0},{1,97},{33,65},{65,33},{97,1},{2,98}... | collective-permute-start | bytes 393224 | tf_op jit(solution)/shard_map/ppermute | solution.py:60
  120.4 2.1 %collective-permute-done.29.w3 = bf16[512,128]{1,0:T(8,128)(2,1)S(1)} collective-permute-done((bf16[512,128]{1,0:T(8,128)(2,1)S(1)}, bf16[512,128]{1,0:T(8,128)(2,1)S(1)}, u32[]{:S(2)}, u32[]{:S(2)}) %collective-permute-start.29) | collective-permute-done | bytes 131104 | tf_op jit(solution)/shard_map/ppermute | solution.py:60
  122.5 2.2 %collective-permute-done.28.w2 = bf16[512,128]{1,0:T(8,128)(2,1)S(1)} collective-permute-done((bf16[512,128]{1,0:T(8,128)(2,1)S(1)}, bf16[512,128]{1,0:T(8,128)(2,1)S(1)}, u32[]{:S(2)}, u32[]{:S(2)}) %collective-permute-start.28) | collective-permute-done | bytes 131104 | tf_op jit(solution)/shard_map/ppermute | solution.py:60
  126.8 3.2 %backward.3 = (f32[512,128]{1,0:T(8,128)S(1)}, bf16[512,128]{1,0:T(8,128)(2,1)S(1)}, bf16[512,128]{1,0:T(8,128)(2,1)S(1)}, bf16[512,128]{1,0:T(8,128)(2,1)S(1)}) custom-call(s32[5]{0:T(128)S(1)} %stack.49.place.refs_0_, s32[512]{0:T(512)S(1)} %reshape.9.coords, bf16[512,128]{1,0:T(8,128)(2,1)S(1)} %weigh.3.w0, ...), custom_call_target="tpu_custom_call" | custom-call | flops 6000000000 | bytes 12582912 | tf_op jit(solution)/shard_map/backward/pallas_call | solution.py:365
  130.1 2.3 %collective-permute-start.31 = (bf16[512,128]{1,0:T(8,128)(2,1)S(1)}, bf16[512,128]{1,0:T(8,128)(2,1)S(1)}, u32[]{:S(2)}, u32[]{:S(2)}) collective-permute-start(bf16[512,128]{1,0:T(8,128)(2,1)S(1)} %get-tuple-element.64), channel_id=1, source_target_pairs={{0,3},{1,2},{2,1},{3,0},{4,7},{5,6},{6,5},{7,4},{8,11},{9,10},{10,... | collective-permute-start | bytes 393224 | tf_op jit(solution)/shard_map/ppermute | solution.py:60
  134.3 4.9 %collective-permute-done.31.r1 = bf16[512,128]{1,0:T(8,128)(2,1)S(1)} collective-permute-done((bf16[512,128]{1,0:T(8,128)(2,1)S(1)}, bf16[512,128]{1,0:T(8,128)(2,1)S(1)}, u32[]{:S(2)}, u32[]{:S(2)}) %collective-permute-start.31) | collective-permute-done | bytes 131104 | tf_op jit(solution)/shard_map/ppermute | solution.py:60
  142.7 2.3 %collective-permute-start.37 = (f32[32,128]{1,0:T(8,128)S(1)}, f32[32,128]{1,0:T(8,128)S(1)}, u32[]{:S(2)}, u32[]{:S(2)}) collective-permute-start(f32[32,128]{1,0:T(8,128)S(1)} %add.3.own), channel_id=1, source_target_pairs={{0,2},{1,3},{2,0},{3,1},{4,6},{5,7},{6,4},{7,5},{8,10},{9,11},{10,... | collective-permute-start | bytes 49160 | tf_op jit(solution)/shard_map/ppermute | solution.py:60
  150.0 2.3 %collective-permute-start.40 = (f32[32,128]{1,0:T(8,128)S(1)}, f32[32,128]{1,0:T(8,128)S(1)}, u32[]{:S(2)}, u32[]{:S(2)}) collective-permute-start(f32[32,128]{1,0:T(8,128)S(1)} %sum.3.own), channel_id=1, source_target_pairs={{0,64},{32,96},{64,0},{96,32},{1,65},{33,97},{65,1},{97,33},{2,66}... | collective-permute-start | bytes 49160 | tf_op jit(solution)/shard_map/ppermute | solution.py:60
  164.2 2.7 %solve.1 = f32[64,1024]{1,0:T(8,128)} custom-call(f32[32,128]{1,0:T(8,128)S(1)} %sum.5.gram, f32[512,128]{1,0:T(8,128)S(1)} %get-tuple-element.68.image), custom_call_target="tpu_custom_call" | custom-call | tf_op jit(solution)/shard_map/solve/pallas_call | solution.py:463
  (87 shorter events, 59.8 us)
Async XLA Ops:
  10.2 9.8 %collective-permute-start.2 = (bf16[608,128]{1,0:T(8,128)(2,1)S(1)}, bf16[608,128]{1,0:T(8,128)(2,1)S(1)}, u32[]{:S(2)}, u32[]{:S(2)}) collective-permute-start(bf16[608,128]{1,0:T(8,128)(2,1)S(1)} %pack.1.b0), channel_id=1, source_target_pairs={{0,3},{1,2},{2,1},{3,0},{4,7},{5,6},{6,5},{7,4},{8,11},{9,10},{10,... | collective-permute-start | bytes 466952 | tf_op jit(solution)/shard_map/ppermute | solution.py:60
  13.4 8.5 %collective-permute-start.1 = (bf16[608,128]{1,0:T(8,128)(2,1)S(1)}, bf16[608,128]{1,0:T(8,128)(2,1)S(1)}, u32[]{:S(2)}, u32[]{:S(2)}) collective-permute-start(bf16[608,128]{1,0:T(8,128)(2,1)S(1)} %pack.1.b0), channel_id=1, source_target_pairs={{0,2},{1,3},{2,0},{3,1},{4,6},{5,7},{6,4},{7,5},{8,10},{9,11},{10,... | collective-permute-start | bytes 466952 | tf_op jit(solution)/shard_map/ppermute | solution.py:60
  14.0 7.8 %collective-permute-start = (bf16[608,128]{1,0:T(8,128)(2,1)S(1)}, bf16[608,128]{1,0:T(8,128)(2,1)S(1)}, u32[]{:S(2)}, u32[]{:S(2)}) collective-permute-start(bf16[608,128]{1,0:T(8,128)(2,1)S(1)} %pack.1.b0), channel_id=1, source_target_pairs={{0,1},{1,0},{2,3},{3,2},{4,5},{5,4},{6,7},{7,6},{8,9},{9,8},{10,11... | collective-permute-start | bytes 466952 | tf_op jit(solution)/shard_map/ppermute | solution.py:60
  27.4 8.9 %collective-permute-start.4 = (bf16[528,128]{1,0:T(8,128)(2,1)S(1)}, bf16[528,128]{1,0:T(8,128)(2,1)S(1)}, u32[]{:S(2)}, u32[]{:S(2)}) collective-permute-start(bf16[528,128]{1,0:T(8,128)(2,1)S(1)} %get-tuple-element.43), channel_id=1, source_target_pairs={{0,96},{32,64},{64,32},{96,0},{1,97},{33,65},{65,33},{97,1},{2,98}... | collective-permute-start | bytes 405512 | tf_op jit(solution)/shard_map/ppermute | solution.py:60
  30.3 8.0 %collective-permute-start.5 = (bf16[528,128]{1,0:T(8,128)(2,1)S(1)}, bf16[528,128]{1,0:T(8,128)(2,1)S(1)}, u32[]{:S(2)}, u32[]{:S(2)}) collective-permute-start(bf16[528,128]{1,0:T(8,128)(2,1)S(1)} %get-tuple-element.44), channel_id=1, source_target_pairs={{0,64},{32,96},{64,0},{96,32},{1,65},{33,97},{65,1},{97,33},{2,66}... | collective-permute-start | bytes 405512 | tf_op jit(solution)/shard_map/ppermute | solution.py:60
  31.1 7.2 %collective-permute-start.6 = (bf16[528,128]{1,0:T(8,128)(2,1)S(1)}, bf16[528,128]{1,0:T(8,128)(2,1)S(1)}, u32[]{:S(2)}, u32[]{:S(2)}) collective-permute-start(bf16[528,128]{1,0:T(8,128)(2,1)S(1)} %get-tuple-element.45), channel_id=1, source_target_pairs={{0,32},{32,0},{64,96},{96,64},{1,33},{33,1},{65,97},{97,65},{2,34}... | collective-permute-start | bytes 405512 | tf_op jit(solution)/shard_map/ppermute | solution.py:60
  38.3 8.7 %collective-permute-start.9 = (bf16[528,128]{1,0:T(8,128)(2,1)S(1)}, bf16[528,128]{1,0:T(8,128)(2,1)S(1)}, u32[]{:S(2)}, u32[]{:S(2)}) collective-permute-start(bf16[528,128]{1,0:T(8,128)(2,1)S(1)} %total.2.refs_1_), channel_id=1, source_target_pairs={{0,24},{8,16},{16,8},{24,0},{1,25},{9,17},{17,9},{25,1},{2,26},{10... | collective-permute-start | bytes 405512 | tf_op jit(solution)/shard_map/ppermute | solution.py:60
  42.4 6.9 %collective-permute-start.8 = (bf16[528,128]{1,0:T(8,128)(2,1)S(1)}, bf16[528,128]{1,0:T(8,128)(2,1)S(1)}, u32[]{:S(2)}, u32[]{:S(2)}) collective-permute-start(bf16[528,128]{1,0:T(8,128)(2,1)S(1)} %total.2.refs_1_), channel_id=1, source_target_pairs={{0,16},{8,24},{16,0},{24,8},{1,17},{9,25},{17,1},{25,9},{2,18},{10... | collective-permute-start | bytes 405512 | tf_op jit(solution)/shard_map/ppermute | solution.py:60
  42.4 6.9 %collective-permute-start.7 = (bf16[528,128]{1,0:T(8,128)(2,1)S(1)}, bf16[528,128]{1,0:T(8,128)(2,1)S(1)}, u32[]{:S(2)}, u32[]{:S(2)}) collective-permute-start(bf16[528,128]{1,0:T(8,128)(2,1)S(1)} %total.2.refs_1_), channel_id=1, source_target_pairs={{0,8},{8,0},{16,24},{24,16},{1,9},{9,1},{17,25},{25,17},{2,10},{10... | collective-permute-start | bytes 405512 | tf_op jit(solution)/shard_map/ppermute | solution.py:60
  49.9 6.8 %collective-permute-start.12 = (bf16[512,128]{1,0:T(8,128)(2,1)S(1)}, bf16[512,128]{1,0:T(8,128)(2,1)S(1)}, u32[]{:S(2)}, u32[]{:S(2)}) collective-permute-start(bf16[512,128]{1,0:T(8,128)(2,1)S(1)} %get-tuple-element.46.w0), channel_id=1, source_target_pairs={{0,96},{32,64},{64,32},{96,0},{1,97},{33,65},{65,33},{97,1},{2,98}... | collective-permute-start | bytes 393224 | tf_op jit(solution)/shard_map/ppermute | solution.py:60
  52.8 6.5 %collective-permute-start.11 = (bf16[512,128]{1,0:T(8,128)(2,1)S(1)}, bf16[512,128]{1,0:T(8,128)(2,1)S(1)}, u32[]{:S(2)}, u32[]{:S(2)}) collective-permute-start(bf16[512,128]{1,0:T(8,128)(2,1)S(1)} %get-tuple-element.46.w0), channel_id=1, source_target_pairs={{0,64},{32,96},{64,0},{96,32},{1,65},{33,97},{65,1},{97,33},{2,66}... | collective-permute-start | bytes 393224 | tf_op jit(solution)/shard_map/ppermute | solution.py:60
  53.6 5.7 %collective-permute-start.10 = (bf16[512,128]{1,0:T(8,128)(2,1)S(1)}, bf16[512,128]{1,0:T(8,128)(2,1)S(1)}, u32[]{:S(2)}, u32[]{:S(2)}) collective-permute-start(bf16[512,128]{1,0:T(8,128)(2,1)S(1)} %get-tuple-element.46.w0), channel_id=1, source_target_pairs={{0,32},{32,0},{64,96},{96,64},{1,33},{33,1},{65,97},{97,65},{2,34}... | collective-permute-start | bytes 393224 | tf_op jit(solution)/shard_map/ppermute | solution.py:60
  64.6 8.8 %collective-permute-start.14 = (bf16[512,128]{1,0:T(8,128)(2,1)S(1)}, bf16[512,128]{1,0:T(8,128)(2,1)S(1)}, u32[]{:S(2)}, u32[]{:S(2)}) collective-permute-start(bf16[512,128]{1,0:T(8,128)(2,1)S(1)} %get-tuple-element.48), channel_id=1, source_target_pairs={{0,3},{1,2},{2,1},{3,0},{4,7},{5,6},{6,5},{7,4},{8,11},{9,10},{10,... | collective-permute-start | bytes 393224 | tf_op jit(solution)/shard_map/ppermute | solution.py:60
  67.1 7.9 %collective-permute-start.15 = (bf16[512,128]{1,0:T(8,128)(2,1)S(1)}, bf16[512,128]{1,0:T(8,128)(2,1)S(1)}, u32[]{:S(2)}, u32[]{:S(2)}) collective-permute-start(bf16[512,128]{1,0:T(8,128)(2,1)S(1)} %get-tuple-element.49), channel_id=1, source_target_pairs={{0,2},{1,3},{2,0},{3,1},{4,6},{5,7},{6,4},{7,5},{8,10},{9,11},{10,... | collective-permute-start | bytes 393224 | tf_op jit(solution)/shard_map/ppermute | solution.py:60
  67.7 7.3 %collective-permute-start.16 = (bf16[512,128]{1,0:T(8,128)(2,1)S(1)}, bf16[512,128]{1,0:T(8,128)(2,1)S(1)}, u32[]{:S(2)}, u32[]{:S(2)}) collective-permute-start(bf16[512,128]{1,0:T(8,128)(2,1)S(1)} %get-tuple-element.50), channel_id=1, source_target_pairs={{0,1},{1,0},{2,3},{3,2},{4,5},{5,4},{6,7},{7,6},{8,9},{9,8},{10,11... | collective-permute-start | bytes 393224 | tf_op jit(solution)/shard_map/ppermute | solution.py:60
  76.2 8.9 %collective-permute-start.19 = (bf16[608,128]{1,0:T(8,128)(2,1)S(1)}, bf16[608,128]{1,0:T(8,128)(2,1)S(1)}, u32[]{:S(2)}, u32[]{:S(2)}) collective-permute-start(bf16[608,128]{1,0:T(8,128)(2,1)S(1)} %image.2.b0), channel_id=1, source_target_pairs={{0,3},{1,2},{2,1},{3,0},{4,7},{5,6},{6,5},{7,4},{8,11},{9,10},{10,... | collective-permute-start | bytes 466952 | tf_op jit(solution)/shard_map/ppermute | solution.py:60
  78.6 7.9 %collective-permute-start.18 = (bf16[608,128]{1,0:T(8,128)(2,1)S(1)}, bf16[608,128]{1,0:T(8,128)(2,1)S(1)}, u32[]{:S(2)}, u32[]{:S(2)}) collective-permute-start(bf16[608,128]{1,0:T(8,128)(2,1)S(1)} %image.2.b0), channel_id=1, source_target_pairs={{0,2},{1,3},{2,0},{3,1},{4,6},{5,7},{6,4},{7,5},{8,10},{9,11},{10,... | collective-permute-start | bytes 466952 | tf_op jit(solution)/shard_map/ppermute | solution.py:60
  79.2 7.3 %collective-permute-start.17 = (bf16[608,128]{1,0:T(8,128)(2,1)S(1)}, bf16[608,128]{1,0:T(8,128)(2,1)S(1)}, u32[]{:S(2)}, u32[]{:S(2)}) collective-permute-start(bf16[608,128]{1,0:T(8,128)(2,1)S(1)} %image.2.b0), channel_id=1, source_target_pairs={{0,1},{1,0},{2,3},{3,2},{4,5},{5,4},{6,7},{7,6},{8,9},{9,8},{10,11... | collective-permute-start | bytes 466952 | tf_op jit(solution)/shard_map/ppermute | solution.py:60
  92.1 10.7 %collective-permute-start.21 = (bf16[608,128]{1,0:T(8,128)(2,1)S(1)}, bf16[608,128]{1,0:T(8,128)(2,1)S(1)}, u32[]{:S(2)}, u32[]{:S(2)}) collective-permute-start(bf16[608,128]{1,0:T(8,128)(2,1)S(1)} %get-tuple-element.56), channel_id=1, source_target_pairs={{0,96},{32,64},{64,32},{96,0},{1,97},{33,65},{65,33},{97,1},{2,98}... | collective-permute-start | bytes 466952 | tf_op jit(solution)/shard_map/ppermute | solution.py:60
  94.2 8.6 %collective-permute-start.22 = (bf16[608,128]{1,0:T(8,128)(2,1)S(1)}, bf16[608,128]{1,0:T(8,128)(2,1)S(1)}, u32[]{:S(2)}, u32[]{:S(2)}) collective-permute-start(bf16[608,128]{1,0:T(8,128)(2,1)S(1)} %get-tuple-element.57), channel_id=1, source_target_pairs={{0,64},{32,96},{64,0},{96,32},{1,65},{33,97},{65,1},{97,33},{2,66}... | collective-permute-start | bytes 466952 | tf_op jit(solution)/shard_map/ppermute | solution.py:60
  95.0 8.5 %collective-permute-start.23 = (bf16[608,128]{1,0:T(8,128)(2,1)S(1)}, bf16[608,128]{1,0:T(8,128)(2,1)S(1)}, u32[]{:S(2)}, u32[]{:S(2)}) collective-permute-start(bf16[608,128]{1,0:T(8,128)(2,1)S(1)} %get-tuple-element.58), channel_id=1, source_target_pairs={{0,32},{32,0},{64,96},{96,64},{1,33},{33,1},{65,97},{97,65},{2,34}... | collective-permute-start | bytes 466952 | tf_op jit(solution)/shard_map/ppermute | solution.py:60
  103.7 8.6 %collective-permute-start.26 = (bf16[608,128]{1,0:T(8,128)(2,1)S(1)}, bf16[608,128]{1,0:T(8,128)(2,1)S(1)}, u32[]{:S(2)}, u32[]{:S(2)}) collective-permute-start(bf16[608,128]{1,0:T(8,128)(2,1)S(1)} %get-tuple-element.60.refs_0_), channel_id=1, source_target_pairs={{0,24},{8,16},{16,8},{24,0},{1,25},{9,17},{17,9},{25,1},{2,26},{10... | collective-permute-start | bytes 466952 | tf_op jit(solution)/shard_map/ppermute | solution.py:60
  106.3 7.9 %collective-permute-start.25 = (bf16[608,128]{1,0:T(8,128)(2,1)S(1)}, bf16[608,128]{1,0:T(8,128)(2,1)S(1)}, u32[]{:S(2)}, u32[]{:S(2)}) collective-permute-start(bf16[608,128]{1,0:T(8,128)(2,1)S(1)} %get-tuple-element.60.refs_0_), channel_id=1, source_target_pairs={{0,16},{8,24},{16,0},{24,8},{1,17},{9,25},{17,1},{25,9},{2,18},{10... | collective-permute-start | bytes 466952 | tf_op jit(solution)/shard_map/ppermute | solution.py:60
  106.3 7.9 %collective-permute-start.24 = (bf16[608,128]{1,0:T(8,128)(2,1)S(1)}, bf16[608,128]{1,0:T(8,128)(2,1)S(1)}, u32[]{:S(2)}, u32[]{:S(2)}) collective-permute-start(bf16[608,128]{1,0:T(8,128)(2,1)S(1)} %get-tuple-element.60.refs_0_), channel_id=1, source_target_pairs={{0,8},{8,0},{16,24},{24,16},{1,9},{9,1},{17,25},{25,17},{2,10},{10... | collective-permute-start | bytes 466952 | tf_op jit(solution)/shard_map/ppermute | solution.py:60
  116.2 6.3 %collective-permute-start.29 = (bf16[512,128]{1,0:T(8,128)(2,1)S(1)}, bf16[512,128]{1,0:T(8,128)(2,1)S(1)}, u32[]{:S(2)}, u32[]{:S(2)}) collective-permute-start(bf16[512,128]{1,0:T(8,128)(2,1)S(1)} %weigh.3.w0), channel_id=1, source_target_pairs={{0,96},{32,64},{64,32},{96,0},{1,97},{33,65},{65,33},{97,1},{2,98}... | collective-permute-start | bytes 393224 | tf_op jit(solution)/shard_map/ppermute | solution.py:60
  118.3 6.5 %collective-permute-start.28 = (bf16[512,128]{1,0:T(8,128)(2,1)S(1)}, bf16[512,128]{1,0:T(8,128)(2,1)S(1)}, u32[]{:S(2)}, u32[]{:S(2)}) collective-permute-start(bf16[512,128]{1,0:T(8,128)(2,1)S(1)} %weigh.3.w0), channel_id=1, source_target_pairs={{0,64},{32,96},{64,0},{96,32},{1,65},{33,97},{65,1},{97,33},{2,66}... | collective-permute-start | bytes 393224 | tf_op jit(solution)/shard_map/ppermute | solution.py:60
  119.0 5.7 %collective-permute-start.27 = (bf16[512,128]{1,0:T(8,128)(2,1)S(1)}, bf16[512,128]{1,0:T(8,128)(2,1)S(1)}, u32[]{:S(2)}, u32[]{:S(2)}) collective-permute-start(bf16[512,128]{1,0:T(8,128)(2,1)S(1)} %weigh.3.w0), channel_id=1, source_target_pairs={{0,32},{32,0},{64,96},{96,64},{1,33},{33,1},{65,97},{97,65},{2,34}... | collective-permute-start | bytes 393224 | tf_op jit(solution)/shard_map/ppermute | solution.py:60
  130.1 9.1 %collective-permute-start.31 = (bf16[512,128]{1,0:T(8,128)(2,1)S(1)}, bf16[512,128]{1,0:T(8,128)(2,1)S(1)}, u32[]{:S(2)}, u32[]{:S(2)}) collective-permute-start(bf16[512,128]{1,0:T(8,128)(2,1)S(1)} %get-tuple-element.64), channel_id=1, source_target_pairs={{0,3},{1,2},{2,1},{3,0},{4,7},{5,6},{6,5},{7,4},{8,11},{9,10},{10,... | collective-permute-start | bytes 393224 | tf_op jit(solution)/shard_map/ppermute | solution.py:60
  132.4 7.9 %collective-permute-start.32 = (bf16[512,128]{1,0:T(8,128)(2,1)S(1)}, bf16[512,128]{1,0:T(8,128)(2,1)S(1)}, u32[]{:S(2)}, u32[]{:S(2)}) collective-permute-start(bf16[512,128]{1,0:T(8,128)(2,1)S(1)} %get-tuple-element.65), channel_id=1, source_target_pairs={{0,2},{1,3},{2,0},{3,1},{4,6},{5,7},{6,4},{7,5},{8,10},{9,11},{10,... | collective-permute-start | bytes 393224 | tf_op jit(solution)/shard_map/ppermute | solution.py:60
  133.0 7.4 %collective-permute-start.33 = (bf16[512,128]{1,0:T(8,128)(2,1)S(1)}, bf16[512,128]{1,0:T(8,128)(2,1)S(1)}, u32[]{:S(2)}, u32[]{:S(2)}) collective-permute-start(bf16[512,128]{1,0:T(8,128)(2,1)S(1)} %get-tuple-element.66), channel_id=1, source_target_pairs={{0,1},{1,0},{2,3},{3,2},{4,5},{5,4},{6,7},{7,6},{8,9},{9,8},{10,11... | collective-permute-start | bytes 393224 | tf_op jit(solution)/shard_map/ppermute | solution.py:60
  150.0 5.3 %collective-permute-start.40 = (f32[32,128]{1,0:T(8,128)S(1)}, f32[32,128]{1,0:T(8,128)S(1)}, u32[]{:S(2)}, u32[]{:S(2)}) collective-permute-start(f32[32,128]{1,0:T(8,128)S(1)} %sum.3.own), channel_id=1, source_target_pairs={{0,64},{32,96},{64,0},{96,32},{1,65},{33,97},{65,1},{97,33},{2,66}... | collective-permute-start | bytes 49160 | tf_op jit(solution)/shard_map/ppermute | solution.py:60
  157.2 5.3 %collective-permute-start.43 = (f32[32,128]{1,0:T(8,128)S(1)}, f32[32,128]{1,0:T(8,128)S(1)}, u32[]{:S(2)}, u32[]{:S(2)}) collective-permute-start(f32[32,128]{1,0:T(8,128)S(1)} %sum.4.own), channel_id=1, source_target_pairs={{0,16},{8,24},{16,0},{24,8},{1,17},{9,25},{17,1},{25,9},{2,18},{10... | collective-permute-start | bytes 49160 | tf_op jit(solution)/shard_map/ppermute | solution.py:60
  (15 other events, 76.7 us)

commit v5 on v4

--- a/solution.py
+++ b/solution.py
@@ -22,7 +22,7 @@
 TURN = 32
 SEND = (1, 2, 3)
 PIVOTS = 8
-UNROLL = 128
+UNROLL = 256
 PREP_STEP = 32
 MIB = 1 << 20
 PREP_LIMIT = 32 * MIB

time: 167 us -> 166 us (level)
  no operation moved by 1% of the time
where the time goes in v5:
time: 166 us
  waiting for transfers between devices  78.4 us (47%)
  starting transfers between devices  53.6 us (32%)
  Pallas kernels  31.1 us (19%)
  local copies, waits for them, and re-layouts  1.81 us (1%)
    ppermute x44, waiting for transfers between devices, swap(): return lax.ppermute(value, axis, [(i, i ^ mask) for i in range(size)])  78.4 us
    ppermute x44, starting transfers between devices, swap(): return lax.ppermute(value, axis, [(i, i ^ mask) for i in range(size)])  53.6 us
    pallas_call x1, Pallas kernels, prep(): pl.pallas_call(prep_kernel, out_shape=(shape(SLOTS, TILE, TILE, dtype=bf1...  7.72 us
    pallas_call x2, Pallas kernels, forward(): call(functools.partial(forward_kernel, first), 'forward', outs, [SMEM, SM...  6.46 us
    pallas_call x2, Pallas kernels, backward(): call(backward_kernel, 'backward', tuple(outs), [SMEM, SMEM] + [VMEM] * 6,...  6.02 us
  transfers between devices with their start and end apart: 44, of which 33 were waited for; matrix products, arithmetic and copies ran while one was open for 0% of the time, Pallas kernels for 2%

profile of v5, /device:TPU:0, one launch (start us, length us, event | category | flops | bytes accessed | tf_op | source)
XLA Modules:
  0.0 166.0 jit_solution(15234795177540619565)
XLA Ops:
  2.5 7.7 %prep.1 = (bf16[256,128,128]{2,1,0:T(8,128)(2,1)S(1)}, f32[32,128]{1,0:T(8,128)S(1)}, f32[64,128]{1,0:T(8,128)S(1)}) custom-call(s32[5]{0:T(128)S(1)} %stack.49.place.refs_0_, s32[512]{0:T(512)S(1)} %reshape.9.coords, f32[64,128]{1,0:T(8,128)S(1)} %bitcast.19, s32[256,128,128]{2,1,0:T(8,128)} %bitcast.28), custom_call_target="tpu_custom_call" | custom-call | flops 1000000000 | bytes 25165824 | tf_op jit(solution)/shard_map/prep/pallas_call | solution.py:154
  10.2 3.2 %collective-permute-start.2 = (bf16[608,128]{1,0:T(8,128)(2,1)S(1)}, bf16[608,128]{1,0:T(8,128)(2,1)S(1)}, u32[]{:S(2)}, u32[]{:S(2)}) collective-permute-start(bf16[608,128]{1,0:T(8,128)(2,1)S(1)} %pack.1.b0), channel_id=1, source_target_pairs={{0,3},{1,2},{2,1},{3,0},{4,7},{5,6},{6,5},{7,4},{8,11},{9,10},{10,... | collective-permute-start | bytes 466952 | tf_op jit(solution)/shard_map/ppermute | solution.py:60
  14.4 2.6 %turn.1.refs_1_.turned = bf16[256,128,128]{2,1,0:T(8,128)(2,1)S(1)} custom-call(bf16[256,128,128]{2,1,0:T(8,128)(2,1)S(1)} %get-tuple-element.38.pattern), custom_call_target="tpu_custom_call" | custom-call | bytes 16777216 | tf_op jit(solution)/shard_map/turn/pallas_call | solution.py:426
  17.0 3.0 %collective-permute-done.2.b3 = bf16[608,128]{1,0:T(8,128)(2,1)S(1)} collective-permute-done((bf16[608,128]{1,0:T(8,128)(2,1)S(1)}, bf16[608,128]{1,0:T(8,128)(2,1)S(1)}, u32[]{:S(2)}, u32[]{:S(2)}) %collective-permute-start.2) | collective-permute-done | bytes 155680 | tf_op jit(solution)/shard_map/ppermute | solution.py:60
  21.9 3.3 %forward.2 = (f32[2112,128]{1,0:T(8,128)S(1)}, bf16[2112,128]{1,0:T(8,128)(2,1)S(1)}, f32[32,128]{1,0:T(8,128)S(1)}) custom-call(s32[5]{0:T(128)S(1)} %stack.49.place.refs_0_, s32[512]{0:T(512)S(1)} %reshape.9.coords, bf16[608,128]{1,0:T(8,128)(2,1)S(1)} %pack.1.b0, bf16[608,128]{1,0:T(8,128)(2,1)S(1)} %collective-permute-done.b1, ...), custom_call_target="tpu_custom_call" | custom-call | flops 6000000000 | bytes 12582912 | tf_op jit(solution)/shard_map/forward/pallas_call | solution.py:248
  27.3 2.8 %collective-permute-start.4 = (bf16[528,128]{1,0:T(8,128)(2,1)S(1)}, bf16[528,128]{1,0:T(8,128)(2,1)S(1)}, u32[]{:S(2)}, u32[]{:S(2)}) collective-permute-start(bf16[528,128]{1,0:T(8,128)(2,1)S(1)} %get-tuple-element.43), channel_id=1, source_target_pairs={{0,96},{32,64},{64,32},{96,0},{1,97},{33,65},{65,33},{97,1},{2,98}... | collective-permute-start | bytes 405512 | tf_op jit(solution)/shard_map/ppermute | solution.py:60
  31.4 4.7 %collective-permute-done.4.refs_1_ = bf16[528,128]{1,0:T(8,128)(2,1)S(1)} collective-permute-done((bf16[528,128]{1,0:T(8,128)(2,1)S(1)}, bf16[528,128]{1,0:T(8,128)(2,1)S(1)}, u32[]{:S(2)}, u32[]{:S(2)}) %collective-permute-start.4) | collective-permute-done | bytes 135200 | tf_op jit(solution)/shard_map/ppermute | solution.py:60
  38.1 4.1 %collective-permute-start.9 = (bf16[528,128]{1,0:T(8,128)(2,1)S(1)}, bf16[528,128]{1,0:T(8,128)(2,1)S(1)}, u32[]{:S(2)}, u32[]{:S(2)}) collective-permute-start(bf16[528,128]{1,0:T(8,128)(2,1)S(1)} %total.2.refs_1_), channel_id=1, source_target_pairs={{0,24},{8,16},{16,8},{24,0},{1,25},{9,17},{17,9},{25,1},{2,26},{10... | collective-permute-start | bytes 405512 | tf_op jit(solution)/shard_map/ppermute | solution.py:60
  43.2 3.6 %collective-permute-done.9.refs_4_ = bf16[528,128]{1,0:T(8,128)(2,1)S(1)} collective-permute-done((bf16[528,128]{1,0:T(8,128)(2,1)S(1)}, bf16[528,128]{1,0:T(8,128)(2,1)S(1)}, u32[]{:S(2)}, u32[]{:S(2)}) %collective-permute-start.9) | collective-permute-done | bytes 135200 | tf_op jit(solution)/shard_map/ppermute | solution.py:60
  46.9 2.3 %collective-permute-done.8.refs_3_ = bf16[528,128]{1,0:T(8,128)(2,1)S(1)} collective-permute-done((bf16[528,128]{1,0:T(8,128)(2,1)S(1)}, bf16[528,128]{1,0:T(8,128)(2,1)S(1)}, u32[]{:S(2)}, u32[]{:S(2)}) %collective-permute-start.8) | collective-permute-done | bytes 135200 | tf_op jit(solution)/shard_map/ppermute | solution.py:60
  49.8 2.8 %collective-permute-start.12 = (bf16[512,128]{1,0:T(8,128)(2,1)S(1)}, bf16[512,128]{1,0:T(8,128)(2,1)S(1)}, u32[]{:S(2)}, u32[]{:S(2)}) collective-permute-start(bf16[512,128]{1,0:T(8,128)(2,1)S(1)} %get-tuple-element.46.w0), channel_id=1, source_target_pairs={{0,96},{32,64},{64,32},{96,0},{1,97},{33,65},{65,33},{97,1},{2,98}... | collective-permute-start | bytes 393224 | tf_op jit(solution)/shard_map/ppermute | solution.py:60
  53.9 2.6 %collective-permute-done.12.w3 = bf16[512,128]{1,0:T(8,128)(2,1)S(1)} collective-permute-done((bf16[512,128]{1,0:T(8,128)(2,1)S(1)}, bf16[512,128]{1,0:T(8,128)(2,1)S(1)}, u32[]{:S(2)}, u32[]{:S(2)}) %collective-permute-start.12) | collective-permute-done | bytes 131104 | tf_op jit(solution)/shard_map/ppermute | solution.py:60
  56.5 2.5 %collective-permute-done.11.w2 = bf16[512,128]{1,0:T(8,128)(2,1)S(1)} collective-permute-done((bf16[512,128]{1,0:T(8,128)(2,1)S(1)}, bf16[512,128]{1,0:T(8,128)(2,1)S(1)}, u32[]{:S(2)}, u32[]{:S(2)}) %collective-permute-start.11) | collective-permute-done | bytes 131104 | tf_op jit(solution)/shard_map/ppermute | solution.py:60
  61.1 3.0 %backward.2 = (f32[512,128]{1,0:T(8,128)S(1)}, bf16[512,128]{1,0:T(8,128)(2,1)S(1)}, bf16[512,128]{1,0:T(8,128)(2,1)S(1)}, bf16[512,128]{1,0:T(8,128)(2,1)S(1)}) custom-call(s32[5]{0:T(128)S(1)} %stack.49.place.refs_0_, s32[512]{0:T(512)S(1)} %reshape.9.coords, bf16[512,128]{1,0:T(8,128)(2,1)S(1)} %get-tuple-element.46.w0, ...), custom_call_target="tpu_custom_call" | custom-call | flops 6000000000 | bytes 12582912 | tf_op jit(solution)/shard_map/backward/pallas_call | solution.py:365
  64.2 2.6 %collective-permute-start.14 = (bf16[512,128]{1,0:T(8,128)(2,1)S(1)}, bf16[512,128]{1,0:T(8,128)(2,1)S(1)}, u32[]{:S(2)}, u32[]{:S(2)}) collective-permute-start(bf16[512,128]{1,0:T(8,128)(2,1)S(1)} %get-tuple-element.48), channel_id=1, source_target_pairs={{0,3},{1,2},{2,1},{3,0},{4,7},{5,6},{6,5},{7,4},{8,11},{9,10},{10,... | collective-permute-start | bytes 393224 | tf_op jit(solution)/shard_map/ppermute | solution.py:60
  68.3 4.7 %collective-permute-done.14.r1 = bf16[512,128]{1,0:T(8,128)(2,1)S(1)} collective-permute-done((bf16[512,128]{1,0:T(8,128)(2,1)S(1)}, bf16[512,128]{1,0:T(8,128)(2,1)S(1)}, u32[]{:S(2)}, u32[]{:S(2)}) %collective-permute-start.14) | collective-permute-done | bytes 131104 | tf_op jit(solution)/shard_map/ppermute | solution.py:60
  75.8 2.4 %collective-permute-start.19 = (bf16[608,128]{1,0:T(8,128)(2,1)S(1)}, bf16[608,128]{1,0:T(8,128)(2,1)S(1)}, u32[]{:S(2)}, u32[]{:S(2)}) collective-permute-start(bf16[608,128]{1,0:T(8,128)(2,1)S(1)} %image.2.b0), channel_id=1, source_target_pairs={{0,3},{1,2},{2,1},{3,0},{4,7},{5,6},{6,5},{7,4},{8,11},{9,10},{10,... | collective-permute-start | bytes 466952 | tf_op jit(solution)/shard_map/ppermute | solution.py:60
  80.0 4.7 %collective-permute-done.19.b3 = bf16[608,128]{1,0:T(8,128)(2,1)S(1)} collective-permute-done((bf16[608,128]{1,0:T(8,128)(2,1)S(1)}, bf16[608,128]{1,0:T(8,128)(2,1)S(1)}, u32[]{:S(2)}, u32[]{:S(2)}) %collective-permute-start.19) | collective-permute-done | bytes 155680 | tf_op jit(solution)/shard_map/ppermute | solution.py:60
  86.1 3.2 %forward.3 = (f32[2048,128]{1,0:T(8,128)S(1)}, bf16[2144,128]{1,0:T(8,128)(2,1)S(1)}, f32[64,64]{1,0:T(8,128)S(1)}) custom-call(s32[5]{0:T(128)S(1)} %stack.49.place.refs_0_, s32[512]{0:T(512)S(1)} %reshape.9.coords, bf16[608,128]{1,0:T(8,128)(2,1)S(1)} %image.2.b0, bf16[608,128]{1,0:T(8,128)(2,1)S(1)} %collective-permute-done.17.b1, ...), custom_call_target="tpu_custom_call" | custom-call | flops 6000000000 | bytes 12582912 | tf_op jit(solution)/shard_map/forward/pallas_call | solution.py:248
  91.5 2.0 %collective-permute-start.21 = (bf16[608,128]{1,0:T(8,128)(2,1)S(1)}, bf16[608,128]{1,0:T(8,128)(2,1)S(1)}, u32[]{:S(2)}, u32[]{:S(2)}) collective-permute-start(bf16[608,128]{1,0:T(8,128)(2,1)S(1)} %get-tuple-element.56), channel_id=1, source_target_pairs={{0,96},{32,64},{64,32},{96,0},{1,97},{33,65},{65,33},{97,1},{2,98}... | collective-permute-start | bytes 466952 | tf_op jit(solution)/shard_map/ppermute | solution.py:60
  95.7 6.5 %collective-permute-done.21.refs_1_ = bf16[608,128]{1,0:T(8,128)(2,1)S(1)} collective-permute-done((bf16[608,128]{1,0:T(8,128)(2,1)S(1)}, bf16[608,128]{1,0:T(8,128)(2,1)S(1)}, u32[]{:S(2)}, u32[]{:S(2)}) %collective-permute-start.21) | collective-permute-done | bytes 155680 | tf_op jit(solution)/shard_map/ppermute | solution.py:60
  103.1 2.6 %collective-permute-start.26 = (bf16[608,128]{1,0:T(8,128)(2,1)S(1)}, bf16[608,128]{1,0:T(8,128)(2,1)S(1)}, u32[]{:S(2)}, u32[]{:S(2)}) collective-permute-start(bf16[608,128]{1,0:T(8,128)(2,1)S(1)} %get-tuple-element.60.refs_0_), channel_id=1, source_target_pairs={{0,24},{8,16},{16,8},{24,0},{1,25},{9,17},{17,9},{25,1},{2,26},{10... | collective-permute-start | bytes 466952 | tf_op jit(solution)/shard_map/ppermute | solution.py:60
  107.2 4.4 %collective-permute-done.26.refs_3_ = bf16[608,128]{1,0:T(8,128)(2,1)S(1)} collective-permute-done((bf16[608,128]{1,0:T(8,128)(2,1)S(1)}, bf16[608,128]{1,0:T(8,128)(2,1)S(1)}, u32[]{:S(2)}, u32[]{:S(2)}) %collective-permute-start.26) | collective-permute-done | bytes 155680 | tf_op jit(solution)/shard_map/ppermute | solution.py:60
  115.6 2.0 %collective-permute-start.29 = (bf16[512,128]{1,0:T(8,128)(2,1)S(1)}, bf16[512,128]{1,0:T(8,128)(2,1)S(1)}, u32[]{:S(2)}, u32[]{:S(2)}) collective-permute-start(bf16[512,128]{1,0:T(8,128)(2,1)S(1)} %weigh.3.w0), channel_id=1, source_target_pairs={{0,96},{32,64},{64,32},{96,0},{1,97},{33,65},{65,33},{97,1},{2,98}... | collective-permute-start | bytes 393224 | tf_op jit(solution)/shard_map/ppermute | solution.py:60
  119.8 2.1 %collective-permute-done.29.w3 = bf16[512,128]{1,0:T(8,128)(2,1)S(1)} collective-permute-done((bf16[512,128]{1,0:T(8,128)(2,1)S(1)}, bf16[512,128]{1,0:T(8,128)(2,1)S(1)}, u32[]{:S(2)}, u32[]{:S(2)}) %collective-permute-start.29) | collective-permute-done | bytes 131104 | tf_op jit(solution)/shard_map/ppermute | solution.py:60
  121.9 2.3 %collective-permute-done.28.w2 = bf16[512,128]{1,0:T(8,128)(2,1)S(1)} collective-permute-done((bf16[512,128]{1,0:T(8,128)(2,1)S(1)}, bf16[512,128]{1,0:T(8,128)(2,1)S(1)}, u32[]{:S(2)}, u32[]{:S(2)}) %collective-permute-start.28) | collective-permute-done | bytes 131104 | tf_op jit(solution)/shard_map/ppermute | solution.py:60
  126.2 3.0 %backward.3 = (f32[512,128]{1,0:T(8,128)S(1)}, bf16[512,128]{1,0:T(8,128)(2,1)S(1)}, bf16[512,128]{1,0:T(8,128)(2,1)S(1)}, bf16[512,128]{1,0:T(8,128)(2,1)S(1)}) custom-call(s32[5]{0:T(128)S(1)} %stack.49.place.refs_0_, s32[512]{0:T(512)S(1)} %reshape.9.coords, bf16[512,128]{1,0:T(8,128)(2,1)S(1)} %weigh.3.w0, ...), custom_call_target="tpu_custom_call" | custom-call | flops 6000000000 | bytes 12582912 | tf_op jit(solution)/shard_map/backward/pallas_call | solution.py:365
  129.2 2.3 %collective-permute-start.31 = (bf16[512,128]{1,0:T(8,128)(2,1)S(1)}, bf16[512,128]{1,0:T(8,128)(2,1)S(1)}, u32[]{:S(2)}, u32[]{:S(2)}) collective-permute-start(bf16[512,128]{1,0:T(8,128)(2,1)S(1)} %get-tuple-element.64), channel_id=1, source_target_pairs={{0,3},{1,2},{2,1},{3,0},{4,7},{5,6},{6,5},{7,4},{8,11},{9,10},{10,... | collective-permute-start | bytes 393224 | tf_op jit(solution)/shard_map/ppermute | solution.py:60
  133.4 4.9 %collective-permute-done.31.r1 = bf16[512,128]{1,0:T(8,128)(2,1)S(1)} collective-permute-done((bf16[512,128]{1,0:T(8,128)(2,1)S(1)}, bf16[512,128]{1,0:T(8,128)(2,1)S(1)}, u32[]{:S(2)}, u32[]{:S(2)}) %collective-permute-start.31) | collective-permute-done | bytes 131104 | tf_op jit(solution)/shard_map/ppermute | solution.py:60
  141.8 2.3 %collective-permute-start.37 = (f32[32,128]{1,0:T(8,128)S(1)}, f32[32,128]{1,0:T(8,128)S(1)}, u32[]{:S(2)}, u32[]{:S(2)}) collective-permute-start(f32[32,128]{1,0:T(8,128)S(1)} %add.3.own), channel_id=1, source_target_pairs={{0,2},{1,3},{2,0},{3,1},{4,6},{5,7},{6,4},{7,5},{8,10},{9,11},{10,... | collective-permute-start | bytes 49160 | tf_op jit(solution)/shard_map/ppermute | solution.py:60
  149.1 2.3 %collective-permute-start.40 = (f32[32,128]{1,0:T(8,128)S(1)}, f32[32,128]{1,0:T(8,128)S(1)}, u32[]{:S(2)}, u32[]{:S(2)}) collective-permute-start(f32[32,128]{1,0:T(8,128)S(1)} %sum.3.own), channel_id=1, source_target_pairs={{0,64},{32,96},{64,0},{96,32},{1,65},{33,97},{65,1},{97,33},{2,66}... | collective-permute-start | bytes 49160 | tf_op jit(solution)/shard_map/ppermute | solution.py:60
  163.3 2.7 %solve.1 = f32[64,1024]{1,0:T(8,128)} custom-call(f32[32,128]{1,0:T(8,128)S(1)} %sum.5.gram, f32[512,128]{1,0:T(8,128)S(1)} %get-tuple-element.68.image), custom_call_target="tpu_custom_call" | custom-call | tf_op jit(solution)/shard_map/solve/pallas_call | solution.py:463
  (87 shorter events, 59.9 us)
Async XLA Ops:
  10.2 9.8 %collective-permute-start.2 = (bf16[608,128]{1,0:T(8,128)(2,1)S(1)}, bf16[608,128]{1,0:T(8,128)(2,1)S(1)}, u32[]{:S(2)}, u32[]{:S(2)}) collective-permute-start(bf16[608,128]{1,0:T(8,128)(2,1)S(1)} %pack.1.b0), channel_id=1, source_target_pairs={{0,3},{1,2},{2,1},{3,0},{4,7},{5,6},{6,5},{7,4},{8,11},{9,10},{10,... | collective-permute-start | bytes 466952 | tf_op jit(solution)/shard_map/ppermute | solution.py:60
  13.4 8.5 %collective-permute-start.1 = (bf16[608,128]{1,0:T(8,128)(2,1)S(1)}, bf16[608,128]{1,0:T(8,128)(2,1)S(1)}, u32[]{:S(2)}, u32[]{:S(2)}) collective-permute-start(bf16[608,128]{1,0:T(8,128)(2,1)S(1)} %pack.1.b0), channel_id=1, source_target_pairs={{0,2},{1,3},{2,0},{3,1},{4,6},{5,7},{6,4},{7,5},{8,10},{9,11},{10,... | collective-permute-start | bytes 466952 | tf_op jit(solution)/shard_map/ppermute | solution.py:60
  14.0 7.8 %collective-permute-start = (bf16[608,128]{1,0:T(8,128)(2,1)S(1)}, bf16[608,128]{1,0:T(8,128)(2,1)S(1)}, u32[]{:S(2)}, u32[]{:S(2)}) collective-permute-start(bf16[608,128]{1,0:T(8,128)(2,1)S(1)} %pack.1.b0), channel_id=1, source_target_pairs={{0,1},{1,0},{2,3},{3,2},{4,5},{5,4},{6,7},{7,6},{8,9},{9,8},{10,11... | collective-permute-start | bytes 466952 | tf_op jit(solution)/shard_map/ppermute | solution.py:60
  27.3 8.9 %collective-permute-start.4 = (bf16[528,128]{1,0:T(8,128)(2,1)S(1)}, bf16[528,128]{1,0:T(8,128)(2,1)S(1)}, u32[]{:S(2)}, u32[]{:S(2)}) collective-permute-start(bf16[528,128]{1,0:T(8,128)(2,1)S(1)} %get-tuple-element.43), channel_id=1, source_target_pairs={{0,96},{32,64},{64,32},{96,0},{1,97},{33,65},{65,33},{97,1},{2,98}... | collective-permute-start | bytes 405512 | tf_op jit(solution)/shard_map/ppermute | solution.py:60
  30.1 8.0 %collective-permute-start.5 = (bf16[528,128]{1,0:T(8,128)(2,1)S(1)}, bf16[528,128]{1,0:T(8,128)(2,1)S(1)}, u32[]{:S(2)}, u32[]{:S(2)}) collective-permute-start(bf16[528,128]{1,0:T(8,128)(2,1)S(1)} %get-tuple-element.44), channel_id=1, source_target_pairs={{0,64},{32,96},{64,0},{96,32},{1,65},{33,97},{65,1},{97,33},{2,66}... | collective-permute-start | bytes 405512 | tf_op jit(solution)/shard_map/ppermute | solution.py:60
  30.9 7.2 %collective-permute-start.6 = (bf16[528,128]{1,0:T(8,128)(2,1)S(1)}, bf16[528,128]{1,0:T(8,128)(2,1)S(1)}, u32[]{:S(2)}, u32[]{:S(2)}) collective-permute-start(bf16[528,128]{1,0:T(8,128)(2,1)S(1)} %get-tuple-element.45), channel_id=1, source_target_pairs={{0,32},{32,0},{64,96},{96,64},{1,33},{33,1},{65,97},{97,65},{2,34}... | collective-permute-start | bytes 405512 | tf_op jit(solution)/shard_map/ppermute | solution.py:60
  38.1 8.7 %collective-permute-start.9 = (bf16[528,128]{1,0:T(8,128)(2,1)S(1)}, bf16[528,128]{1,0:T(8,128)(2,1)S(1)}, u32[]{:S(2)}, u32[]{:S(2)}) collective-permute-start(bf16[528,128]{1,0:T(8,128)(2,1)S(1)} %total.2.refs_1_), channel_id=1, source_target_pairs={{0,24},{8,16},{16,8},{24,0},{1,25},{9,17},{17,9},{25,1},{2,26},{10... | collective-permute-start | bytes 405512 | tf_op jit(solution)/shard_map/ppermute | solution.py:60
  42.3 6.9 %collective-permute-start.8 = (bf16[528,128]{1,0:T(8,128)(2,1)S(1)}, bf16[528,128]{1,0:T(8,128)(2,1)S(1)}, u32[]{:S(2)}, u32[]{:S(2)}) collective-permute-start(bf16[528,128]{1,0:T(8,128)(2,1)S(1)} %total.2.refs_1_), channel_id=1, source_target_pairs={{0,16},{8,24},{16,0},{24,8},{1,17},{9,25},{17,1},{25,9},{2,18},{10... | collective-permute-start | bytes 405512 | tf_op jit(solution)/shard_map/ppermute | solution.py:60
  42.3 6.9 %collective-permute-start.7 = (bf16[528,128]{1,0:T(8,128)(2,1)S(1)}, bf16[528,128]{1,0:T(8,128)(2,1)S(1)}, u32[]{:S(2)}, u32[]{:S(2)}) collective-permute-start(bf16[528,128]{1,0:T(8,128)(2,1)S(1)} %total.2.refs_1_), channel_id=1, source_target_pairs={{0,8},{8,0},{16,24},{24,16},{1,9},{9,1},{17,25},{25,17},{2,10},{10... | collective-permute-start | bytes 405512 | tf_op jit(solution)/shard_map/ppermute | solution.py:60
  49.8 6.8 %collective-permute-start.12 = (bf16[512,128]{1,0:T(8,128)(2,1)S(1)}, bf16[512,128]{1,0:T(8,128)(2,1)S(1)}, u32[]{:S(2)}, u32[]{:S(2)}) collective-permute-start(bf16[512,128]{1,0:T(8,128)(2,1)S(1)} %get-tuple-element.46.w0), channel_id=1, source_target_pairs={{0,96},{32,64},{64,32},{96,0},{1,97},{33,65},{65,33},{97,1},{2,98}... | collective-permute-start | bytes 393224 | tf_op jit(solution)/shard_map/ppermute | solution.py:60
  52.6 6.5 %collective-permute-start.11 = (bf16[512,128]{1,0:T(8,128)(2,1)S(1)}, bf16[512,128]{1,0:T(8,128)(2,1)S(1)}, u32[]{:S(2)}, u32[]{:S(2)}) collective-permute-start(bf16[512,128]{1,0:T(8,128)(2,1)S(1)} %get-tuple-element.46.w0), channel_id=1, source_target_pairs={{0,64},{32,96},{64,0},{96,32},{1,65},{33,97},{65,1},{97,33},{2,66}... | collective-permute-start | bytes 393224 | tf_op jit(solution)/shard_map/ppermute | solution.py:60
  53.4 5.7 %collective-permute-start.10 = (bf16[512,128]{1,0:T(8,128)(2,1)S(1)}, bf16[512,128]{1,0:T(8,128)(2,1)S(1)}, u32[]{:S(2)}, u32[]{:S(2)}) collective-permute-start(bf16[512,128]{1,0:T(8,128)(2,1)S(1)} %get-tuple-element.46.w0), channel_id=1, source_target_pairs={{0,32},{32,0},{64,96},{96,64},{1,33},{33,1},{65,97},{97,65},{2,34}... | collective-permute-start | bytes 393224 | tf_op jit(solution)/shard_map/ppermute | solution.py:60
  64.2 8.8 %collective-permute-start.14 = (bf16[512,128]{1,0:T(8,128)(2,1)S(1)}, bf16[512,128]{1,0:T(8,128)(2,1)S(1)}, u32[]{:S(2)}, u32[]{:S(2)}) collective-permute-start(bf16[512,128]{1,0:T(8,128)(2,1)S(1)} %get-tuple-element.48), channel_id=1, source_target_pairs={{0,3},{1,2},{2,1},{3,0},{4,7},{5,6},{6,5},{7,4},{8,11},{9,10},{10,... | collective-permute-start | bytes 393224 | tf_op jit(solution)/shard_map/ppermute | solution.py:60
  66.7 7.9 %collective-permute-start.15 = (bf16[512,128]{1,0:T(8,128)(2,1)S(1)}, bf16[512,128]{1,0:T(8,128)(2,1)S(1)}, u32[]{:S(2)}, u32[]{:S(2)}) collective-permute-start(bf16[512,128]{1,0:T(8,128)(2,1)S(1)} %get-tuple-element.49), channel_id=1, source_target_pairs={{0,2},{1,3},{2,0},{3,1},{4,6},{5,7},{6,4},{7,5},{8,10},{9,11},{10,... | collective-permute-start | bytes 393224 | tf_op jit(solution)/shard_map/ppermute | solution.py:60
  67.3 7.3 %collective-permute-start.16 = (bf16[512,128]{1,0:T(8,128)(2,1)S(1)}, bf16[512,128]{1,0:T(8,128)(2,1)S(1)}, u32[]{:S(2)}, u32[]{:S(2)}) collective-permute-start(bf16[512,128]{1,0:T(8,128)(2,1)S(1)} %get-tuple-element.50), channel_id=1, source_target_pairs={{0,1},{1,0},{2,3},{3,2},{4,5},{5,4},{6,7},{7,6},{8,9},{9,8},{10,11... | collective-permute-start | bytes 393224 | tf_op jit(solution)/shard_map/ppermute | solution.py:60
  75.8 8.9 %collective-permute-start.19 = (bf16[608,128]{1,0:T(8,128)(2,1)S(1)}, bf16[608,128]{1,0:T(8,128)(2,1)S(1)}, u32[]{:S(2)}, u32[]{:S(2)}) collective-permute-start(bf16[608,128]{1,0:T(8,128)(2,1)S(1)} %image.2.b0), channel_id=1, source_target_pairs={{0,3},{1,2},{2,1},{3,0},{4,7},{5,6},{6,5},{7,4},{8,11},{9,10},{10,... | collective-permute-start | bytes 466952 | tf_op jit(solution)/shard_map/ppermute | solution.py:60
  78.1 7.9 %collective-permute-start.18 = (bf16[608,128]{1,0:T(8,128)(2,1)S(1)}, bf16[608,128]{1,0:T(8,128)(2,1)S(1)}, u32[]{:S(2)}, u32[]{:S(2)}) collective-permute-start(bf16[608,128]{1,0:T(8,128)(2,1)S(1)} %image.2.b0), channel_id=1, source_target_pairs={{0,2},{1,3},{2,0},{3,1},{4,6},{5,7},{6,4},{7,5},{8,10},{9,11},{10,... | collective-permute-start | bytes 466952 | tf_op jit(solution)/shard_map/ppermute | solution.py:60
  78.8 7.3 %collective-permute-start.17 = (bf16[608,128]{1,0:T(8,128)(2,1)S(1)}, bf16[608,128]{1,0:T(8,128)(2,1)S(1)}, u32[]{:S(2)}, u32[]{:S(2)}) collective-permute-start(bf16[608,128]{1,0:T(8,128)(2,1)S(1)} %image.2.b0), channel_id=1, source_target_pairs={{0,1},{1,0},{2,3},{3,2},{4,5},{5,4},{6,7},{7,6},{8,9},{9,8},{10,11... | collective-permute-start | bytes 466952 | tf_op jit(solution)/shard_map/ppermute | solution.py:60
  91.5 10.7 %collective-permute-start.21 = (bf16[608,128]{1,0:T(8,128)(2,1)S(1)}, bf16[608,128]{1,0:T(8,128)(2,1)S(1)}, u32[]{:S(2)}, u32[]{:S(2)}) collective-permute-start(bf16[608,128]{1,0:T(8,128)(2,1)S(1)} %get-tuple-element.56), channel_id=1, source_target_pairs={{0,96},{32,64},{64,32},{96,0},{1,97},{33,65},{65,33},{97,1},{2,98}... | collective-permute-start | bytes 466952 | tf_op jit(solution)/shard_map/ppermute | solution.py:60
  93.5 8.7 %collective-permute-start.22 = (bf16[608,128]{1,0:T(8,128)(2,1)S(1)}, bf16[608,128]{1,0:T(8,128)(2,1)S(1)}, u32[]{:S(2)}, u32[]{:S(2)}) collective-permute-start(bf16[608,128]{1,0:T(8,128)(2,1)S(1)} %get-tuple-element.57), channel_id=1, source_target_pairs={{0,64},{32,96},{64,0},{96,32},{1,65},{33,97},{65,1},{97,33},{2,66}... | collective-permute-start | bytes 466952 | tf_op jit(solution)/shard_map/ppermute | solution.py:60
  94.3 8.5 %collective-permute-start.23 = (bf16[608,128]{1,0:T(8,128)(2,1)S(1)}, bf16[608,128]{1,0:T(8,128)(2,1)S(1)}, u32[]{:S(2)}, u32[]{:S(2)}) collective-permute-start(bf16[608,128]{1,0:T(8,128)(2,1)S(1)} %get-tuple-element.58), channel_id=1, source_target_pairs={{0,32},{32,0},{64,96},{96,64},{1,33},{33,1},{65,97},{97,65},{2,34}... | collective-permute-start | bytes 466952 | tf_op jit(solution)/shard_map/ppermute | solution.py:60
  103.1 8.6 %collective-permute-start.26 = (bf16[608,128]{1,0:T(8,128)(2,1)S(1)}, bf16[608,128]{1,0:T(8,128)(2,1)S(1)}, u32[]{:S(2)}, u32[]{:S(2)}) collective-permute-start(bf16[608,128]{1,0:T(8,128)(2,1)S(1)} %get-tuple-element.60.refs_0_), channel_id=1, source_target_pairs={{0,24},{8,16},{16,8},{24,0},{1,25},{9,17},{17,9},{25,1},{2,26},{10... | collective-permute-start | bytes 466952 | tf_op jit(solution)/shard_map/ppermute | solution.py:60
  105.7 7.9 %collective-permute-start.25 = (bf16[608,128]{1,0:T(8,128)(2,1)S(1)}, bf16[608,128]{1,0:T(8,128)(2,1)S(1)}, u32[]{:S(2)}, u32[]{:S(2)}) collective-permute-start(bf16[608,128]{1,0:T(8,128)(2,1)S(1)} %get-tuple-element.60.refs_0_), channel_id=1, source_target_pairs={{0,16},{8,24},{16,0},{24,8},{1,17},{9,25},{17,1},{25,9},{2,18},{10... | collective-permute-start | bytes 466952 | tf_op jit(solution)/shard_map/ppermute | solution.py:60
  105.7 7.9 %collective-permute-start.24 = (bf16[608,128]{1,0:T(8,128)(2,1)S(1)}, bf16[608,128]{1,0:T(8,128)(2,1)S(1)}, u32[]{:S(2)}, u32[]{:S(2)}) collective-permute-start(bf16[608,128]{1,0:T(8,128)(2,1)S(1)} %get-tuple-element.60.refs_0_), channel_id=1, source_target_pairs={{0,8},{8,0},{16,24},{24,16},{1,9},{9,1},{17,25},{25,17},{2,10},{10... | collective-permute-start | bytes 466952 | tf_op jit(solution)/shard_map/ppermute | solution.py:60
  115.6 6.3 %collective-permute-start.29 = (bf16[512,128]{1,0:T(8,128)(2,1)S(1)}, bf16[512,128]{1,0:T(8,128)(2,1)S(1)}, u32[]{:S(2)}, u32[]{:S(2)}) collective-permute-start(bf16[512,128]{1,0:T(8,128)(2,1)S(1)} %weigh.3.w0), channel_id=1, source_target_pairs={{0,96},{32,64},{64,32},{96,0},{1,97},{33,65},{65,33},{97,1},{2,98}... | collective-permute-start | bytes 393224 | tf_op jit(solution)/shard_map/ppermute | solution.py:60
  117.6 6.5 %collective-permute-start.28 = (bf16[512,128]{1,0:T(8,128)(2,1)S(1)}, bf16[512,128]{1,0:T(8,128)(2,1)S(1)}, u32[]{:S(2)}, u32[]{:S(2)}) collective-permute-start(bf16[512,128]{1,0:T(8,128)(2,1)S(1)} %weigh.3.w0), channel_id=1, source_target_pairs={{0,64},{32,96},{64,0},{96,32},{1,65},{33,97},{65,1},{97,33},{2,66}... | collective-permute-start | bytes 393224 | tf_op jit(solution)/shard_map/ppermute | solution.py:60
  118.4 5.7 %collective-permute-start.27 = (bf16[512,128]{1,0:T(8,128)(2,1)S(1)}, bf16[512,128]{1,0:T(8,128)(2,1)S(1)}, u32[]{:S(2)}, u32[]{:S(2)}) collective-permute-start(bf16[512,128]{1,0:T(8,128)(2,1)S(1)} %weigh.3.w0), channel_id=1, source_target_pairs={{0,32},{32,0},{64,96},{96,64},{1,33},{33,1},{65,97},{97,65},{2,34}... | collective-permute-start | bytes 393224 | tf_op jit(solution)/shard_map/ppermute | solution.py:60
  129.2 9.1 %collective-permute-start.31 = (bf16[512,128]{1,0:T(8,128)(2,1)S(1)}, bf16[512,128]{1,0:T(8,128)(2,1)S(1)}, u32[]{:S(2)}, u32[]{:S(2)}) collective-permute-start(bf16[512,128]{1,0:T(8,128)(2,1)S(1)} %get-tuple-element.64), channel_id=1, source_target_pairs={{0,3},{1,2},{2,1},{3,0},{4,7},{5,6},{6,5},{7,4},{8,11},{9,10},{10,... | collective-permute-start | bytes 393224 | tf_op jit(solution)/shard_map/ppermute | solution.py:60
  131.5 7.9 %collective-permute-start.32 = (bf16[512,128]{1,0:T(8,128)(2,1)S(1)}, bf16[512,128]{1,0:T(8,128)(2,1)S(1)}, u32[]{:S(2)}, u32[]{:S(2)}) collective-permute-start(bf16[512,128]{1,0:T(8,128)(2,1)S(1)} %get-tuple-element.65), channel_id=1, source_target_pairs={{0,2},{1,3},{2,0},{3,1},{4,6},{5,7},{6,4},{7,5},{8,10},{9,11},{10,... | collective-permute-start | bytes 393224 | tf_op jit(solution)/shard_map/ppermute | solution.py:60
  132.1 7.4 %collective-permute-start.33 = (bf16[512,128]{1,0:T(8,128)(2,1)S(1)}, bf16[512,128]{1,0:T(8,128)(2,1)S(1)}, u32[]{:S(2)}, u32[]{:S(2)}) collective-permute-start(bf16[512,128]{1,0:T(8,128)(2,1)S(1)} %get-tuple-element.66), channel_id=1, source_target_pairs={{0,1},{1,0},{2,3},{3,2},{4,5},{5,4},{6,7},{7,6},{8,9},{9,8},{10,11... | collective-permute-start | bytes 393224 | tf_op jit(solution)/shard_map/ppermute | solution.py:60
  149.1 5.3 %collective-permute-start.40 = (f32[32,128]{1,0:T(8,128)S(1)}, f32[32,128]{1,0:T(8,128)S(1)}, u32[]{:S(2)}, u32[]{:S(2)}) collective-permute-start(f32[32,128]{1,0:T(8,128)S(1)} %sum.3.own), channel_id=1, source_target_pairs={{0,64},{32,96},{64,0},{96,32},{1,65},{33,97},{65,1},{97,33},{2,66}... | collective-permute-start | bytes 49160 | tf_op jit(solution)/shard_map/ppermute | solution.py:60
  156.3 5.3 %collective-permute-start.43 = (f32[32,128]{1,0:T(8,128)S(1)}, f32[32,128]{1,0:T(8,128)S(1)}, u32[]{:S(2)}, u32[]{:S(2)}) collective-permute-start(f32[32,128]{1,0:T(8,128)S(1)} %sum.4.own), channel_id=1, source_target_pairs={{0,16},{8,24},{16,0},{24,8},{1,17},{9,25},{17,1},{25,9},{2,18},{10... | collective-permute-start | bytes 49160 | tf_op jit(solution)/shard_map/ppermute | solution.py:60
  (15 other events, 76.5 us)
